TPU v7x, 512 devices: a whole 4x8x8 slice. The times are simulated.
512 devices in a mesh: grp: 4 (over x), head: 16 (over z, core), sub: 8 (over y).
Axes of the slice: x: 4, y: 8, z: 8, core: 2. Of those that a mesh axis runs over, the one named last changes fastest.
Arguments:
- inputs: bfloat16 [512, 2048], P('grp', 'sub'), may hold values from -6 to 6
- in_gain: float32 [2048], P('sub'), may hold values from 0.5 to 1.5
- w_qkvz: bfloat16 [2048, 8192], P('sub', 'head'), may hold values from -0.125 to 0.125
- w_ab: bfloat16 [2048, 32], P('sub', 'head'), may hold values from -0.125 to 0.125
- a_log: float32 [16], P('head'), may hold values from -1.5 to 1.5
- dt_bias: float32 [16], P('head'), may hold values from -2 to 1
- state_values: bfloat16 [512, 16, 128, 128], P(('grp', 'sub'), 'head'), may hold values from -1 to 1
- state_scales: float32 [512, 16, 128], P(('grp', 'sub'), 'head'), may hold values from 0.05 to 0.5
- norm_gain: float32 [128], replicated, may hold values from 0.5 to 1.5
- w_out: bfloat16 [2048, 2048], P('head', 'sub'), may hold values from -0.125 to 0.125
- post_gain: float32 [2048], replicated, may hold values from 0.5 to 1.5
- routes: int32 [512, 10], P(('grp', 'head')), may hold values from 0 to 255, all different within a row; in each aligned block of 8 rows (0 to 7, 8 to 15, ...) at most 2 rows name the same one
- route_scale: int32 [512, 10], P(('grp', 'head')), may hold values from 8 to 32
- w_gate_up: bfloat16 [512, 2048, 512], P(('grp', 'head', 'sub')), may hold values from -0.125 to 0.125
- w_down: bfloat16 [512, 256, 2048], P(('grp', 'head', 'sub')), may hold values from -0.25 to 0.25
Outputs:
- out: bfloat16 [512, 2048], P(('grp', 'head'), 'sub')
- new_values: bfloat16 [512, 16, 128, 128], P(('grp', 'sub'), 'head')
- new_scales: float32 [512, 16, 128], P(('grp', 'sub'), 'head')
Inputs may be any that keep to these rules, and one draw needn't show every extreme that they name: `routes`: each row names 10 different experts; within each aligned block of 8 rows no expert is named by more than 2 rows.
All inputs are finite; a program needn't handle non-finite values. Where the computation divides by a largest or mean magnitude, that divisor is 1e-20 or more.
Results may differ from a plain program's by a relative error of at most 0.03.
Values may be sent and summed in bfloat16 or wider, within the bound.
No kernel may reach another device: no remote copies, remote signals or barrier semaphores. Data moves between devices by JAX's collectives and lax.ppermute only.
A program may use at most 64 MiB of HBM per device.

v0:
```python
import jax
import jax.numpy as jnp
from jax import lax
from jax.sharding import PartitionSpec as P

D = 2048
HEAD_DIM = 128
TOPK = 10


def expert_block(received, w_gate_up, w_down):
    half_units = w_down.shape[1]
    flat = received.reshape(-1, received.shape[-1])
    gate_up_joint = jnp.dot(flat, w_gate_up[0], preferred_element_type=jnp.float32)
    activated_hidden = (
        jax.nn.silu(gate_up_joint[:, :half_units]) * gate_up_joint[:, half_units:]
    ).astype(jnp.bfloat16)
    result = jnp.dot(activated_hidden, w_down[0], preferred_element_type=jnp.float32).astype(
        jnp.bfloat16
    )
    return result.reshape(received.shape)


def local(
    inputs,
    in_gain,
    w_qkvz,
    w_ab,
    a_log,
    dt_bias,
    state_values,
    state_scales,
    norm_gain,
    w_out,
    post_gain,
    routes,
    route_scale,
    w_gate_up,
    w_down,
):
    highest_precision = lax.Precision.HIGHEST
    width = HEAD_DIM
    xf = inputs.astype(jnp.float32)
    squares = jnp.sum(xf * xf, axis=1)
    xg = (xf * in_gain).astype(jnp.bfloat16)
    term = jnp.dot(xg, w_qkvz, preferred_element_type=jnp.float32)
    gate_term = jnp.dot(xg, w_ab, preferred_element_type=jnp.float32)
    totals = lax.psum(squares, "sub")
    proj, gates = (
        lax.psum_scatter(term, "sub", scatter_dimension=0, tiled=True),
        lax.psum_scatter(gate_term, "sub", scatter_dimension=0, tiled=True),
    )
    local_rows = proj.shape[0]
    mine = lax.dynamic_slice_in_dim(totals, lax.axis_index("sub") * local_rows, local_rows, 0)
    scale = lax.rsqrt(mine / D + 1e-05)[:, None]
    proj = proj * scale
    gates = gates * scale
    query = jax.nn.silu(proj[:, :width])
    keys = jax.nn.silu(proj[:, width : 2 * width])
    value = jax.nn.silu(proj[:, 2 * width : 3 * width])
    zgate = proj[:, 3 * width :]
    query = (
        query
        * lax.rsqrt(jnp.sum(query * query, axis=-1, keepdims=True) + 1e-06)
        / jnp.sqrt(jnp.float32(width))
    )
    keys = keys * lax.rsqrt(jnp.sum(keys * keys, axis=-1, keepdims=True) + 1e-06)
    beta = jax.nn.sigmoid(gates[:, 1])
    decay = jnp.exp(-jnp.exp(a_log[0]) * jax.nn.softplus(gates[:, 0] + dt_bias[0]))
    state = state_values[:, 0].astype(jnp.float32) * state_scales[:, 0][:, :, None]
    state = state * decay[:, None, None]
    memory = jnp.einsum("rkv,rk->rv", state, keys, precision=highest_precision)
    delta = (value - memory) * beta[:, None]
    state = state + keys[:, :, None] * delta[:, None, :]
    core = jnp.einsum("rkv,rk->rv", state, query, precision=highest_precision)
    gated = (
        core
        * lax.rsqrt(jnp.mean(core * core, axis=-1, keepdims=True) + 1e-06)
        * norm_gain
        * jax.nn.silu(zgate)
    )
    gated = gated.astype(jnp.bfloat16)
    peak = jnp.max(jnp.abs(state), axis=-1) + 1e-06
    new_values = (state / peak[:, :, None]).astype(jnp.bfloat16)[:, None]
    new_scales = peak[:, None]
    gathered = lax.all_gather(gated, "sub", axis=0, tiled=True)
    block_rows = gathered.shape[0] // lax.axis_size("head")
    attn = lax.psum_scatter(
        jnp.dot(gathered, w_out, preferred_element_type=jnp.float32).astype(jnp.bfloat16),
        "head",
        scatter_dimension=0,
        tiled=True,
    ).astype(jnp.float32)
    resid = lax.dynamic_slice_in_dim(xf, lax.axis_index("head") * block_rows, block_rows, 0)
    hidden = (resid + attn).astype(jnp.bfloat16)
    hidden_f = hidden.astype(jnp.float32)
    hsq = lax.psum(jnp.sum(hidden_f * hidden_f, axis=1), "sub")
    cols = hidden.shape[1]
    gain_part = lax.dynamic_slice_in_dim(post_gain, lax.axis_index("sub") * cols, cols, 0)
    normed_part = (hidden_f * lax.rsqrt(hsq / D + 1e-05)[:, None] * gain_part).astype(jnp.bfloat16)
    normed = lax.all_gather(normed_part, "sub", axis=1, tiled=True)
    nsub = lax.axis_size("sub")
    pairs_sub = nsub // 2
    ngrp = lax.axis_size("grp")
    nhead = lax.axis_size("head")
    ndest = ngrp * nhead
    experts_all = ndest * pairs_sub
    block_count = routes.shape[0]
    slots_most = max(2, (block_count * TOPK + experts_all - 1) // experts_all)
    mine_pair = routes % pairs_sub == lax.axis_index("sub") // 2
    target = routes // pairs_sub
    onehot = jnp.where(
        (target[:, :, None] == jnp.arange(ndest, dtype=jnp.int32)[None, None, :])
        & mine_pair[:, :, None],
        1,
        0,
    ).astype(jnp.int32)
    sends = jnp.sum(onehot, axis=1)
    slot = jnp.cumsum(sends, axis=0) - sends
    slot_hit = (slot[:, :, None] == jnp.arange(slots_most, dtype=jnp.int32)[None, None, :]) & (
        sends[:, :, None] > 0
    )
    select = jnp.where(slot_hit, 1.0, 0.0).astype(jnp.bfloat16)
    buffer = jnp.einsum("rdc,rf->dcf", select, normed, preferred_element_type=jnp.float32).astype(
        jnp.bfloat16
    )
    back = lax.all_to_all(
        expert_block(
            lax.all_to_all(buffer, ("grp", "head"), split_axis=0, concat_axis=0, tiled=True),
            w_gate_up,
            w_down,
        ),
        ("grp", "head"),
        split_axis=0,
        concat_axis=0,
        tiled=True,
    )
    weights = jnp.where(mine_pair, route_scale.astype(jnp.float32) / 32.0, 0.0)
    per_dest = jnp.sum(weights[:, :, None] * onehot.astype(jnp.float32), axis=1)
    combine = per_dest[:, :, None] * jnp.where(slot_hit, 1.0, 0.0)
    combine = combine.reshape(combine.shape[0], ndest * slots_most)
    moe_part = jnp.dot(
        combine,
        back.reshape(ndest * slots_most, back.shape[-1]).astype(jnp.float32),
        precision=highest_precision,
    )
    moe = lax.psum_scatter(
        moe_part.astype(jnp.bfloat16), "sub", scatter_dimension=1, tiled=True
    ).astype(jnp.float32)
    out = (hidden_f + moe).astype(jnp.bfloat16)
    return (out, new_values, new_scales)


def solution(mesh):
    placed = (
        P("grp", "sub"),
        P("sub"),
        P("sub", "head"),
        P("sub", "head"),
        P("head"),
        P("head"),
        P(("grp", "sub"), "head", None, None),
        P(("grp", "sub"), "head", None),
        P(),
        P("head", "sub"),
        P(),
        P(("grp", "head"), None),
        P(("grp", "head"), None),
        P(("grp", "head", "sub"), None, None),
        P(("grp", "head", "sub"), None, None),
    )
    return jax.shard_map(
        local,
        mesh=mesh,
        in_specs=placed,
        out_specs=(
            P(("grp", "head"), "sub"),
            P(("grp", "sub"), "head", None, None),
            P(("grp", "sub"), "head", None),
        ),
        check_vma=False,
    )
```

profile of v0, /device:TPU:1, one launch (start us, length us, event | category | flops | bytes accessed | tf_op | source)
XLA Modules:
  0.0 317.8 jit_solution(3441253061661708448)
XLA Ops:
  7.3 1.8 fusion.26
  9.1 1.9 fusion.25
  11.1 0.9 multiply_reduce_fusion
  12.0 0.9 convert_element_type.65
  14.2 14.7 %psum.14 = f32[128]{0:T(128)S(1)} all-reduce(f32[128]{0:T(128)S(1)} %multiply_reduce_fusion), channel_id=1, replica_groups=mesh['grp'=4,'head'=16,'sub'=8] {'sub'}, use_global_device_ids=true, to_apply=%region_2.0 | all-reduce | flops 128 | bytes 1024 | tf_op jit(solution)/shard_map/psum | solution.py:48
  31.5 18.2 %reduce-scatter.13.cloned.1.call-done = f32[16,2]{1,0:T(8,128)} async-done(((f32[128,2]{1,0:T(8,128)}), f32[16,2]{1,0:T(8,128)}) %reduce-scatter.13.cloned.1.call-update) | async-done | bytes 144
  50.5 40.9 %reduce-scatter.7.cloned.1.call-done = f32[16,512]{1,0:T(8,128)} async-done(((f32[128,512]{1,0:T(8,128)}), f32[16,512]{1,0:T(8,128)}) %reduce-scatter.7.cloned.1.call-update) | async-done | bytes 32784 | tf_op jit(solution)/shard_map/reduce_scatter | solution.py:50
  92.5 2.2 fusion.6
  94.8 1.4 fusion.13
  96.4 18.1 %all_gather.6 = bf16[128,128]{1,0:T(8,128)(2,1)S(1)} all-gather(bf16[16,128]{1,0:T(8,128)(2,1)S(1)} %multiply_convert_fusion.3), channel_id=1, replica_groups=mesh['grp'=4,'head'=16,'sub'=8] {'sub'}, dimensions={0}, use_global_device_ids=true | all-gather | bytes 36864 | tf_op jit(solution)/shard_map/all_gather | solution.py:86
  115.4 67.5 %reduce-scatter.9.cloned.1.call-done = bf16[8,256]{1,0:T(8,128)(2,1)} async-done(((bf16[128,256]{1,0:T(8,128)(2,1)}), bf16[8,256]{1,0:T(8,128)(2,1)}) %reduce-scatter.9.cloned.1.call-update) | async-done | bytes 4112 | tf_op jit(solution)/shard_map/reduce_scatter | solution.py:88
  183.7 13.1 %psum.15 = f32[8]{0:T(128)S(1)} all-reduce(f32[8]{0:T(128)S(1)} %get-tuple-element.7), channel_id=1, replica_groups=mesh['grp'=4,'head'=16,'sub'=8] {'sub'}, use_global_device_ids=true, to_apply=%region_12.13 | all-reduce | flops 8 | bytes 64 | tf_op jit(solution)/shard_map/psum | solution.py:97
  196.9 18.1 %all_gather.7 = bf16[8,2048]{1,0:T(8,128)(2,1)S(1)} all-gather(bf16[8,256]{1,0:T(8,128)(2,1)S(1)} %fusion.33), channel_id=1, replica_groups=mesh['grp'=4,'head'=16,'sub'=8] {'sub'}, dimensions={1}, use_global_device_ids=true | all-gather | bytes 36864 | tf_op jit(solution)/shard_map/all_gather | solution.py:101
  215.9 37.5 %all_to_all.10 = bf16[64,2,2048]{2,1,0:T(2,128)(2,1)S(1)} all-to-all(bf16[64,2,2048]{2,1,0:T(2,128)(2,1)S(1)} %copy.26), channel_id=1, replica_groups=mesh['grp'=4,'head'=16,'sub'=8] {'grp','head'}, dimensions={0} | all-to-all | bytes 1048576 | tf_op jit(solution)/shard_map/all_to_all | solution.py:129
  253.4 1.0 reshape.95
  254.4 1.6 fusion.1
  256.3 1.1 reshape.96
  257.5 6.3 %all-to-all-start.1 = ((bf16[64,2,2048]{2,1,0:T(2,128)(2,1)}), bf16[64,2,2048]{2,1,0:T(2,128)(2,1)S(1)}, u32[]{:S(2)}, u32[]{:S(2)}) async-start(bf16[64,2,2048]{2,1,0:T(2,128)(2,1)} %reshape.96), calls=%async_computation.3 | async-start | bytes 1048576 | tf_op jit(solution)/shard_map/all_to_all | solution.py:127
  264.0 1.0 abs_reduce_fusion
  265.1 16.0 %all-to-all-done.1 = bf16[64,2,2048]{2,1,0:T(2,128)(2,1)S(1)} async-done(((bf16[64,2,2048]{2,1,0:T(2,128)(2,1)}), bf16[64,2,2048]{2,1,0:T(2,128)(2,1)S(1)}, u32[]{:S(2)}, u32[]{:S(2)}) %all-to-all-start.1) | async-done | bytes 524320 | tf_op jit(solution)/shard_map/all_to_all | solution.py:127
  281.1 1.0 fusion
  282.1 1.7 fusion.12
  283.8 26.2 %reduce-scatter.11.cloned.1.call-done = bf16[8,256]{1,0:T(8,128)(2,1)} async-done(((bf16[8,2048]{1,0:T(8,128)(2,1)}), bf16[8,256]{1,0:T(8,128)(2,1)}) %reduce-scatter.11.cloned.1.call-update) | async-done | bytes 4112 | tf_op jit(solution)/shard_map/reduce_scatter | solution.py:147
  310.0 1.3 fusion.34
  (55 shorter events, 8.0 us)
Async XLA Ops:
  7.2 247.2 %copy-start = (bf16[1,2048,512]{2,1,0:T(8,128)(2,1)S(1)}, bf16[1,2048,512]{2,1,0:T(8,128)(2,1)}, u32[]{:S(2)}) copy-start(bf16[1,2048,512]{2,1,0:T(8,128)(2,1)} %param.28) | copy-start | bytes 6291460
  7.2 87.6 %copy-start.1 = (bf16[16,1,128,128]{3,2,1,0:T(8,128)(2,1)S(1)}, bf16[16,1,128,128]{3,2,1,0:T(8,128)(2,1)}, u32[]{:S(2)}) copy-start(bf16[16,1,128,128]{3,2,1,0:T(8,128)(2,1)} %param.21) | copy-start | bytes 1572868
  7.2 87.6 %copy-start.4 = (f32[16,1,128]{2,1,0:T(1,128)S(1)}, f32[16,1,128]{2,1,0:T(1,128)}, u32[]{:S(2)}) copy-start(f32[16,1,128]{2,1,0:T(1,128)} %param.22) | copy-start | bytes 24580
  7.2 89.2 %copy-start.6 = (f32[128]{0:T(128)S(1)}, f32[128]{0:T(128)}, u32[]{:S(2)}) copy-start(f32[128]{0:T(128)} %param.23) | copy-start | bytes 1540
  7.2 42.5 %reduce-scatter.13.cloned.1.call-start = ((), (), s32[]{:S(2)}) async-start(), calls=%async_computation.9 | async-start | bytes 73728
  9.0 105.5 %copy-start.3 = (bf16[128,256]{1,0:T(8,128)(2,1)S(1)}, bf16[128,256]{1,0:T(8,128)(2,1)}, u32[]{:S(2)}) copy-start(bf16[128,256]{1,0:T(8,128)(2,1)} %param.24) | copy-start | bytes 196612
  9.0 82.4 %reduce-scatter.7.cloned.1.call-start = ((), (), s32[]{:S(2)}) async-start(), calls=%async_computation.6 | async-start | bytes 294912 | tf_op jit(solution)/shard_map/reduce_scatter | solution.py:50
  11.0 171.9 %reduce-scatter.9.cloned.1.call-start = ((), (), s32[]{:S(2)}) async-start(), calls=%async_computation.7 | async-start | bytes 69632 | tf_op jit(solution)/shard_map/reduce_scatter | solution.py:88
  254.4 1.6 copy-start.2
  257.5 23.6 %all-to-all-start.1 = ((bf16[64,2,2048]{2,1,0:T(2,128)(2,1)}), bf16[64,2,2048]{2,1,0:T(2,128)(2,1)S(1)}, u32[]{:S(2)}, u32[]{:S(2)}) async-start(bf16[64,2,2048]{2,1,0:T(2,128)(2,1)} %reshape.96), calls=%async_computation.3 | async-start | bytes 1048576 | tf_op jit(solution)/shard_map/all_to_all | solution.py:127
  263.8 46.3 %reduce-scatter.11.cloned.1.call-start = ((), (), s32[]{:S(2)}) async-start(), calls=%async_computation.8 | async-start | bytes 36864 | tf_op jit(solution)/shard_map/reduce_scatter | solution.py:147
  265.1 46.3 %copy-start.5 = (f32[16,128]{1,0:T(8,128)}, f32[16,128]{1,0:T(8,128)S(1)}, u32[]{:S(2)}) copy-start(f32[16,128]{1,0:T(8,128)S(1)} %broadcast_add_fusion) | copy-start | bytes 24580
Sparse Core Ops, SparseCore 0:
  10.8 38.8 reduce-scatter.12
  53.3 38.1 reduce-scatter.6
  115.5 67.3 reduce-scatter.8
  282.3 27.7 reduce-scatter.10
where the time goes:
time: 323 us; the launch traced here: 318 us
  waiting for transfers between devices  169 us (52%)
  blocking collectives  102 us (32%)
  between operations  15.3 us (5%)
  matrix products  11.4 us (4%)
  other arithmetic  9.73 us (3%)
  starting transfers between devices  6.44 us (2%)
  local copies, waits for them, and re-layouts  4.53 us (1%)
    reduce_scatter x1, waiting for transfers between devices, local(): lax.psum_scatter(jnp.dot(gathered, w_out, preferred_element_type=jnp.floa...  67.5 us
    reduce_scatter x1, waiting for transfers between devices, local(): lax.psum_scatter(term, 'sub', scatter_dimension=0, tiled=True)  40.9 us
    all_to_all x1, blocking collectives, local(): lax.all_to_all(buffer, ('grp', 'head'), split_axis=0, concat_axis=0, tile...  37.5 us
    reduce_scatter x1, waiting for transfers between devices, local(): lax.psum_scatter(moe_part.astype(jnp.bfloat16), 'sub', scatter_dimension=...  26.2 us
    unnamed x5, waiting for transfers between devices  18.3 us
    all_gather x1, blocking collectives, local(): gathered = lax.all_gather(gated, 'sub', axis=0, tiled=True)  18.1 us
    all_gather x1, blocking collectives, local(): normed = lax.all_gather(normed_part, 'sub', axis=1, tiled=True)  18.1 us
    all_to_all x1, waiting for transfers between devices, local(): lax.all_to_all(expert_block(lax.all_to_all(buffer, ('grp', 'head'), split...  16 us
  transfers between devices with their start and end apart: 5, of which 5 were waited for; matrix products, arithmetic and copies ran while one was open for 3% of the time, Pallas kernels for 0%

commit v1 on v0

v1 whole, which is shorter than its diff:
```python
import jax
import jax.numpy as jnp
from jax import lax
from jax.experimental import pallas as pl
from jax.experimental.pallas import tpu as pltpu
from jax.sharding import PartitionSpec as P

D = 2048
HD = 128
TOPK = 10
F32 = jnp.float32
BF16 = jnp.bfloat16

VM = pl.BlockSpec(memory_space=pltpu.VMEM)
SM = pl.BlockSpec(memory_space=pltpu.SMEM)


def call(body, outs, ins, operands, scratch=(), vmem=32 << 20):
    return pl.pallas_call(
        body,
        out_shape=outs,
        in_specs=ins,
        out_specs=jax.tree.map(lambda _: VM, outs),
        scratch_shapes=list(scratch),
        compiler_params=pltpu.CompilerParams(vmem_limit_bytes=vmem),
    )(*operands)


def split_hi(x):
    hi = x.astype(BF16).astype(F32)
    return hi, x - hi


def project_body(x_ref, gain_ref, w_ref, wab_ref, out_ref):
    xf = x_ref[...].astype(F32)
    xg = (xf * gain_ref[...]).astype(BF16)
    proj = jnp.dot(xg, w_ref[...], preferred_element_type=F32)
    key_hi, key_lo = split_hi(proj[:, 128:256])
    out_ref[:, :128] = proj[:, :128].astype(BF16)
    out_ref[:, 128:256] = key_hi.astype(BF16)
    out_ref[:, 256:512] = proj[:, 256:].astype(BF16)
    out_ref[:, 512:640] = key_lo.astype(BF16)
    xgf = xg.astype(F32)
    a = jnp.sum(xgf * wab_ref[0:1, :].astype(F32), axis=1, keepdims=True)
    b = jnp.sum(xgf * wab_ref[1:2, :].astype(F32), axis=1, keepdims=True)
    s = jnp.sum(xf * xf, axis=1, keepdims=True)
    lane = lax.broadcasted_iota(jnp.int32, (xf.shape[0], 128), 1)
    tail = jnp.zeros((xf.shape[0], 128), F32)
    at = 0
    for v in (a, b, s):
        hi, lo = split_hi(v)
        tail = jnp.where(lane == at, hi, tail)
        tail = jnp.where(lane == at + 1, lo, tail)
        at += 2
    out_ref[:, 640:] = tail.astype(BF16)


def silu(x):
    return x * jax.nn.sigmoid(x)


def recur_body(
    p_ref, alog_ref, bias_ref, sv_ref, ss_ref, gain_ref, gated_ref, keys_ref, delta_ref, sd_ref
):
    rows = 16
    t = p_ref[0:rows, :].astype(F32)
    for i in range(1, 8):
        t = t + p_ref[i * rows : (i + 1) * rows, :].astype(F32)
    tail = t[:, 640:]
    lane = lax.broadcasted_iota(jnp.int32, (rows, 128), 1)

    def column(i):
        return jnp.sum(
            jnp.where((lane == i) | (lane == i + 1), tail, 0.0), axis=1, keepdims=True
        )

    scale = lax.rsqrt(column(4) / D + 1e-05)
    proj = t[:, :512] * scale
    av = column(0) * scale
    bv = column(2) * scale
    query = silu(proj[:, :128])
    keys = silu(proj[:, 128:256] + t[:, 512:640] * scale)
    value = silu(proj[:, 256:384])
    zgate = proj[:, 384:512]
    query = (
        query
        * lax.rsqrt(jnp.sum(query * query, axis=-1, keepdims=True) + 1e-06)
        * (1.0 / 128.0**0.5)
    )
    keys = keys * lax.rsqrt(jnp.sum(keys * keys, axis=-1, keepdims=True) + 1e-06)
    beta = jax.nn.sigmoid(bv)
    rate = jnp.exp(jnp.zeros((1, 1), F32) + alog_ref[0])
    pre = av + bias_ref[0]
    soft = jnp.maximum(pre, 0.0) + jnp.log(1.0 + jnp.exp(-jnp.abs(pre)))
    decay = jnp.exp(-rate * soft)
    sd = ss_ref[...] * decay
    kd = (keys * sd).T
    qd = (query * sd).T
    mems = []
    cores = []
    for r in range(rows):
        v = sv_ref[r].astype(F32)
        mems.append(jnp.sum(v * kd[:, r : r + 1], axis=0, keepdims=True))
        cores.append(jnp.sum(v * qd[:, r : r + 1], axis=0, keepdims=True))
    memory = jnp.concatenate(mems, axis=0)
    core0 = jnp.concatenate(cores, axis=0)
    delta = (value - memory) * beta
    core = core0 + jnp.sum(query * keys, axis=-1, keepdims=True) * delta
    gated = (
        core
        * lax.rsqrt(jnp.mean(core * core, axis=-1, keepdims=True) + 1e-06)
        * gain_ref[...]
        * silu(zgate)
    )
    gated_ref[...] = gated.astype(BF16)
    keys_ref[...] = keys
    delta_ref[...] = delta
    sd_ref[...] = sd


def state_body(sv_ref, sd_ref, keys_ref, delta_ref, nv_ref, ns_ref):
    rows = 16
    sdt = sd_ref[...].T
    kt = keys_ref[...].T
    lane = lax.broadcasted_iota(jnp.int32, (128, rows), 1)
    peaks = jnp.zeros((128, rows), F32)
    for r in range(rows):
        s = sv_ref[r].astype(F32) * sdt[:, r : r + 1] + kt[:, r : r + 1] * delta_ref[r : r + 1, :]
        peak = jnp.max(jnp.abs(s), axis=1, keepdims=True) + 1e-06
        nv_ref[r] = (s / peak).astype(BF16)
        peaks = jnp.where(lane == r, peak, peaks)
    ns_ref[...] = peaks.T


def route_body(pair_ref, routes_ref, scale_ref, mt_ref, w_ref):
    n = 1024
    lane = lax.broadcasted_iota(jnp.int32, (8, n), 1)
    expert = lane // 16 * 4 + pair_ref[0]
    slot_of = lane // 8 % 2
    chunk = lane % 8
    sends = jnp.zeros((8, n), F32)
    weight = jnp.zeros((8, n), F32)
    for k in range(TOPK):
        hit = routes_ref[:, k : k + 1] == expert
        sends = jnp.where(hit, 1.0, sends)
        weight = jnp.where(hit, scale_ref[:, k : k + 1].astype(F32) / 32.0, weight)
    row = lax.broadcasted_iota(jnp.int32, (8, n), 0)
    slot = jnp.zeros((8, n), F32)
    for r in range(7):
        slot = slot + jnp.where(row > r, sends[r : r + 1, :], 0.0)
    keep = (sends > 0.0) & (slot == slot_of.astype(F32))
    sel = jnp.where(keep, 1.0, 0.0)
    wsel = jnp.where(keep, weight, 0.0)
    selects = []
    weights = []
    for c in range(8):
        selects.append(jnp.where(chunk == c, sel, 0.0))
        weights.append(jnp.where(chunk == c, wsel, 0.0))
    mt_ref[...] = jnp.concatenate(selects, axis=0).T.astype(BF16)
    w_ref[...] = jnp.concatenate(weights, axis=0).astype(BF16)


def dispatch_body(h_ref, gain_ref, mt_ref, out_ref):
    h = h_ref[...].astype(F32)
    h3 = h.reshape(8, 8, 256)
    sq = jnp.sum(jnp.sum(h3 * h3, axis=0), axis=1, keepdims=True)
    rs = lax.rsqrt(sq / D + 1e-05)
    normed = (h3 * rs[None] * gain_ref[...]).reshape(64, 256).astype(BF16)
    out_ref[...] = jnp.dot(mt_ref[...], normed, preferred_element_type=F32).astype(BF16)


def expert_body(x_ref, wgu_ref, wd_ref, out_ref, scr):
    for half in range(2):
        scr[half * 1024 : (half + 1) * 1024, :] = x_ref[:, half * 128 : (half + 1) * 128].astype(
            F32
        )
    acc = jnp.zeros((128, 512), F32)
    for c in range(8):
        xc = jnp.concatenate(
            [scr[pl.ds(half * 1024 + c, 128, stride=8), :] for half in range(2)], axis=1
        ).astype(BF16)
        acc = acc + jnp.dot(
            xc, wgu_ref[0, c * 256 : (c + 1) * 256, :], preferred_element_type=F32
        )
    act = (silu(acc[:, :256]) * acc[:, 256:]).astype(BF16)
    for c in range(8):
        o = jnp.dot(act, wd_ref[0, :, c * 256 : (c + 1) * 256], preferred_element_type=F32)
        for half in range(2):
            scr[pl.ds(half * 1024 + c, 128, stride=8), :] = o[:, half * 128 : (half + 1) * 128]
    for half in range(2):
        out_ref[:, half * 128 : (half + 1) * 128] = scr[
            half * 1024 : (half + 1) * 1024, :
        ].astype(BF16)


def combine_body(w_ref, x_ref, out_ref):
    out_ref[...] = jnp.dot(w_ref[...], x_ref[...], preferred_element_type=F32).astype(BF16)


def shape(dims, dtype=BF16):
    return jax.ShapeDtypeStruct(dims, dtype)


def a2a(x, axes):
    return lax.all_to_all(x, axes, split_axis=0, concat_axis=0, tiled=True)


def local(
    inputs,
    in_gain,
    w_qkvz,
    w_ab,
    a_log,
    dt_bias,
    state_values,
    state_scales,
    norm_gain,
    w_out,
    post_gain,
    routes,
    route_scale,
    w_gate_up,
    w_down,
):
    pair = (lax.axis_index("sub") // 2).astype(jnp.int32).reshape(1)
    sv = state_values.reshape(16, 128, 128)
    ss = state_scales.reshape(16, 128)
    part = call(
        project_body,
        shape((128, 768)),
        [VM] * 4,
        (inputs, in_gain.reshape(1, 256), w_qkvz, w_ab.T),
    )
    part = a2a(part, "sub")
    mt, wsel = call(
        route_body,
        (shape((1024, 64)), shape((64, 1024))),
        [SM, VM, VM],
        (pair, routes, route_scale),
    )
    gated, keys, delta, sd = call(
        recur_body,
        (shape((16, 128)), shape((16, 128), F32), shape((16, 128), F32), shape((16, 128), F32)),
        [VM, SM, SM, VM, VM, VM],
        (part, a_log, dt_bias, sv, ss, norm_gain.reshape(1, 128)),
    )
    gathered = a2a(jnp.broadcast_to(gated[None], (8, 16, 128)), "sub").reshape(128, 128)
    new_values, new_scales = call(
        state_body,
        (shape((16, 128, 128)), shape((16, 128), F32)),
        [VM] * 4,
        (sv, sd, keys, delta),
    )
    attn = jnp.dot(gathered, w_out, preferred_element_type=F32).astype(BF16)
    attn = a2a(attn, "head").reshape(16, 8, 256)
    attn = jnp.sum(attn.astype(F32), axis=0)
    resid = lax.dynamic_slice_in_dim(inputs, lax.axis_index("head") * 8, 8, 0).astype(F32)
    hidden = (resid + attn).astype(BF16)
    whole = a2a(jnp.broadcast_to(hidden[None], (8, 8, 256)), "sub").reshape(64, 256)
    buffer = call(
        dispatch_body,
        shape((1024, 256)),
        [VM] * 3,
        (whole, post_gain.reshape(8, 1, 256), mt),
    )
    received = a2a(buffer.reshape(64, 16, 256), ("grp", "head")).reshape(1024, 256)
    result = call(
        expert_body,
        shape((1024, 256)),
        [VM] * 3,
        (received, w_gate_up, w_down),
        [pltpu.VMEM((2048, 128), F32)],
    )
    back = a2a(result.reshape(64, 16, 256), ("grp", "head")).reshape(1024, 256)
    moe = call(combine_body, shape((64, 256)), [VM] * 2, (wsel, back))
    moe = a2a(moe.reshape(8, 8, 256), "sub")
    moe = jnp.sum(moe.astype(F32), axis=0)
    out = (hidden.astype(F32) + moe).astype(BF16)
    return (out, new_values.reshape(16, 1, 128, 128), new_scales.reshape(16, 1, 128))


def solution(mesh):
    placed = (
        P("grp", "sub"),
        P("sub"),
        P("sub", "head"),
        P("sub", "head"),
        P("head"),
        P("head"),
        P(("grp", "sub"), "head", None, None),
        P(("grp", "sub"), "head", None),
        P(),
        P("head", "sub"),
        P(),
        P(("grp", "head"), None),
        P(("grp", "head"), None),
        P(("grp", "head", "sub"), None, None),
        P(("grp", "head", "sub"), None, None),
    )
    return jax.shard_map(
        local,
        mesh=mesh,
        in_specs=placed,
        out_specs=(
            P(("grp", "head"), "sub"),
            P(("grp", "sub"), "head", None, None),
            P(("grp", "sub"), "head", None),
        ),
        check_vma=False,
    )
```

time: 323 us -> 130 us (0.40); the launches traced: 318 us -> 129 us
  waiting for transfers between devices: 169 us -> 24.3 us
  blocking collectives: 102 us -> 56.5 us
  starting transfers between devices: 6.44 us -> 28.5 us
  between operations: 15.3 us -> 2.05 us
  matrix products: 11.4 us -> 0.78 us
  other arithmetic: 9.73 us -> 1.33 us
  Pallas kernels: 0 us -> 7.14 us
  local copies, waits for them, and re-layouts: 4.53 us -> 8.37 us
    reduce_scatter x3 -> x0, waiting for transfers between devices: 135 us -> none  [the longest x1 67.5 us: local(): lax.psum_scatter(jnp.dot(gathered, w_out, preferred_element_type=jnp.floa...]
    all_gather x2 -> x0, blocking collectives: 36.2 us -> none  [the longest x1 18.1 us: local(): gathered = lax.all_gather(gated, 'sub', axis=0, tiled=True)]
    psum x2 -> x0, blocking collectives: 27.8 us -> none  [the longest x1 14.7 us: local(): totals = lax.psum(squares, 'sub')]
    all_to_all x1 -> x4, starting transfers between devices: 6.28 us -> 28.5 us  [a2a(): return lax.all_to_all(x, axes, split_axis=0, concat_axis=0, tiled=True)]
    all_to_all x1 -> x3, blocking collectives: 37.5 us -> 56.5 us  [a2a(): return lax.all_to_all(x, axes, split_axis=0, concat_axis=0, tiled=True)]
    unnamed x5 -> x0, waiting for transfers between devices: 18.3 us -> none
    dot_general x8 -> x1, matrix products: 9.6 us -> 0.78 us  [local(): attn = jnp.dot(gathered, w_out, preferred_element_type=F32).astype(BF16)]
    all_to_all x1 -> x4, waiting for transfers between devices: 16 us -> 24.3 us  [a2a(): return lax.all_to_all(x, axes, split_axis=0, concat_axis=0, tiled=True)]
  transfers between devices with their start and end apart: 5 -> 4, of which waited for: 5 -> 4; matrix products, arithmetic and copies ran while one was open for 3% -> 0% of each run, Pallas kernels for 0% -> 2%
where the time goes in v1:
time: 130 us; the launch traced here: 129 us
  blocking collectives  56.5 us (43%)
  starting transfers between devices  28.5 us (22%)
  waiting for transfers between devices  24.3 us (19%)
  local copies, waits for them, and re-layouts  8.37 us (6%)
  Pallas kernels  7.14 us (5%)
  between operations  2.05 us (2%)
  other arithmetic  1.33 us (1%)
    all_to_all x3, blocking collectives, a2a(): return lax.all_to_all(x, axes, split_axis=0, concat_axis=0, tiled=True)  56.5 us
    all_to_all x4, starting transfers between devices, a2a(): return lax.all_to_all(x, axes, split_axis=0, concat_axis=0, tiled=True)  28.5 us
    all_to_all x4, waiting for transfers between devices, a2a(): return lax.all_to_all(x, axes, split_axis=0, concat_axis=0, tiled=True)  24.3 us
    unnamed x28, local copies, waits for them, and re-layouts  7.74 us
    pallas_call x7, Pallas kernels, call(): pl.pallas_call(body, out_shape=outs, in_specs=ins, out_specs=jax.tree.map...  7.14 us
  transfers between devices with their start and end apart: 4, of which 4 were waited for; matrix products, arithmetic and copies ran while one was open for 0% of the time, Pallas kernels for 2%

profile of v1, /device:TPU:1, one launch (start us, length us, event | category | flops | bytes accessed | tf_op | source)
XLA Modules:
  0.0 128.9 jit_solution(4623261752932436806)
XLA Ops:
  0.7 1.0 copy-done.5
  1.6 0.8 copy-done.6
  3.8 0.9 shard_map.166
  4.7 7.7 %all-to-all-start = ((bf16[8,16,768]{2,1,0:T(8,128)(2,1)}), bf16[8,16,768]{2,1,0:T(8,128)(2,1)S(1)}, u32[]{:S(2)}, u32[]{:S(2)}) async-start(bf16[8,16,768]{2,1,0:T(8,128)(2,1)} %bitcast.2), calls=%async_computation | async-start | bytes 393216 | tf_op jit(solution)/shard_map/all_to_all | solution.py:205
  13.7 7.4 %all-to-all-done = bf16[8,16,768]{2,1,0:T(8,128)(2,1)S(1)} async-done(((bf16[8,16,768]{2,1,0:T(8,128)(2,1)}), bf16[8,16,768]{2,1,0:T(8,128)(2,1)S(1)}, u32[]{:S(2)}, u32[]{:S(2)}) %all-to-all-start) | async-done | bytes 196640 | tf_op jit(solution)/shard_map/all_to_all | solution.py:205
  21.1 1.0 copy-done.2
  22.1 0.7 copy-done.7
  23.5 1.0 shard_map.167
  24.6 9.2 %all_to_all.45 = bf16[8,16,128]{2,1,0:T(8,128)(2,1)S(1)} all-to-all(bf16[8,16,128]{2,1,0:T(8,128)(2,1)S(1)} %broadcast_in_dim.4), channel_id=1, replica_groups=mesh['grp'=4,'head'=16,'sub'=8] {'sub'}, dimensions={0} | all-to-all | bytes 65536 | tf_op jit(solution)/shard_map/all_to_all | solution.py:205
  33.8 0.8 fusion
  34.6 14.2 %all-to-all-start.2 = ((bf16[16,8,256]{2,1,0:T(8,128)(2,1)}), bf16[16,8,256]{2,1,0:T(8,128)(2,1)S(1)}, u32[]{:S(2)}, u32[]{:S(2)}) async-start(bf16[16,8,256]{2,1,0:T(8,128)(2,1)} %fusion), calls=%async_computation.2 | async-start | bytes 131072 | tf_op jit(solution)/shard_map/all_to_all | solution.py:205
  48.8 7.8 %all-to-all-done.2 = bf16[16,8,256]{2,1,0:T(8,128)(2,1)S(1)} async-done(((bf16[16,8,256]{2,1,0:T(8,128)(2,1)}), bf16[16,8,256]{2,1,0:T(8,128)(2,1)S(1)}, u32[]{:S(2)}, u32[]{:S(2)}) %all-to-all-start.2) | async-done | bytes 65568 | tf_op jit(solution)/shard_map/all_to_all | solution.py:205
  56.6 0.7 add_convert_fusion.1
  57.9 3.3 %all-to-all-start.3 = ((bf16[8,8,256]{2,1,0:T(8,128)(2,1)}), bf16[8,8,256]{2,1,0:T(8,128)(2,1)S(1)}, u32[]{:S(2)}, u32[]{:S(2)}) async-start(bf16[8,8,256]{2,1,0:T(8,128)(2,1)} %broadcast_in_dim.5), calls=%async_computation.3 | async-start | bytes 65536 | tf_op jit(solution)/shard_map/all_to_all | solution.py:205
  62.0 0.7 copy-done.10
  62.9 5.1 %all-to-all-done.3 = bf16[8,8,256]{2,1,0:T(8,128)(2,1)S(1)} async-done(((bf16[8,8,256]{2,1,0:T(8,128)(2,1)}), bf16[8,8,256]{2,1,0:T(8,128)(2,1)S(1)}, u32[]{:S(2)}, u32[]{:S(2)}) %all-to-all-start.3) | async-done | bytes 32800 | tf_op jit(solution)/shard_map/all_to_all | solution.py:205
  68.1 0.8 copy-done.8
  69.2 23.9 %all_to_all.46 = bf16[64,16,256]{2,1,0:T(8,128)(2,1)S(1)} all-to-all(bf16[64,16,256]{2,1,0:T(8,128)(2,1)S(1)} %bitcast.29), channel_id=1, replica_groups=mesh['grp'=4,'head'=16,'sub'=8] {'grp','head'}, dimensions={0} | all-to-all | bytes 1048576 | tf_op jit(solution)/shard_map/all_to_all | solution.py:205
  93.1 0.9 shard_map.170
  93.9 23.4 %all_to_all.47 = bf16[64,16,256]{2,1,0:T(8,128)(2,1)S(1)} all-to-all(bf16[64,16,256]{2,1,0:T(8,128)(2,1)S(1)} %bitcast.31), channel_id=1, replica_groups=mesh['grp'=4,'head'=16,'sub'=8] {'grp','head'}, dimensions={0} | all-to-all | bytes 1048576 | tf_op jit(solution)/shard_map/all_to_all | solution.py:205
  117.3 0.8 shard_map.171
  118.2 3.3 %all-to-all-start.6 = ((bf16[8,8,256]{2,1,0:T(8,128)(2,1)}), bf16[8,8,256]{2,1,0:T(8,128)(2,1)S(1)}, u32[]{:S(2)}, u32[]{:S(2)}) async-start(bf16[8,8,256]{2,1,0:T(8,128)(2,1)} %bitcast.16), calls=%async_computation.6 | async-start | bytes 65536 | tf_op jit(solution)/shard_map/all_to_all | solution.py:205
  121.5 2.9 %shard_map.172 = (bf16[16,128,128]{2,1,0:T(8,128)(2,1)}, f32[16,128]{1,0:T(8,128)}) custom-call(bf16[16,128,128]{2,1,0:T(8,128)(2,1)S(1)} %bitcast.27, f32[16,128]{1,0:T(8,128)S(1)} %get-tuple-element.14.sd_ref, f32[16,128]{1,0:T(8,128)S(1)} %get-tuple-element.15.keys_ref, f32[16,128]{1,0:T(8,128)S(1)} %get-tuple-element.16.delta_ref), custom_call_target="tpu_custom_call" | custom-call | tf_op jit(solution)/shard_map/pallas_call | solution.py:19
  124.4 3.9 %all-to-all-done.6 = bf16[8,8,256]{2,1,0:T(8,128)(2,1)S(1)} async-done(((bf16[8,8,256]{2,1,0:T(8,128)(2,1)}), bf16[8,8,256]{2,1,0:T(8,128)(2,1)S(1)}, u32[]{:S(2)}, u32[]{:S(2)}) %all-to-all-start.6) | async-done | bytes 32800 | tf_op jit(solution)/shard_map/all_to_all | solution.py:205
  (29 shorter events, 4.6 us)
Async XLA Ops:
  0.6 33.2 %copy-start = (bf16[128,256]{1,0:T(8,128)(2,1)S(1)}, bf16[128,256]{1,0:T(8,128)(2,1)}, u32[]{:S(2)}) copy-start(bf16[128,256]{1,0:T(8,128)(2,1)} %param.24) | copy-start | bytes 196612
  0.6 1.0 copy-start.5
  1.6 0.8 copy-start.6
  2.5 0.7 copy-start.11
  3.1 0.7 copy-start.12
  3.8 89.2 %copy-start.1 = (bf16[1,2048,512]{2,1,0:T(8,128)(2,1)S(1)}, bf16[1,2048,512]{2,1,0:T(8,128)(2,1)}, u32[]{:S(2)}) copy-start(bf16[1,2048,512]{2,1,0:T(8,128)(2,1)} %wgu_ref.1) | copy-start | bytes 6291460
  4.7 16.4 %all-to-all-start = ((bf16[8,16,768]{2,1,0:T(8,128)(2,1)}), bf16[8,16,768]{2,1,0:T(8,128)(2,1)S(1)}, u32[]{:S(2)}, u32[]{:S(2)}) async-start(bf16[8,16,768]{2,1,0:T(8,128)(2,1)} %bitcast.2), calls=%async_computation | async-start | bytes 393216 | tf_op jit(solution)/shard_map/all_to_all | solution.py:205
  21.1 1.0 copy-start.2
  22.1 0.7 copy-start.7
  22.8 0.7 copy-start.13
  34.6 22.0 %all-to-all-start.2 = ((bf16[16,8,256]{2,1,0:T(8,128)(2,1)}), bf16[16,8,256]{2,1,0:T(8,128)(2,1)S(1)}, u32[]{:S(2)}, u32[]{:S(2)}) async-start(bf16[16,8,256]{2,1,0:T(8,128)(2,1)} %fusion), calls=%async_computation.2 | async-start | bytes 131072 | tf_op jit(solution)/shard_map/all_to_all | solution.py:205
  57.9 10.1 %all-to-all-start.3 = ((bf16[8,8,256]{2,1,0:T(8,128)(2,1)}), bf16[8,8,256]{2,1,0:T(8,128)(2,1)S(1)}, u32[]{:S(2)}, u32[]{:S(2)}) async-start(bf16[8,8,256]{2,1,0:T(8,128)(2,1)} %broadcast_in_dim.5), calls=%async_computation.3 | async-start | bytes 65536 | tf_op jit(solution)/shard_map/all_to_all | solution.py:205
  61.3 0.7 copy-start.9
  62.0 0.7 copy-start.10
  68.0 25.0 %copy-start.4 = (bf16[1,256,2048]{2,1,0:T(8,128)(2,1)S(1)}, bf16[1,256,2048]{2,1,0:T(8,128)(2,1)}, u32[]{:S(2)}) copy-start(bf16[1,256,2048]{2,1,0:T(8,128)(2,1)} %wd_ref.1) | copy-start | bytes 3145732
  68.0 0.8 copy-start.8
  93.1 28.4 %copy-start.3 = (bf16[16,1,128,128]{3,2,1,0:T(8,128)(2,1)S(1)}, bf16[16,1,128,128]{3,2,1,0:T(8,128)(2,1)}, u32[]{:S(2)}) copy-start(bf16[16,1,128,128]{3,2,1,0:T(8,128)(2,1)} %param.21) | copy-start | bytes 1572868
  118.2 10.1 %all-to-all-start.6 = ((bf16[8,8,256]{2,1,0:T(8,128)(2,1)}), bf16[8,8,256]{2,1,0:T(8,128)(2,1)S(1)}, u32[]{:S(2)}, u32[]{:S(2)}) async-start(bf16[8,8,256]{2,1,0:T(8,128)(2,1)} %bitcast.16), calls=%async_computation.6 | async-start | bytes 65536 | tf_op jit(solution)/shard_map/all_to_all | solution.py:205

commit v2 on v1

--- a/solution.py
+++ b/solution.py
@@ -13,15 +13,49 @@
 
 VM = pl.BlockSpec(memory_space=pltpu.VMEM)
 SM = pl.BlockSpec(memory_space=pltpu.SMEM)
+HB = pl.BlockSpec(memory_space=pltpu.HBM)
+KEEP = pl.BlockSpec(memory_space=pltpu.HBM)
+
+
+class Fetched:
+    def __init__(self, src, dst, sem):
+        self.copy = pltpu.make_async_copy(src, dst, sem)
+        self.copy.start()
+        self.dst = dst
+        self.done = False
+
+    def get(self):
+        if not self.done:
+            self.copy.wait()
+            self.done = True
+        return self.dst
 
 
 def call(body, outs, ins, operands, scratch=(), vmem=32 << 20):
+    fetched = [i for i, spec in enumerate(ins) if spec is HB]
+    buffers = [pltpu.VMEM(operands[i].shape, operands[i].dtype) for i in fetched]
+
+    def kernel(*refs):
+        refs = list(refs)
+        if fetched:
+            sems = refs.pop()
+            dsts = refs[len(refs) - len(fetched) :]
+            refs = refs[: len(refs) - len(fetched)]
+            for j, i in enumerate(fetched):
+                refs[i] = Fetched(refs[i], dsts[j], sems.at[j])
+        body(*refs)
+
+    operands = [
+        pltpu.with_memory_space_constraint(o, pltpu.HBM) if ins[i] is HB or ins[i] is KEEP else o
+        for i, o in enumerate(operands)
+    ]
+    extra = buffers + ([pltpu.SemaphoreType.DMA((len(fetched),))] if fetched else [])
     return pl.pallas_call(
-        body,
+        kernel,
         out_shape=outs,
         in_specs=ins,
         out_specs=jax.tree.map(lambda _: VM, outs),
-        scratch_shapes=list(scratch),
+        scratch_shapes=list(scratch) + extra,
         compiler_params=pltpu.CompilerParams(vmem_limit_bytes=vmem),
     )(*operands)
 
@@ -31,15 +65,19 @@
     return hi, x - hi
 
 
-def project_body(x_ref, gain_ref, w_ref, wab_ref, out_ref):
+def project_body(sub_ref, head_ref, x_in, gain_in, w_in, wab_in, *rest):
+    held, outs, resid_ref, kept, scr, sems = rest[:5], rest[5:13], rest[13], rest[14:19], rest[19], rest[20]
+    copies = [pltpu.make_async_copy(held[i], kept[i], sems.at[i]) for i in range(5)]
+    for copy in copies:
+        copy.start()
+    x_ref = x_in.get()
     xf = x_ref[...].astype(F32)
-    xg = (xf * gain_ref[...]).astype(BF16)
-    proj = jnp.dot(xg, w_ref[...], preferred_element_type=F32)
-    key_hi, key_lo = split_hi(proj[:, 128:256])
-    out_ref[:, :128] = proj[:, :128].astype(BF16)
-    out_ref[:, 128:256] = key_hi.astype(BF16)
-    out_ref[:, 256:512] = proj[:, 256:].astype(BF16)
-    out_ref[:, 512:640] = key_lo.astype(BF16)
+    xg = (xf * gain_in.get()[...]).astype(BF16)
+    head = head_ref[0]
+    start = pl.multiple_of(lax.div(head, 2) * 16, 16)
+    near = x_ref[pl.ds(start, 16), :].astype(F32)
+    resid_ref[...] = jnp.where(lax.rem(head, 2) == 1, near[8:], near[:8])
+    wab_ref = wab_in.get()
     xgf = xg.astype(F32)
     a = jnp.sum(xgf * wab_ref[0:1, :].astype(F32), axis=1, keepdims=True)
     b = jnp.sum(xgf * wab_ref[1:2, :].astype(F32), axis=1, keepdims=True)
@@ -52,20 +90,31 @@
         tail = jnp.where(lane == at, hi, tail)
         tail = jnp.where(lane == at + 1, lo, tail)
         at += 2
-    out_ref[:, 640:] = tail.astype(BF16)
+    scr[:, 640:] = tail.astype(BF16)
+    proj = jnp.dot(xg, w_in.get()[...], preferred_element_type=F32)
+    key_hi, key_lo = split_hi(proj[:, 128:256])
+    scr[:, :128] = proj[:, :128].astype(BF16)
+    scr[:, 128:256] = key_hi.astype(BF16)
+    scr[:, 256:512] = proj[:, 256:].astype(BF16)
+    scr[:, 512:640] = key_lo.astype(BF16)
+    for k in range(8):
+        to = lax.rem(sub_ref[0] + k, 8)
+        outs[k][...] = scr[pl.ds(pl.multiple_of(to * 16, 16), 16), :]
+    for copy in copies:
+        copy.wait()
 
 
 def silu(x):
     return x * jax.nn.sigmoid(x)
 
 
-def recur_body(
-    p_ref, alog_ref, bias_ref, sv_ref, ss_ref, gain_ref, gated_ref, keys_ref, delta_ref, sd_ref
-):
+def recur_body(*refs):
+    parts = refs[:8]
+    alog_ref, bias_ref, sv_ref, ss_ref, gain_ref, gated_ref, keys_ref, delta_ref, sd_ref = refs[8:]
     rows = 16
-    t = p_ref[0:rows, :].astype(F32)
+    t = parts[0][...].astype(F32)
     for i in range(1, 8):
-        t = t + p_ref[i * rows : (i + 1) * rows, :].astype(F32)
+        t = t + parts[i][...].astype(F32)
     tail = t[:, 640:]
     lane = lax.broadcasted_iota(jnp.int32, (rows, 128), 1)
 
@@ -132,7 +181,8 @@
     ns_ref[...] = peaks.T
 
 
-def route_body(pair_ref, routes_ref, scale_ref, mt_ref, w_ref):
+def route_body(pair_ref, routes_in, scale_in, mt_ref, w_ref):
+    routes_ref, scale_ref = routes_in.get(), scale_in.get()
     n = 1024
     lane = lax.broadcasted_iota(jnp.int32, (8, n), 1)
     expert = lane // 16 * 4 + pair_ref[0]
@@ -160,9 +210,25 @@
     w_ref[...] = jnp.concatenate(weights, axis=0).astype(BF16)
 
 
-def dispatch_body(h_ref, gain_ref, mt_ref, out_ref):
-    h = h_ref[...].astype(F32)
-    h3 = h.reshape(8, 8, 256)
+def outproj_body(sub_ref, *refs):
+    parts, w_ref, out_ref, scr = refs[:8], refs[8], refs[9], refs[10]
+    for k in range(8):
+        source = lax.rem(sub_ref[0] + 8 - k, 8)
+        scr[pl.ds(pl.multiple_of(source * 16, 16), 16), :] = parts[k][...]
+    out_ref[...] = jnp.dot(scr[...], w_ref[...], preferred_element_type=F32).astype(BF16)
+
+
+def hidden_body(attn_ref, resid_ref, out_ref):
+    attn = jnp.sum(attn_ref[...].astype(F32), axis=0)
+    out_ref[...] = (resid_ref[...] + attn).astype(BF16)
+
+
+def dispatch_body(sub_ref, *refs):
+    parts, gain_ref, mt_ref, out_ref, scr = refs[:8], refs[8], refs[9], refs[10], refs[11]
+    for k in range(8):
+        source = lax.rem(sub_ref[0] + 8 - k, 8)
+        scr[pl.ds(pl.multiple_of(source * 8, 8), 8), :] = parts[k][...].astype(F32)
+    h3 = scr[...].reshape(8, 8, 256)
     sq = jnp.sum(jnp.sum(h3 * h3, axis=0), axis=1, keepdims=True)
     rs = lax.rsqrt(sq / D + 1e-05)
     normed = (h3 * rs[None] * gain_ref[...]).reshape(64, 256).astype(BF16)
@@ -193,8 +259,20 @@
         ].astype(BF16)
 
 
-def combine_body(w_ref, x_ref, out_ref):
-    out_ref[...] = jnp.dot(w_ref[...], x_ref[...], preferred_element_type=F32).astype(BF16)
+def combine_body(sub_ref, w_ref, x_ref, *rest):
+    outs, scr = rest[:8], rest[8]
+    scr[...] = jnp.dot(w_ref[...], x_ref[...], preferred_element_type=F32)
+    for k in range(8):
+        to = lax.rem(sub_ref[0] + k, 8)
+        outs[k][...] = scr[pl.ds(pl.multiple_of(to * 8, 8), 8), :].astype(BF16)
+
+
+def final_body(h_ref, *refs):
+    parts, out_ref = refs[:8], refs[8]
+    moe = parts[0][...].astype(F32)
+    for k in range(1, 8):
+        moe = moe + parts[k][...].astype(F32)
+    out_ref[...] = (h_ref[...].astype(F32) + moe).astype(BF16)
 
 
 def shape(dims, dtype=BF16):
@@ -203,6 +281,13 @@
 
 def a2a(x, axes):
     return lax.all_to_all(x, axes, split_axis=0, concat_axis=0, tiled=True)
+
+
+def exchange(pieces):
+    n = len(pieces)
+    return [pieces[0]] + [
+        lax.ppermute(pieces[k], "sub", [(i, (i + k) % n) for i in range(n)]) for k in range(1, n)
+    ]
 
 
 def local(
@@ -222,46 +307,74 @@
     w_gate_up,
     w_down,
 ):
-    pair = (lax.axis_index("sub") // 2).astype(jnp.int32).reshape(1)
+    sub = lax.axis_index("sub").astype(jnp.int32).reshape(1)
+    head = lax.axis_index("head").astype(jnp.int32).reshape(1)
     sv = state_values.reshape(16, 128, 128)
     ss = state_scales.reshape(16, 128)
     part = call(
         project_body,
-        shape((128, 768)),
-        [VM] * 4,
-        (inputs, in_gain.reshape(1, 256), w_qkvz, w_ab.T),
-    )
-    part = a2a(part, "sub")
+        (shape((16, 768)),) * 8
+        + (
+            shape((8, 256), F32),
+            shape((16, 128, 128)),
+            shape((16, 128), F32),
+            shape((1, 128), F32),
+            shape((128, 256)),
+            shape((8, 1, 256), F32),
+        ),
+        [SM, SM, HB, HB, HB, HB] + [KEEP] * 5,
+        (
+            sub,
+            head,
+            inputs,
+            in_gain.reshape(1, 256),
+            w_qkvz,
+            w_ab.T,
+            sv,
+            ss,
+            norm_gain.reshape(1, 128),
+            w_out,
+            post_gain.reshape(8, 1, 256),
+        ),
+        [pltpu.VMEM((128, 768), BF16), pltpu.SemaphoreType.DMA((5,))],
+    )
+    part, (resid, sv, ss, ngain, w_out, pgain) = part[:8], part[8:]
+    part = exchange(part)
     mt, wsel = call(
         route_body,
         (shape((1024, 64)), shape((64, 1024))),
-        [SM, VM, VM],
-        (pair, routes, route_scale),
+        [SM, HB, HB],
+        (sub // 2, routes, route_scale),
     )
     gated, keys, delta, sd = call(
         recur_body,
         (shape((16, 128)), shape((16, 128), F32), shape((16, 128), F32), shape((16, 128), F32)),
-        [VM, SM, SM, VM, VM, VM],
-        (part, a_log, dt_bias, sv, ss, norm_gain.reshape(1, 128)),
-    )
-    gathered = a2a(jnp.broadcast_to(gated[None], (8, 16, 128)), "sub").reshape(128, 128)
+        [VM] * 8 + [SM, SM, VM, VM, VM],
+        (*part, a_log, dt_bias, sv, ss, ngain),
+    )
+    gathered = exchange([gated] * 8)
     new_values, new_scales = call(
         state_body,
         (shape((16, 128, 128)), shape((16, 128), F32)),
         [VM] * 4,
         (sv, sd, keys, delta),
     )
-    attn = jnp.dot(gathered, w_out, preferred_element_type=F32).astype(BF16)
-    attn = a2a(attn, "head").reshape(16, 8, 256)
-    attn = jnp.sum(attn.astype(F32), axis=0)
-    resid = lax.dynamic_slice_in_dim(inputs, lax.axis_index("head") * 8, 8, 0).astype(F32)
-    hidden = (resid + attn).astype(BF16)
-    whole = a2a(jnp.broadcast_to(hidden[None], (8, 8, 256)), "sub").reshape(64, 256)
+    attn = call(
+        outproj_body,
+        shape((128, 256)),
+        [SM] + [VM] * 9,
+        (sub, *gathered, w_out),
+        [pltpu.VMEM((128, 128), BF16)],
+    )
+    attn = a2a(attn.reshape(16, 8, 256), "head")
+    hidden = call(hidden_body, shape((8, 256)), [VM, VM], (attn, resid))
+    whole = exchange([hidden] * 8)
     buffer = call(
         dispatch_body,
         shape((1024, 256)),
-        [VM] * 3,
-        (whole, post_gain.reshape(8, 1, 256), mt),
+        [SM] + [VM] * 10,
+        (sub, *whole, pgain, mt),
+        [pltpu.VMEM((64, 256), F32)],
     )
     received = a2a(buffer.reshape(64, 16, 256), ("grp", "head")).reshape(1024, 256)
     result = call(
@@ -272,10 +385,15 @@
         [pltpu.VMEM((2048, 128), F32)],
     )
     back = a2a(result.reshape(64, 16, 256), ("grp", "head")).reshape(1024, 256)
-    moe = call(combine_body, shape((64, 256)), [VM] * 2, (wsel, back))
-    moe = a2a(moe.reshape(8, 8, 256), "sub")
-    moe = jnp.sum(moe.astype(F32), axis=0)
-    out = (hidden.astype(F32) + moe).astype(BF16)
+    moe = call(
+        combine_body,
+        (shape((8, 256)),) * 8,
+        [SM, VM, VM],
+        (sub, wsel, back),
+        [pltpu.VMEM((64, 256), F32)],
+    )
+    moe = exchange(moe)
+    out = call(final_body, shape((8, 256)), [VM] * 9, (hidden, *moe))
     return (out, new_values.reshape(16, 1, 128, 128), new_scales.reshape(16, 1, 128))
 
 

time: 130 us -> 194 us (1.49)
  starting transfers between devices: 28.5 us -> 104 us
  waiting for transfers between devices: 24.3 us -> 4.49 us
  blocking collectives: 56.5 us -> 72.6 us
  local copies, waits for them, and re-layouts: 8.37 us -> 0.01 us
    ppermute x0 -> x28, starting transfers between devices: none -> 104 us  [exchange(): lax.ppermute(pieces[k], 'sub', [(i, (i + k) % n) for i in range(n)])]
    all_to_all x4 -> x0, starting transfers between devices: 28.5 us -> none  [a2a(): return lax.all_to_all(x, axes, split_axis=0, concat_axis=0, tiled=True)]
    all_to_all x4 -> x0, waiting for transfers between devices: 24.3 us -> none  [a2a(): return lax.all_to_all(x, axes, split_axis=0, concat_axis=0, tiled=True)]
    all_to_all x3, blocking collectives: 56.5 us -> 72.6 us  [a2a(): return lax.all_to_all(x, axes, split_axis=0, concat_axis=0, tiled=True)]
    unnamed x28 -> x4, local copies, waits for them, and re-layouts: 7.74 us -> 0.01 us
    ppermute x0 -> x28, waiting for transfers between devices: none -> 4.49 us  [exchange(): lax.ppermute(pieces[k], 'sub', [(i, (i + k) % n) for i in range(n)])]
    pallas_call x7 -> x10, Pallas kernels: 7.14 us -> 8.83 us  [call(): pl.pallas_call(kernel, out_shape=outs, in_specs=ins, out_specs=jax.tree.m...]
  transfers between devices with their start and end apart: 4 -> 28, of which waited for: 4 -> 4; matrix products, arithmetic and copies ran while one was open for 0% -> 0% of each run, Pallas kernels for 2% -> 2%
where the time goes in v2:
time: 194 us; the launch traced here: 192 us
  starting transfers between devices  104 us (54%)
  blocking collectives  72.6 us (37%)
  Pallas kernels  8.83 us (5%)
  waiting for transfers between devices  4.49 us (2%)
  between operations  2.4 us (1%)
    ppermute x28, starting transfers between devices, exchange(): lax.ppermute(pieces[k], 'sub', [(i, (i + k) % n) for i in range(n)])  104 us
    all_to_all x3, blocking collectives, a2a(): return lax.all_to_all(x, axes, split_axis=0, concat_axis=0, tiled=True)  72.6 us
    pallas_call x10, Pallas kernels, call(): pl.pallas_call(kernel, out_shape=outs, in_specs=ins, out_specs=jax.tree.m...  8.83 us
    ppermute x28, waiting for transfers between devices, exchange(): lax.ppermute(pieces[k], 'sub', [(i, (i + k) % n) for i in range(n)])  4.49 us
  transfers between devices with their start and end apart: 28, of which 4 were waited for; matrix products, arithmetic and copies ran while one was open for 0% of the time, Pallas kernels for 2%

profile of v2, /device:TPU:1, one launch (start us, length us, event | category | flops | bytes accessed | tf_op | source)
XLA Modules:
  0.0 192.0 jit_solution(11853870468311698225)
XLA Ops:
  2.3 4.0 %collective-permute-start = (bf16[16,768]{1,0:T(8,128)(2,1)S(1)}, bf16[16,768]{1,0:T(8,128)(2,1)S(1)}, u32[]{:S(2)}, u32[]{:S(2)}) collective-permute-start(bf16[16,768]{1,0:T(8,128)(2,1)S(1)} %get-tuple-element.34), channel_id=1, source_target_pairs={{0,1},{1,2},{2,3},{3,4},{4,5},{5,6},{6,7},{7,0},{8,9},{9,10},{10,1... | collective-permute-start | bytes 73736 | tf_op jit(solution)/shard_map/ppermute | solution.py:289
  6.3 4.2 %collective-permute-start.1 = (bf16[16,768]{1,0:T(8,128)(2,1)S(1)}, bf16[16,768]{1,0:T(8,128)(2,1)S(1)}, u32[]{:S(2)}, u32[]{:S(2)}) collective-permute-start(bf16[16,768]{1,0:T(8,128)(2,1)S(1)} %get-tuple-element.35), channel_id=1, source_target_pairs={{0,2},{1,3},{2,4},{3,5},{4,6},{5,7},{6,0},{7,1},{8,10},{9,11},{10,... | collective-permute-start | bytes 73736 | tf_op jit(solution)/shard_map/ppermute | solution.py:289
  10.6 4.6 %collective-permute-start.2 = (bf16[16,768]{1,0:T(8,128)(2,1)S(1)}, bf16[16,768]{1,0:T(8,128)(2,1)S(1)}, u32[]{:S(2)}, u32[]{:S(2)}) collective-permute-start(bf16[16,768]{1,0:T(8,128)(2,1)S(1)} %get-tuple-element.36), channel_id=1, source_target_pairs={{0,3},{1,4},{2,5},{3,6},{4,7},{5,0},{6,1},{7,2},{8,11},{9,12},{10,... | collective-permute-start | bytes 73736 | tf_op jit(solution)/shard_map/ppermute | solution.py:289
  15.2 3.5 %collective-permute-start.3 = (bf16[16,768]{1,0:T(8,128)(2,1)S(1)}, bf16[16,768]{1,0:T(8,128)(2,1)S(1)}, u32[]{:S(2)}, u32[]{:S(2)}) collective-permute-start(bf16[16,768]{1,0:T(8,128)(2,1)S(1)} %get-tuple-element.37), channel_id=1, source_target_pairs={{0,4},{1,5},{2,6},{3,7},{4,0},{5,1},{6,2},{7,3},{8,12},{9,13},{10,... | collective-permute-start | bytes 73736 | tf_op jit(solution)/shard_map/ppermute | solution.py:289
  18.8 4.9 %collective-permute-start.4 = (bf16[16,768]{1,0:T(8,128)(2,1)S(1)}, bf16[16,768]{1,0:T(8,128)(2,1)S(1)}, u32[]{:S(2)}, u32[]{:S(2)}) collective-permute-start(bf16[16,768]{1,0:T(8,128)(2,1)S(1)} %get-tuple-element.38), channel_id=1, source_target_pairs={{0,5},{1,6},{2,7},{3,0},{4,1},{5,2},{6,3},{7,4},{8,13},{9,14},{10,... | collective-permute-start | bytes 73736 | tf_op jit(solution)/shard_map/ppermute | solution.py:289
  23.7 5.0 %collective-permute-start.5 = (bf16[16,768]{1,0:T(8,128)(2,1)S(1)}, bf16[16,768]{1,0:T(8,128)(2,1)S(1)}, u32[]{:S(2)}, u32[]{:S(2)}) collective-permute-start(bf16[16,768]{1,0:T(8,128)(2,1)S(1)} %get-tuple-element.39), channel_id=1, source_target_pairs={{0,6},{1,7},{2,0},{3,1},{4,2},{5,3},{6,4},{7,5},{8,14},{9,15},{10,... | collective-permute-start | bytes 73736 | tf_op jit(solution)/shard_map/ppermute | solution.py:289
  28.6 3.0 %collective-permute-start.6 = (bf16[16,768]{1,0:T(8,128)(2,1)S(1)}, bf16[16,768]{1,0:T(8,128)(2,1)S(1)}, u32[]{:S(2)}, u32[]{:S(2)}) collective-permute-start(bf16[16,768]{1,0:T(8,128)(2,1)S(1)} %get-tuple-element.40), channel_id=1, source_target_pairs={{0,7},{1,0},{2,1},{3,2},{4,3},{5,4},{6,5},{7,6},{8,15},{9,8},{10,9... | collective-permute-start | bytes 73736 | tf_op jit(solution)/shard_map/ppermute | solution.py:289
  34.7 3.9 %collective-permute-start.13 = (bf16[16,128]{1,0:T(8,128)(2,1)S(1)}, bf16[16,128]{1,0:T(8,128)(2,1)S(1)}, u32[]{:S(2)}, u32[]{:S(2)}) collective-permute-start(bf16[16,128]{1,0:T(8,128)(2,1)S(1)} %get-tuple-element.44.refs_1_), channel_id=1, source_target_pairs={{0,7},{1,0},{2,1},{3,2},{4,3},{5,4},{6,5},{7,6},{8,15},{9,8},{10,9... | collective-permute-start | bytes 12296 | tf_op jit(solution)/shard_map/ppermute | solution.py:289
  43.3 6.4 %collective-permute-start.10 = (bf16[16,128]{1,0:T(8,128)(2,1)S(1)}, bf16[16,128]{1,0:T(8,128)(2,1)S(1)}, u32[]{:S(2)}, u32[]{:S(2)}) collective-permute-start(bf16[16,128]{1,0:T(8,128)(2,1)S(1)} %get-tuple-element.44.refs_1_), channel_id=1, source_target_pairs={{0,4},{1,5},{2,6},{3,7},{4,0},{5,1},{6,2},{7,3},{8,12},{9,13},{10,... | collective-permute-start | bytes 12296 | tf_op jit(solution)/shard_map/ppermute | solution.py:289
  51.8 3.5 %collective-permute-start.8 = (bf16[16,128]{1,0:T(8,128)(2,1)S(1)}, bf16[16,128]{1,0:T(8,128)(2,1)S(1)}, u32[]{:S(2)}, u32[]{:S(2)}) collective-permute-start(bf16[16,128]{1,0:T(8,128)(2,1)S(1)} %get-tuple-element.44.refs_1_), channel_id=1, source_target_pairs={{0,2},{1,3},{2,4},{3,5},{4,6},{5,7},{6,0},{7,1},{8,10},{9,11},{10,... | collective-permute-start | bytes 12296 | tf_op jit(solution)/shard_map/ppermute | solution.py:289
  61.0 24.0 %all_to_all.15.refs_0_ = bf16[16,8,256]{2,1,0:T(8,128)(2,1)S(1)} all-to-all(bf16[16,8,256]{2,1,0:T(8,128)(2,1)S(1)} %bitcast.23), channel_id=1, replica_groups=mesh['grp'=4,'head'=16,'sub'=8] {'head'}, dimensions={0} | all-to-all | bytes 131072 | tf_op jit(solution)/shard_map/all_to_all | solution.py:283
  87.7 4.0 %collective-permute-start.19 = (bf16[8,256]{1,0:T(8,128)(2,1)S(1)}, bf16[8,256]{1,0:T(8,128)(2,1)S(1)}, u32[]{:S(2)}, u32[]{:S(2)}) collective-permute-start(bf16[8,256]{1,0:T(8,128)(2,1)S(1)} %shard_map.169.refs_1_.refs_0_), channel_id=1, source_target_pairs={{0,6},{1,7},{2,0},{3,1},{4,2},{5,3},{6,4},{7,5},{8,14},{9,15},{10,... | collective-permute-start | bytes 12296 | tf_op jit(solution)/shard_map/ppermute | solution.py:289
  91.7 4.6 %collective-permute-start.18 = (bf16[8,256]{1,0:T(8,128)(2,1)S(1)}, bf16[8,256]{1,0:T(8,128)(2,1)S(1)}, u32[]{:S(2)}, u32[]{:S(2)}) collective-permute-start(bf16[8,256]{1,0:T(8,128)(2,1)S(1)} %shard_map.169.refs_1_.refs_0_), channel_id=1, source_target_pairs={{0,5},{1,6},{2,7},{3,0},{4,1},{5,2},{6,3},{7,4},{8,13},{9,14},{10,... | collective-permute-start | bytes 12296 | tf_op jit(solution)/shard_map/ppermute | solution.py:289
  96.3 3.7 %collective-permute-start.17 = (bf16[8,256]{1,0:T(8,128)(2,1)S(1)}, bf16[8,256]{1,0:T(8,128)(2,1)S(1)}, u32[]{:S(2)}, u32[]{:S(2)}) collective-permute-start(bf16[8,256]{1,0:T(8,128)(2,1)S(1)} %shard_map.169.refs_1_.refs_0_), channel_id=1, source_target_pairs={{0,4},{1,5},{2,6},{3,7},{4,0},{5,1},{6,2},{7,3},{8,12},{9,13},{10,... | collective-permute-start | bytes 12296 | tf_op jit(solution)/shard_map/ppermute | solution.py:289
  100.0 3.4 %collective-permute-start.16 = (bf16[8,256]{1,0:T(8,128)(2,1)S(1)}, bf16[8,256]{1,0:T(8,128)(2,1)S(1)}, u32[]{:S(2)}, u32[]{:S(2)}) collective-permute-start(bf16[8,256]{1,0:T(8,128)(2,1)S(1)} %shard_map.169.refs_1_.refs_0_), channel_id=1, source_target_pairs={{0,3},{1,4},{2,5},{3,6},{4,7},{5,0},{6,1},{7,2},{8,11},{9,12},{10,... | collective-permute-start | bytes 12296 | tf_op jit(solution)/shard_map/ppermute | solution.py:289
  103.4 5.2 %collective-permute-start.15 = (bf16[8,256]{1,0:T(8,128)(2,1)S(1)}, bf16[8,256]{1,0:T(8,128)(2,1)S(1)}, u32[]{:S(2)}, u32[]{:S(2)}) collective-permute-start(bf16[8,256]{1,0:T(8,128)(2,1)S(1)} %shard_map.169.refs_1_.refs_0_), channel_id=1, source_target_pairs={{0,2},{1,3},{2,4},{3,5},{4,6},{5,7},{6,0},{7,1},{8,10},{9,11},{10,... | collective-permute-start | bytes 12296 | tf_op jit(solution)/shard_map/ppermute | solution.py:289
  108.7 3.4 %collective-permute-start.14 = (bf16[8,256]{1,0:T(8,128)(2,1)S(1)}, bf16[8,256]{1,0:T(8,128)(2,1)S(1)}, u32[]{:S(2)}, u32[]{:S(2)}) collective-permute-start(bf16[8,256]{1,0:T(8,128)(2,1)S(1)} %shard_map.169.refs_1_.refs_0_), channel_id=1, source_target_pairs={{0,1},{1,2},{2,3},{3,4},{4,5},{5,6},{6,7},{7,0},{8,9},{9,10},{10,1... | collective-permute-start | bytes 12296 | tf_op jit(solution)/shard_map/ppermute | solution.py:289
  114.6 25.2 %all_to_all.16 = bf16[64,16,256]{2,1,0:T(8,128)(2,1)S(1)} all-to-all(bf16[64,16,256]{2,1,0:T(8,128)(2,1)S(1)} %bitcast.20), channel_id=1, replica_groups=mesh['grp'=4,'head'=16,'sub'=8] {'grp','head'}, dimensions={0} | all-to-all | bytes 1048576 | tf_op jit(solution)/shard_map/all_to_all | solution.py:283
  140.7 23.4 %all_to_all.17 = bf16[64,16,256]{2,1,0:T(8,128)(2,1)S(1)} all-to-all(bf16[64,16,256]{2,1,0:T(8,128)(2,1)S(1)} %bitcast.22), channel_id=1, replica_groups=mesh['grp'=4,'head'=16,'sub'=8] {'grp','head'}, dimensions={0} | all-to-all | bytes 1048576 | tf_op jit(solution)/shard_map/all_to_all | solution.py:283
  168.7 3.2 %collective-permute-start.23 = (bf16[8,256]{1,0:T(8,128)(2,1)S(1)}, bf16[8,256]{1,0:T(8,128)(2,1)S(1)}, u32[]{:S(2)}, u32[]{:S(2)}) collective-permute-start(bf16[8,256]{1,0:T(8,128)(2,1)S(1)} %get-tuple-element.53), channel_id=1, source_target_pairs={{0,3},{1,4},{2,5},{3,6},{4,7},{5,0},{6,1},{7,2},{8,11},{9,12},{10,... | collective-permute-start | bytes 12296 | tf_op jit(solution)/shard_map/ppermute | solution.py:289
  171.9 6.0 %collective-permute-start.24 = (bf16[8,256]{1,0:T(8,128)(2,1)S(1)}, bf16[8,256]{1,0:T(8,128)(2,1)S(1)}, u32[]{:S(2)}, u32[]{:S(2)}) collective-permute-start(bf16[8,256]{1,0:T(8,128)(2,1)S(1)} %get-tuple-element.54), channel_id=1, source_target_pairs={{0,4},{1,5},{2,6},{3,7},{4,0},{5,1},{6,2},{7,3},{8,12},{9,13},{10,... | collective-permute-start | bytes 12296 | tf_op jit(solution)/shard_map/ppermute | solution.py:289
  177.9 4.0 %collective-permute-start.25 = (bf16[8,256]{1,0:T(8,128)(2,1)S(1)}, bf16[8,256]{1,0:T(8,128)(2,1)S(1)}, u32[]{:S(2)}, u32[]{:S(2)}) collective-permute-start(bf16[8,256]{1,0:T(8,128)(2,1)S(1)} %get-tuple-element.55), channel_id=1, source_target_pairs={{0,5},{1,6},{2,7},{3,0},{4,1},{5,2},{6,3},{7,4},{8,13},{9,14},{10,... | collective-permute-start | bytes 12296 | tf_op jit(solution)/shard_map/ppermute | solution.py:289
  182.0 3.1 %collective-permute-start.26 = (bf16[8,256]{1,0:T(8,128)(2,1)S(1)}, bf16[8,256]{1,0:T(8,128)(2,1)S(1)}, u32[]{:S(2)}, u32[]{:S(2)}) collective-permute-start(bf16[8,256]{1,0:T(8,128)(2,1)S(1)} %get-tuple-element.56), channel_id=1, source_target_pairs={{0,6},{1,7},{2,0},{3,1},{4,2},{5,3},{6,4},{7,5},{8,14},{9,15},{10,... | collective-permute-start | bytes 12296 | tf_op jit(solution)/shard_map/ppermute | solution.py:289
  185.1 3.4 %collective-permute-start.27 = (bf16[8,256]{1,0:T(8,128)(2,1)S(1)}, bf16[8,256]{1,0:T(8,128)(2,1)S(1)}, u32[]{:S(2)}, u32[]{:S(2)}) collective-permute-start(bf16[8,256]{1,0:T(8,128)(2,1)S(1)} %get-tuple-element.57), channel_id=1, source_target_pairs={{0,7},{1,0},{2,1},{3,2},{4,3},{5,4},{6,5},{7,6},{8,15},{9,8},{10,9... | collective-permute-start | bytes 12296 | tf_op jit(solution)/shard_map/ppermute | solution.py:289
  (49 shorter events, 30.0 us)
Async XLA Ops:
  2.3 21.3 %collective-permute-start = (bf16[16,768]{1,0:T(8,128)(2,1)S(1)}, bf16[16,768]{1,0:T(8,128)(2,1)S(1)}, u32[]{:S(2)}, u32[]{:S(2)}) collective-permute-start(bf16[16,768]{1,0:T(8,128)(2,1)S(1)} %get-tuple-element.34), channel_id=1, source_target_pairs={{0,1},{1,2},{2,3},{3,4},{4,5},{5,6},{6,7},{7,0},{8,9},{9,10},{10,1... | collective-permute-start | bytes 73736 | tf_op jit(solution)/shard_map/ppermute | solution.py:289
  6.3 22.3 %collective-permute-start.1 = (bf16[16,768]{1,0:T(8,128)(2,1)S(1)}, bf16[16,768]{1,0:T(8,128)(2,1)S(1)}, u32[]{:S(2)}, u32[]{:S(2)}) collective-permute-start(bf16[16,768]{1,0:T(8,128)(2,1)S(1)} %get-tuple-element.35), channel_id=1, source_target_pairs={{0,2},{1,3},{2,4},{3,5},{4,6},{5,7},{6,0},{7,1},{8,10},{9,11},{10,... | collective-permute-start | bytes 73736 | tf_op jit(solution)/shard_map/ppermute | solution.py:289
  10.6 22.4 %collective-permute-start.2 = (bf16[16,768]{1,0:T(8,128)(2,1)S(1)}, bf16[16,768]{1,0:T(8,128)(2,1)S(1)}, u32[]{:S(2)}, u32[]{:S(2)}) collective-permute-start(bf16[16,768]{1,0:T(8,128)(2,1)S(1)} %get-tuple-element.36), channel_id=1, source_target_pairs={{0,3},{1,4},{2,5},{3,6},{4,7},{5,0},{6,1},{7,2},{8,11},{9,12},{10,... | collective-permute-start | bytes 73736 | tf_op jit(solution)/shard_map/ppermute | solution.py:289
  15.2 17.7 %collective-permute-start.3 = (bf16[16,768]{1,0:T(8,128)(2,1)S(1)}, bf16[16,768]{1,0:T(8,128)(2,1)S(1)}, u32[]{:S(2)}, u32[]{:S(2)}) collective-permute-start(bf16[16,768]{1,0:T(8,128)(2,1)S(1)} %get-tuple-element.37), channel_id=1, source_target_pairs={{0,4},{1,5},{2,6},{3,7},{4,0},{5,1},{6,2},{7,3},{8,12},{9,13},{10,... | collective-permute-start | bytes 73736 | tf_op jit(solution)/shard_map/ppermute | solution.py:289
  18.8 14.2 %collective-permute-start.4 = (bf16[16,768]{1,0:T(8,128)(2,1)S(1)}, bf16[16,768]{1,0:T(8,128)(2,1)S(1)}, u32[]{:S(2)}, u32[]{:S(2)}) collective-permute-start(bf16[16,768]{1,0:T(8,128)(2,1)S(1)} %get-tuple-element.38), channel_id=1, source_target_pairs={{0,5},{1,6},{2,7},{3,0},{4,1},{5,2},{6,3},{7,4},{8,13},{9,14},{10,... | collective-permute-start | bytes 73736 | tf_op jit(solution)/shard_map/ppermute | solution.py:289
  23.7 9.3 %collective-permute-start.5 = (bf16[16,768]{1,0:T(8,128)(2,1)S(1)}, bf16[16,768]{1,0:T(8,128)(2,1)S(1)}, u32[]{:S(2)}, u32[]{:S(2)}) collective-permute-start(bf16[16,768]{1,0:T(8,128)(2,1)S(1)} %get-tuple-element.39), channel_id=1, source_target_pairs={{0,6},{1,7},{2,0},{3,1},{4,2},{5,3},{6,4},{7,5},{8,14},{9,15},{10,... | collective-permute-start | bytes 73736 | tf_op jit(solution)/shard_map/ppermute | solution.py:289
  34.7 17.1 %collective-permute-start.13 = (bf16[16,128]{1,0:T(8,128)(2,1)S(1)}, bf16[16,128]{1,0:T(8,128)(2,1)S(1)}, u32[]{:S(2)}, u32[]{:S(2)}) collective-permute-start(bf16[16,128]{1,0:T(8,128)(2,1)S(1)} %get-tuple-element.44.refs_1_), channel_id=1, source_target_pairs={{0,7},{1,0},{2,1},{3,2},{4,3},{5,4},{6,5},{7,6},{8,15},{9,8},{10,9... | collective-permute-start | bytes 12296 | tf_op jit(solution)/shard_map/ppermute | solution.py:289
  38.6 16.6 %collective-permute-start.12 = (bf16[16,128]{1,0:T(8,128)(2,1)S(1)}, bf16[16,128]{1,0:T(8,128)(2,1)S(1)}, u32[]{:S(2)}, u32[]{:S(2)}) collective-permute-start(bf16[16,128]{1,0:T(8,128)(2,1)S(1)} %get-tuple-element.44.refs_1_), channel_id=1, source_target_pairs={{0,6},{1,7},{2,0},{3,1},{4,2},{5,3},{6,4},{7,5},{8,14},{9,15},{10,... | collective-permute-start | bytes 12296 | tf_op jit(solution)/shard_map/ppermute | solution.py:289
  40.5 17.6 %collective-permute-start.11 = (bf16[16,128]{1,0:T(8,128)(2,1)S(1)}, bf16[16,128]{1,0:T(8,128)(2,1)S(1)}, u32[]{:S(2)}, u32[]{:S(2)}) collective-permute-start(bf16[16,128]{1,0:T(8,128)(2,1)S(1)} %get-tuple-element.44.refs_1_), channel_id=1, source_target_pairs={{0,5},{1,6},{2,7},{3,0},{4,1},{5,2},{6,3},{7,4},{8,13},{9,14},{10,... | collective-permute-start | bytes 12296 | tf_op jit(solution)/shard_map/ppermute | solution.py:289
  43.3 14.9 %collective-permute-start.10 = (bf16[16,128]{1,0:T(8,128)(2,1)S(1)}, bf16[16,128]{1,0:T(8,128)(2,1)S(1)}, u32[]{:S(2)}, u32[]{:S(2)}) collective-permute-start(bf16[16,128]{1,0:T(8,128)(2,1)S(1)} %get-tuple-element.44.refs_1_), channel_id=1, source_target_pairs={{0,4},{1,5},{2,6},{3,7},{4,0},{5,1},{6,2},{7,3},{8,12},{9,13},{10,... | collective-permute-start | bytes 12296 | tf_op jit(solution)/shard_map/ppermute | solution.py:289
  49.7 8.4 %collective-permute-start.9 = (bf16[16,128]{1,0:T(8,128)(2,1)S(1)}, bf16[16,128]{1,0:T(8,128)(2,1)S(1)}, u32[]{:S(2)}, u32[]{:S(2)}) collective-permute-start(bf16[16,128]{1,0:T(8,128)(2,1)S(1)} %get-tuple-element.44.refs_1_), channel_id=1, source_target_pairs={{0,3},{1,4},{2,5},{3,6},{4,7},{5,0},{6,1},{7,2},{8,11},{9,12},{10,... | collective-permute-start | bytes 12296 | tf_op jit(solution)/shard_map/ppermute | solution.py:289
  51.8 7.6 %collective-permute-start.8 = (bf16[16,128]{1,0:T(8,128)(2,1)S(1)}, bf16[16,128]{1,0:T(8,128)(2,1)S(1)}, u32[]{:S(2)}, u32[]{:S(2)}) collective-permute-start(bf16[16,128]{1,0:T(8,128)(2,1)S(1)} %get-tuple-element.44.refs_1_), channel_id=1, source_target_pairs={{0,2},{1,3},{2,4},{3,5},{4,6},{5,7},{6,0},{7,1},{8,10},{9,11},{10,... | collective-permute-start | bytes 12296 | tf_op jit(solution)/shard_map/ppermute | solution.py:289
  85.0 18.4 %collective-permute-start.20 = (bf16[8,256]{1,0:T(8,128)(2,1)S(1)}, bf16[8,256]{1,0:T(8,128)(2,1)S(1)}, u32[]{:S(2)}, u32[]{:S(2)}) collective-permute-start(bf16[8,256]{1,0:T(8,128)(2,1)S(1)} %shard_map.169.refs_1_.refs_0_), channel_id=1, source_target_pairs={{0,7},{1,0},{2,1},{3,2},{4,3},{5,4},{6,5},{7,6},{8,15},{9,8},{10,9... | collective-permute-start | bytes 12296 | tf_op jit(solution)/shard_map/ppermute | solution.py:289
  87.7 20.9 %collective-permute-start.19 = (bf16[8,256]{1,0:T(8,128)(2,1)S(1)}, bf16[8,256]{1,0:T(8,128)(2,1)S(1)}, u32[]{:S(2)}, u32[]{:S(2)}) collective-permute-start(bf16[8,256]{1,0:T(8,128)(2,1)S(1)} %shard_map.169.refs_1_.refs_0_), channel_id=1, source_target_pairs={{0,6},{1,7},{2,0},{3,1},{4,2},{5,3},{6,4},{7,5},{8,14},{9,15},{10,... | collective-permute-start | bytes 12296 | tf_op jit(solution)/shard_map/ppermute | solution.py:289
  91.7 21.3 %collective-permute-start.18 = (bf16[8,256]{1,0:T(8,128)(2,1)S(1)}, bf16[8,256]{1,0:T(8,128)(2,1)S(1)}, u32[]{:S(2)}, u32[]{:S(2)}) collective-permute-start(bf16[8,256]{1,0:T(8,128)(2,1)S(1)} %shard_map.169.refs_1_.refs_0_), channel_id=1, source_target_pairs={{0,5},{1,6},{2,7},{3,0},{4,1},{5,2},{6,3},{7,4},{8,13},{9,14},{10,... | collective-permute-start | bytes 12296 | tf_op jit(solution)/shard_map/ppermute | solution.py:289
  96.3 16.7 %collective-permute-start.17 = (bf16[8,256]{1,0:T(8,128)(2,1)S(1)}, bf16[8,256]{1,0:T(8,128)(2,1)S(1)}, u32[]{:S(2)}, u32[]{:S(2)}) collective-permute-start(bf16[8,256]{1,0:T(8,128)(2,1)S(1)} %shard_map.169.refs_1_.refs_0_), channel_id=1, source_target_pairs={{0,4},{1,5},{2,6},{3,7},{4,0},{5,1},{6,2},{7,3},{8,12},{9,13},{10,... | collective-permute-start | bytes 12296 | tf_op jit(solution)/shard_map/ppermute | solution.py:289
  100.0 13.0 %collective-permute-start.16 = (bf16[8,256]{1,0:T(8,128)(2,1)S(1)}, bf16[8,256]{1,0:T(8,128)(2,1)S(1)}, u32[]{:S(2)}, u32[]{:S(2)}) collective-permute-start(bf16[8,256]{1,0:T(8,128)(2,1)S(1)} %shard_map.169.refs_1_.refs_0_), channel_id=1, source_target_pairs={{0,3},{1,4},{2,5},{3,6},{4,7},{5,0},{6,1},{7,2},{8,11},{9,12},{10,... | collective-permute-start | bytes 12296 | tf_op jit(solution)/shard_map/ppermute | solution.py:289
  103.4 9.6 %collective-permute-start.15 = (bf16[8,256]{1,0:T(8,128)(2,1)S(1)}, bf16[8,256]{1,0:T(8,128)(2,1)S(1)}, u32[]{:S(2)}, u32[]{:S(2)}) collective-permute-start(bf16[8,256]{1,0:T(8,128)(2,1)S(1)} %shard_map.169.refs_1_.refs_0_), channel_id=1, source_target_pairs={{0,2},{1,3},{2,4},{3,5},{4,6},{5,7},{6,0},{7,1},{8,10},{9,11},{10,... | collective-permute-start | bytes 12296 | tf_op jit(solution)/shard_map/ppermute | solution.py:289
  164.4 17.6 %collective-permute-start.21 = (bf16[8,256]{1,0:T(8,128)(2,1)S(1)}, bf16[8,256]{1,0:T(8,128)(2,1)S(1)}, u32[]{:S(2)}, u32[]{:S(2)}) collective-permute-start(bf16[8,256]{1,0:T(8,128)(2,1)S(1)} %get-tuple-element.51), channel_id=1, source_target_pairs={{0,1},{1,2},{2,3},{3,4},{4,5},{5,6},{6,7},{7,0},{8,9},{9,10},{10,1... | collective-permute-start | bytes 12296 | tf_op jit(solution)/shard_map/ppermute | solution.py:289
  166.8 18.3 %collective-permute-start.22 = (bf16[8,256]{1,0:T(8,128)(2,1)S(1)}, bf16[8,256]{1,0:T(8,128)(2,1)S(1)}, u32[]{:S(2)}, u32[]{:S(2)}) collective-permute-start(bf16[8,256]{1,0:T(8,128)(2,1)S(1)} %get-tuple-element.52), channel_id=1, source_target_pairs={{0,2},{1,3},{2,4},{3,5},{4,6},{5,7},{6,0},{7,1},{8,10},{9,11},{10,... | collective-permute-start | bytes 12296 | tf_op jit(solution)/shard_map/ppermute | solution.py:289
  168.7 22.7 %collective-permute-start.23 = (bf16[8,256]{1,0:T(8,128)(2,1)S(1)}, bf16[8,256]{1,0:T(8,128)(2,1)S(1)}, u32[]{:S(2)}, u32[]{:S(2)}) collective-permute-start(bf16[8,256]{1,0:T(8,128)(2,1)S(1)} %get-tuple-element.53), channel_id=1, source_target_pairs={{0,3},{1,4},{2,5},{3,6},{4,7},{5,0},{6,1},{7,2},{8,11},{9,12},{10,... | collective-permute-start | bytes 12296 | tf_op jit(solution)/shard_map/ppermute | solution.py:289
  171.9 19.5 %collective-permute-start.24 = (bf16[8,256]{1,0:T(8,128)(2,1)S(1)}, bf16[8,256]{1,0:T(8,128)(2,1)S(1)}, u32[]{:S(2)}, u32[]{:S(2)}) collective-permute-start(bf16[8,256]{1,0:T(8,128)(2,1)S(1)} %get-tuple-element.54), channel_id=1, source_target_pairs={{0,4},{1,5},{2,6},{3,7},{4,0},{5,1},{6,2},{7,3},{8,12},{9,13},{10,... | collective-permute-start | bytes 12296 | tf_op jit(solution)/shard_map/ppermute | solution.py:289
  177.9 13.5 %collective-permute-start.25 = (bf16[8,256]{1,0:T(8,128)(2,1)S(1)}, bf16[8,256]{1,0:T(8,128)(2,1)S(1)}, u32[]{:S(2)}, u32[]{:S(2)}) collective-permute-start(bf16[8,256]{1,0:T(8,128)(2,1)S(1)} %get-tuple-element.55), channel_id=1, source_target_pairs={{0,5},{1,6},{2,7},{3,0},{4,1},{5,2},{6,3},{7,4},{8,13},{9,14},{10,... | collective-permute-start | bytes 12296 | tf_op jit(solution)/shard_map/ppermute | solution.py:289
  182.0 9.4 %collective-permute-start.26 = (bf16[8,256]{1,0:T(8,128)(2,1)S(1)}, bf16[8,256]{1,0:T(8,128)(2,1)S(1)}, u32[]{:S(2)}, u32[]{:S(2)}) collective-permute-start(bf16[8,256]{1,0:T(8,128)(2,1)S(1)} %get-tuple-element.56), channel_id=1, source_target_pairs={{0,6},{1,7},{2,0},{3,1},{4,2},{5,3},{6,4},{7,5},{8,14},{9,15},{10,... | collective-permute-start | bytes 12296 | tf_op jit(solution)/shard_map/ppermute | solution.py:289
  (6 other events, 300.9 us)

commit v3 on v2

--- a/solution.py
+++ b/solution.py
@@ -65,8 +65,8 @@
     return hi, x - hi
 
 
-def project_body(sub_ref, head_ref, x_in, gain_in, w_in, wab_in, *rest):
-    held, outs, resid_ref, kept, scr, sems = rest[:5], rest[5:13], rest[13], rest[14:19], rest[19], rest[20]
+def project_body(head_ref, x_in, gain_in, w_in, wab_in, *rest):
+    held, out_ref, resid_ref, kept, sems = rest[:5], rest[5], rest[6], rest[7:12], rest[12]
     copies = [pltpu.make_async_copy(held[i], kept[i], sems.at[i]) for i in range(5)]
     for copy in copies:
         copy.start()
@@ -90,16 +90,13 @@
         tail = jnp.where(lane == at, hi, tail)
         tail = jnp.where(lane == at + 1, lo, tail)
         at += 2
-    scr[:, 640:] = tail.astype(BF16)
+    out_ref[:, 640:] = tail.astype(BF16)
     proj = jnp.dot(xg, w_in.get()[...], preferred_element_type=F32)
     key_hi, key_lo = split_hi(proj[:, 128:256])
-    scr[:, :128] = proj[:, :128].astype(BF16)
-    scr[:, 128:256] = key_hi.astype(BF16)
-    scr[:, 256:512] = proj[:, 256:].astype(BF16)
-    scr[:, 512:640] = key_lo.astype(BF16)
-    for k in range(8):
-        to = lax.rem(sub_ref[0] + k, 8)
-        outs[k][...] = scr[pl.ds(pl.multiple_of(to * 16, 16), 16), :]
+    out_ref[:, :128] = proj[:, :128].astype(BF16)
+    out_ref[:, 128:256] = key_hi.astype(BF16)
+    out_ref[:, 256:512] = proj[:, 256:].astype(BF16)
+    out_ref[:, 512:640] = key_lo.astype(BF16)
     for copy in copies:
         copy.wait()
 
@@ -108,13 +105,13 @@
     return x * jax.nn.sigmoid(x)
 
 
-def recur_body(*refs):
-    parts = refs[:8]
-    alog_ref, bias_ref, sv_ref, ss_ref, gain_ref, gated_ref, keys_ref, delta_ref, sd_ref = refs[8:]
+def recur_body(
+    p_ref, alog_ref, bias_ref, sv_ref, ss_ref, gain_ref, gated_ref, keys_ref, delta_ref, sd_ref
+):
     rows = 16
-    t = parts[0][...].astype(F32)
+    t = p_ref[0].astype(F32)
     for i in range(1, 8):
-        t = t + parts[i][...].astype(F32)
+        t = t + p_ref[i].astype(F32)
     tail = t[:, 640:]
     lane = lax.broadcasted_iota(jnp.int32, (rows, 128), 1)
 
@@ -161,7 +158,9 @@
         * gain_ref[...]
         * silu(zgate)
     )
-    gated_ref[...] = gated.astype(BF16)
+    gated = gated.astype(BF16)
+    for i in range(8):
+        gated_ref[i] = gated
     keys_ref[...] = keys
     delta_ref[...] = delta
     sd_ref[...] = sd
@@ -181,13 +180,13 @@
     ns_ref[...] = peaks.T
 
 
-def route_body(pair_ref, routes_in, scale_in, mt_ref, w_ref):
+def route_body(routes_in, scale_in, mt_ref, w_ref):
     routes_ref, scale_ref = routes_in.get(), scale_in.get()
-    n = 1024
+    n = 2048
     lane = lax.broadcasted_iota(jnp.int32, (8, n), 1)
-    expert = lane // 16 * 4 + pair_ref[0]
-    slot_of = lane // 8 % 2
-    chunk = lane % 8
+    expert = lane // 8
+    slot_of = lane // 2 % 2
+    half = lane % 2
     sends = jnp.zeros((8, n), F32)
     weight = jnp.zeros((8, n), F32)
     for k in range(TOPK):
@@ -201,78 +200,65 @@
     keep = (sends > 0.0) & (slot == slot_of.astype(F32))
     sel = jnp.where(keep, 1.0, 0.0)
     wsel = jnp.where(keep, weight, 0.0)
-    selects = []
-    weights = []
-    for c in range(8):
-        selects.append(jnp.where(chunk == c, sel, 0.0))
-        weights.append(jnp.where(chunk == c, wsel, 0.0))
+    first = half == 0
+    selects = [jnp.where(first, sel, 0.0), jnp.where(first, 0.0, sel)]
+    weights = [jnp.where(first, wsel, 0.0), jnp.where(first, 0.0, wsel)]
     mt_ref[...] = jnp.concatenate(selects, axis=0).T.astype(BF16)
     w_ref[...] = jnp.concatenate(weights, axis=0).astype(BF16)
 
 
-def outproj_body(sub_ref, *refs):
-    parts, w_ref, out_ref, scr = refs[:8], refs[8], refs[9], refs[10]
-    for k in range(8):
-        source = lax.rem(sub_ref[0] + 8 - k, 8)
-        scr[pl.ds(pl.multiple_of(source * 16, 16), 16), :] = parts[k][...]
-    out_ref[...] = jnp.dot(scr[...], w_ref[...], preferred_element_type=F32).astype(BF16)
-
-
-def hidden_body(attn_ref, resid_ref, out_ref):
+def outproj_body(x_ref, w_ref, out_ref):
+    out_ref[...] = jnp.dot(x_ref[...], w_ref[...], preferred_element_type=F32).astype(BF16)
+
+
+def dispatch_body(attn_ref, resid_ref, mt_ref, hidden_ref, out_ref):
     attn = jnp.sum(attn_ref[...].astype(F32), axis=0)
-    out_ref[...] = (resid_ref[...] + attn).astype(BF16)
-
-
-def dispatch_body(sub_ref, *refs):
-    parts, gain_ref, mt_ref, out_ref, scr = refs[:8], refs[8], refs[9], refs[10], refs[11]
-    for k in range(8):
-        source = lax.rem(sub_ref[0] + 8 - k, 8)
-        scr[pl.ds(pl.multiple_of(source * 8, 8), 8), :] = parts[k][...].astype(F32)
-    h3 = scr[...].reshape(8, 8, 256)
-    sq = jnp.sum(jnp.sum(h3 * h3, axis=0), axis=1, keepdims=True)
-    rs = lax.rsqrt(sq / D + 1e-05)
-    normed = (h3 * rs[None] * gain_ref[...]).reshape(64, 256).astype(BF16)
-    out_ref[...] = jnp.dot(mt_ref[...], normed, preferred_element_type=F32).astype(BF16)
-
-
-def expert_body(x_ref, wgu_ref, wd_ref, out_ref, scr):
-    for half in range(2):
-        scr[half * 1024 : (half + 1) * 1024, :] = x_ref[:, half * 128 : (half + 1) * 128].astype(
-            F32
-        )
+    hidden = (resid_ref[...] + attn).astype(BF16)
+    hidden_ref[...] = hidden
+    hf = hidden.astype(F32)
+    halves = jnp.concatenate([hf[:, :128], hf[:, 128:]], axis=0).astype(BF16)
+    sent = jnp.dot(mt_ref[...], halves, preferred_element_type=F32)
+    out_ref[...] = sent.reshape(512, 4, 128).astype(BF16)
+
+
+def expert_body(x_ref, gain_ref, wgu_ref, wd_ref, out_ref, scr):
+    scr[...] = x_ref[...].astype(F32).reshape(2048, 128)
+
+    def rows_of(c, slot, half):
+        return pl.ds(c * 4 + slot * 2 + half, 64, stride=32)
+
+    chunks = []
+    sq = jnp.zeros((128, 128), F32)
+    for c in range(8):
+        halves = [
+            jnp.concatenate([scr[rows_of(c, slot, half), :] for slot in range(2)], axis=0)
+            for half in range(2)
+        ]
+        sq = sq + halves[0] * halves[0] + halves[1] * halves[1]
+        chunks.append(jnp.concatenate(halves, axis=1))
+    rs = lax.rsqrt(jnp.sum(sq, axis=1, keepdims=True) / D + 1e-05)
     acc = jnp.zeros((128, 512), F32)
     for c in range(8):
-        xc = jnp.concatenate(
-            [scr[pl.ds(half * 1024 + c, 128, stride=8), :] for half in range(2)], axis=1
-        ).astype(BF16)
+        xc = (chunks[c] * rs * gain_ref[c]).astype(BF16)
         acc = acc + jnp.dot(
             xc, wgu_ref[0, c * 256 : (c + 1) * 256, :], preferred_element_type=F32
         )
     act = (silu(acc[:, :256]) * acc[:, 256:]).astype(BF16)
     for c in range(8):
         o = jnp.dot(act, wd_ref[0, :, c * 256 : (c + 1) * 256], preferred_element_type=F32)
-        for half in range(2):
-            scr[pl.ds(half * 1024 + c, 128, stride=8), :] = o[:, half * 128 : (half + 1) * 128]
-    for half in range(2):
-        out_ref[:, half * 128 : (half + 1) * 128] = scr[
-            half * 1024 : (half + 1) * 1024, :
-        ].astype(BF16)
-
-
-def combine_body(sub_ref, w_ref, x_ref, *rest):
-    outs, scr = rest[:8], rest[8]
-    scr[...] = jnp.dot(w_ref[...], x_ref[...], preferred_element_type=F32)
-    for k in range(8):
-        to = lax.rem(sub_ref[0] + k, 8)
-        outs[k][...] = scr[pl.ds(pl.multiple_of(to * 8, 8), 8), :].astype(BF16)
-
-
-def final_body(h_ref, *refs):
-    parts, out_ref = refs[:8], refs[8]
-    moe = parts[0][...].astype(F32)
-    for k in range(1, 8):
-        moe = moe + parts[k][...].astype(F32)
-    out_ref[...] = (h_ref[...].astype(F32) + moe).astype(BF16)
+        for slot in range(2):
+            for half in range(2):
+                scr[rows_of(c, slot, half), :] = o[
+                    slot * 64 : (slot + 1) * 64, half * 128 : (half + 1) * 128
+                ]
+    out_ref[...] = scr[...].reshape(512, 4, 128).astype(BF16)
+
+
+def combine_body(w_ref, x_ref, hidden_ref, out_ref):
+    x = x_ref[...].astype(F32).reshape(2048, 128).astype(BF16)
+    moe = jnp.dot(w_ref[...], x, preferred_element_type=F32)
+    moe = jnp.concatenate([moe[:8], moe[8:]], axis=1)
+    out_ref[...] = (hidden_ref[...].astype(F32) + moe).astype(BF16)
 
 
 def shape(dims, dtype=BF16):
@@ -281,13 +267,6 @@
 
 def a2a(x, axes):
     return lax.all_to_all(x, axes, split_axis=0, concat_axis=0, tiled=True)
-
-
-def exchange(pieces):
-    n = len(pieces)
-    return [pieces[0]] + [
-        lax.ppermute(pieces[k], "sub", [(i, (i + k) % n) for i in range(n)]) for k in range(1, n)
-    ]
 
 
 def local(
@@ -307,14 +286,13 @@
     w_gate_up,
     w_down,
 ):
-    sub = lax.axis_index("sub").astype(jnp.int32).reshape(1)
     head = lax.axis_index("head").astype(jnp.int32).reshape(1)
     sv = state_values.reshape(16, 128, 128)
     ss = state_scales.reshape(16, 128)
-    part = call(
+    part, resid, sv, ss, ngain, w_out, pgain = call(
         project_body,
-        (shape((16, 768)),) * 8
-        + (
+        (
+            shape((128, 768)),
             shape((8, 256), F32),
             shape((16, 128, 128)),
             shape((16, 128), F32),
@@ -322,9 +300,8 @@
             shape((128, 256)),
             shape((8, 1, 256), F32),
         ),
-        [SM, SM, HB, HB, HB, HB] + [KEEP] * 5,
+        [SM, HB, HB, HB, HB] + [KEEP] * 5,
         (
-            sub,
             head,
             inputs,
             in_gain.reshape(1, 256),
@@ -336,64 +313,47 @@
             w_out,
             post_gain.reshape(8, 1, 256),
         ),
-        [pltpu.VMEM((128, 768), BF16), pltpu.SemaphoreType.DMA((5,))],
-    )
-    part, (resid, sv, ss, ngain, w_out, pgain) = part[:8], part[8:]
-    part = exchange(part)
+        [pltpu.SemaphoreType.DMA((5,))],
+    )
+    part = a2a(part.reshape(8, 16, 768), "sub")
     mt, wsel = call(
         route_body,
-        (shape((1024, 64)), shape((64, 1024))),
-        [SM, HB, HB],
-        (sub // 2, routes, route_scale),
+        (shape((2048, 16)), shape((16, 2048))),
+        [HB, HB],
+        (routes, route_scale),
     )
     gated, keys, delta, sd = call(
         recur_body,
-        (shape((16, 128)), shape((16, 128), F32), shape((16, 128), F32), shape((16, 128), F32)),
-        [VM] * 8 + [SM, SM, VM, VM, VM],
-        (*part, a_log, dt_bias, sv, ss, ngain),
-    )
-    gathered = exchange([gated] * 8)
+        (shape((8, 16, 128)), shape((16, 128), F32), shape((16, 128), F32), shape((16, 128), F32)),
+        [VM, SM, SM, VM, VM, VM],
+        (part, a_log, dt_bias, sv, ss, ngain),
+    )
+    gathered = a2a(gated, "sub").reshape(128, 128)
     new_values, new_scales = call(
         state_body,
         (shape((16, 128, 128)), shape((16, 128), F32)),
         [VM] * 4,
         (sv, sd, keys, delta),
     )
-    attn = call(
-        outproj_body,
-        shape((128, 256)),
-        [SM] + [VM] * 9,
-        (sub, *gathered, w_out),
-        [pltpu.VMEM((128, 128), BF16)],
-    )
+    attn = call(outproj_body, shape((128, 256)), [VM] * 2, (gathered, w_out))
     attn = a2a(attn.reshape(16, 8, 256), "head")
-    hidden = call(hidden_body, shape((8, 256)), [VM, VM], (attn, resid))
-    whole = exchange([hidden] * 8)
-    buffer = call(
+    hidden, sent = call(
         dispatch_body,
-        shape((1024, 256)),
-        [SM] + [VM] * 10,
-        (sub, *whole, pgain, mt),
-        [pltpu.VMEM((64, 256), F32)],
-    )
-    received = a2a(buffer.reshape(64, 16, 256), ("grp", "head")).reshape(1024, 256)
+        (shape((8, 256)), shape((512, 4, 128))),
+        [VM] * 3,
+        (attn, resid, mt),
+    )
+    every = ("grp", "head", "sub")
+    received = a2a(sent, every)
     result = call(
         expert_body,
-        shape((1024, 256)),
-        [VM] * 3,
-        (received, w_gate_up, w_down),
+        shape((512, 4, 128)),
+        [VM] * 4,
+        (received, pgain, w_gate_up, w_down),
         [pltpu.VMEM((2048, 128), F32)],
     )
-    back = a2a(result.reshape(64, 16, 256), ("grp", "head")).reshape(1024, 256)
-    moe = call(
-        combine_body,
-        (shape((8, 256)),) * 8,
-        [SM, VM, VM],
-        (sub, wsel, back),
-        [pltpu.VMEM((64, 256), F32)],
-    )
-    moe = exchange(moe)
-    out = call(final_body, shape((8, 256)), [VM] * 9, (hidden, *moe))
+    back = a2a(result, every)
+    out = call(combine_body, shape((8, 256)), [VM] * 3, (wsel, back, hidden))
     return (out, new_values.reshape(16, 1, 128, 128), new_scales.reshape(16, 1, 128))
 
 

time: 194 us -> 119 us (0.61)
  starting transfers between devices: 104 us -> 30.8 us
  blocking collectives: 72.6 us -> 40 us
  waiting for transfers between devices: 4.49 us -> 33.3 us
  Pallas kernels: 8.83 us -> 12.1 us
    ppermute x28 -> x0, starting transfers between devices: 104 us -> none  [exchange(): lax.ppermute(pieces[k], 'sub', [(i, (i + k) % n) for i in range(n)])]
    all_to_all x0 -> x3, waiting for transfers between devices: none -> 33.3 us  [a2a(): return lax.all_to_all(x, axes, split_axis=0, concat_axis=0, tiled=True)]
    all_to_all x3 -> x2, blocking collectives: 72.6 us -> 40 us  [a2a(): return lax.all_to_all(x, axes, split_axis=0, concat_axis=0, tiled=True)]
    all_to_all x0 -> x3, starting transfers between devices: none -> 30.8 us  [a2a(): return lax.all_to_all(x, axes, split_axis=0, concat_axis=0, tiled=True)]
    ppermute x28 -> x0, waiting for transfers between devices: 4.49 us -> none  [exchange(): lax.ppermute(pieces[k], 'sub', [(i, (i + k) % n) for i in range(n)])]
    pallas_call x10 -> x8, Pallas kernels: 8.83 us -> 12.1 us  [call(): pl.pallas_call(kernel, out_shape=outs, in_specs=ins, out_specs=jax.tree.m...]
  transfers between devices with their start and end apart: 28 -> 3, of which waited for: 4 -> 3; matrix products, arithmetic and copies ran while one was open for 0% -> 0% of each run, Pallas kernels for 2% -> 3%
where the time goes in v3:
time: 119 us; the launch traced here: 118 us
  blocking collectives  40 us (34%)
  waiting for transfers between devices  33.3 us (28%)
  starting transfers between devices  30.8 us (26%)
  Pallas kernels  12.1 us (10%)
  between operations  1.98 us (2%)
    all_to_all x2, blocking collectives, a2a(): return lax.all_to_all(x, axes, split_axis=0, concat_axis=0, tiled=True)  40 us
    all_to_all x3, waiting for transfers between devices, a2a(): return lax.all_to_all(x, axes, split_axis=0, concat_axis=0, tiled=True)  33.3 us
    all_to_all x3, starting transfers between devices, a2a(): return lax.all_to_all(x, axes, split_axis=0, concat_axis=0, tiled=True)  30.8 us
    pallas_call x8, Pallas kernels, call(): pl.pallas_call(kernel, out_shape=outs, in_specs=ins, out_specs=jax.tree.m...  12.1 us
  transfers between devices with their start and end apart: 3, of which 3 were waited for; matrix products, arithmetic and copies ran while one was open for 0% of the time, Pallas kernels for 3%

profile of v3, /device:TPU:1, one launch (start us, length us, event | category | flops | bytes accessed | tf_op | source)
XLA Modules:
  0.0 118.2 jit_solution(13526472675200238777)
XLA Ops:
  0.6 0.0 copy-start
  0.6 2.3 %shard_map.167 = (bf16[128,768]{1,0:T(8,128)(2,1)}, f32[8,256]{1,0:T(8,128)S(1)}, bf16[16,128,128]{2,1,0:T(8,128)(2,1)S(1)}, f32[16,128]{1,0:T(8,128)S(1)}, f32[...) custom-call(s32[1]{0:T(128)} %bitcast.refs_0_, bf16[128,256]{1,0:T(8,128)(2,1)} %refs_1_.4, ...), custom_call_target="tpu_custom_call" | custom-call | tf_op jit(solution)/shard_map/pallas_call | solution.py:53
  2.9 7.7 %all-to-all-start = ((bf16[8,16,768]{2,1,0:T(8,128)(2,1)}), bf16[8,16,768]{2,1,0:T(8,128)(2,1)S(1)}, u32[]{:S(2)}, u32[]{:S(2)}) async-start(bf16[8,16,768]{2,1,0:T(8,128)(2,1)} %bitcast.7), calls=%async_computation | async-start | bytes 393216 | tf_op jit(solution)/shard_map/all_to_all | solution.py:269
  11.9 7.4 %all-to-all-done.refs_0_ = bf16[8,16,768]{2,1,0:T(8,128)(2,1)S(1)} async-done(((bf16[8,16,768]{2,1,0:T(8,128)(2,1)}), bf16[8,16,768]{2,1,0:T(8,128)(2,1)S(1)}, u32[]{:S(2)}, u32[]{:S(2)}) %all-to-all-start) | async-done | bytes 196640 | tf_op jit(solution)/shard_map/all_to_all | solution.py:269
  19.3 1.1 shard_map.168
  20.4 9.2 %all_to_all.25 = bf16[8,16,128]{2,1,0:T(8,128)(2,1)S(1)} all-to-all(bf16[8,16,128]{2,1,0:T(8,128)(2,1)S(1)} %get-tuple-element.25), channel_id=1, replica_groups=mesh['grp'=4,'head'=16,'sub'=8] {'sub'}, dimensions={0} | all-to-all | bytes 65536 | tf_op jit(solution)/shard_map/all_to_all | solution.py:269
  29.6 0.8 shard_map.169
  30.4 14.2 %all-to-all-start.2 = ((bf16[16,8,256]{2,1,0:T(8,128)(2,1)}), bf16[16,8,256]{2,1,0:T(8,128)(2,1)S(1)}, u32[]{:S(2)}, u32[]{:S(2)}) async-start(bf16[16,8,256]{2,1,0:T(8,128)(2,1)} %bitcast.9), calls=%async_computation.2 | async-start | bytes 131072 | tf_op jit(solution)/shard_map/all_to_all | solution.py:269
  44.6 1.1 shard_map.166
  45.6 6.7 %all-to-all-done.2.refs_0_ = bf16[16,8,256]{2,1,0:T(8,128)(2,1)S(1)} async-done(((bf16[16,8,256]{2,1,0:T(8,128)(2,1)}), bf16[16,8,256]{2,1,0:T(8,128)(2,1)S(1)}, u32[]{:S(2)}, u32[]{:S(2)}) %all-to-all-start.2) | async-done | bytes 65568 | tf_op jit(solution)/shard_map/all_to_all | solution.py:269
  52.4 0.0 copy-start.1
  52.4 0.3 shard_map.170
  52.7 30.7 %all_to_all.26.refs_0_ = bf16[512,4,128]{2,1,0:T(4,128)(2,1)S(1)} all-to-all(bf16[512,4,128]{2,1,0:T(4,128)(2,1)S(1)} %get-tuple-element.29), channel_id=1, replica_groups=mesh['grp'=4,'head'=16,'sub'=8] {'grp','head','sub'}, dimensions={0} | all-to-all | bytes 1048576 | tf_op jit(solution)/shard_map/all_to_all | solution.py:269
  83.4 0.0 copy-done
  83.4 0.0 copy-done.1
  83.4 2.9 %shard_map.171 = bf16[512,4,128]{2,1,0:T(4,128)(2,1)} custom-call(bf16[512,4,128]{2,1,0:T(4,128)(2,1)S(1)} %all_to_all.26.refs_0_, f32[8,1,256]{2,1,0:T(1,128)S(1)} %get-tuple-element.30.refs_1_, bf16[1,2048,512]{2,1,0:T(8,128)(2,1)S(1)} %copy-done, bf16[1,256,2048]{2,1,0:T(8,128)(2,1)S(1)} %copy-done.1), custom_call_target="tpu_custom_call" | custom-call | tf_op jit(solution)/shard_map/pallas_call | solution.py:53
  86.4 9.0 %all-to-all-start.4 = ((bf16[512,4,128]{2,1,0:T(4,128)(2,1)}), bf16[512,4,128]{2,1,0:T(4,128)(2,1)S(1)}, u32[]{:S(2)}, u32[]{:S(2)}) async-start(bf16[512,4,128]{2,1,0:T(4,128)(2,1)} %shard_map.171), calls=%async_computation.4 | async-start | bytes 1048576 | tf_op jit(solution)/shard_map/all_to_all | solution.py:269
  95.3 2.9 %shard_map.173 = (bf16[16,128,128]{2,1,0:T(8,128)(2,1)}, f32[16,128]{1,0:T(8,128)}) custom-call(bf16[16,128,128]{2,1,0:T(8,128)(2,1)S(1)} %get-tuple-element.22.refs_3_.refs_0_, f32[16,128]{1,0:T(8,128)S(1)} %get-tuple-element.32.refs_1_, f32[16,128]{1,0:T(8,128)S(1)} %get-tuple-element.33.refs_2_, f32[16,128]{1,0:T(8,128)S(1)} %get-tuple-element.34.refs_3_), custom_call_target="tpu_custom_call" | custom-call | tf_op jit(solution)/shard_map/pallas_call | solution.py:53
  98.3 19.1 %all-to-all-done.4.refs_1_ = bf16[512,4,128]{2,1,0:T(4,128)(2,1)S(1)} async-done(((bf16[512,4,128]{2,1,0:T(4,128)(2,1)}), bf16[512,4,128]{2,1,0:T(4,128)(2,1)S(1)}, u32[]{:S(2)}, u32[]{:S(2)}) %all-to-all-start.4) | async-done | bytes 524320 | tf_op jit(solution)/shard_map/all_to_all | solution.py:269
  117.4 0.8 shard_map.172
Async XLA Ops:
  0.6 82.8 %copy-start = (bf16[1,2048,512]{2,1,0:T(8,128)(2,1)S(1)}, bf16[1,2048,512]{2,1,0:T(8,128)(2,1)}, u32[]{:S(2)}) copy-start(bf16[1,2048,512]{2,1,0:T(8,128)(2,1)} %refs_2_.2) | copy-start | bytes 6291460
  2.9 16.4 %all-to-all-start = ((bf16[8,16,768]{2,1,0:T(8,128)(2,1)}), bf16[8,16,768]{2,1,0:T(8,128)(2,1)S(1)}, u32[]{:S(2)}, u32[]{:S(2)}) async-start(bf16[8,16,768]{2,1,0:T(8,128)(2,1)} %bitcast.7), calls=%async_computation | async-start | bytes 393216 | tf_op jit(solution)/shard_map/all_to_all | solution.py:269
  30.4 22.0 %all-to-all-start.2 = ((bf16[16,8,256]{2,1,0:T(8,128)(2,1)}), bf16[16,8,256]{2,1,0:T(8,128)(2,1)S(1)}, u32[]{:S(2)}, u32[]{:S(2)}) async-start(bf16[16,8,256]{2,1,0:T(8,128)(2,1)} %bitcast.9), calls=%async_computation.2 | async-start | bytes 131072 | tf_op jit(solution)/shard_map/all_to_all | solution.py:269
  52.4 31.0 %copy-start.1 = (bf16[1,256,2048]{2,1,0:T(8,128)(2,1)S(1)}, bf16[1,256,2048]{2,1,0:T(8,128)(2,1)}, u32[]{:S(2)}) copy-start(bf16[1,256,2048]{2,1,0:T(8,128)(2,1)} %refs_3_.3) | copy-start | bytes 3145732
  86.4 31.0 %all-to-all-start.4 = ((bf16[512,4,128]{2,1,0:T(4,128)(2,1)}), bf16[512,4,128]{2,1,0:T(4,128)(2,1)S(1)}, u32[]{:S(2)}, u32[]{:S(2)}) async-start(bf16[512,4,128]{2,1,0:T(4,128)(2,1)} %shard_map.171), calls=%async_computation.4 | async-start | bytes 1048576 | tf_op jit(solution)/shard_map/all_to_all | solution.py:269

commit v4 on v3

--- a/solution.py
+++ b/solution.py
@@ -10,6 +10,7 @@
 TOPK = 10
 F32 = jnp.float32
 BF16 = jnp.bfloat16
+SUB = ("quad", "side")
 
 VM = pl.BlockSpec(memory_space=pltpu.VMEM)
 SM = pl.BlockSpec(memory_space=pltpu.SMEM)
@@ -65,11 +66,7 @@
     return hi, x - hi
 
 
-def project_body(head_ref, x_in, gain_in, w_in, wab_in, *rest):
-    held, out_ref, resid_ref, kept, sems = rest[:5], rest[5], rest[6], rest[7:12], rest[12]
-    copies = [pltpu.make_async_copy(held[i], kept[i], sems.at[i]) for i in range(5)]
-    for copy in copies:
-        copy.start()
+def project_body(head_ref, x_in, gain_in, w_in, wab_in, out_ref, resid_ref):
     x_ref = x_in.get()
     xf = x_ref[...].astype(F32)
     xg = (xf * gain_in.get()[...]).astype(BF16)
@@ -97,16 +94,13 @@
     out_ref[:, 128:256] = key_hi.astype(BF16)
     out_ref[:, 256:512] = proj[:, 256:].astype(BF16)
     out_ref[:, 512:640] = key_lo.astype(BF16)
-    for copy in copies:
-        copy.wait()
-
 
 def silu(x):
     return x * jax.nn.sigmoid(x)
 
 
 def recur_body(
-    p_ref, alog_ref, bias_ref, sv_ref, ss_ref, gain_ref, gated_ref, keys_ref, delta_ref, sd_ref
+    sub_ref, p_ref, alog_ref, bias_ref, sv_ref, ss_ref, gain_ref, gated_ref, keys_ref, delta_ref, sd_ref
 ):
     rows = 16
     t = p_ref[0].astype(F32)
@@ -158,9 +152,11 @@
         * gain_ref[...]
         * silu(zgate)
     )
-    gated = gated.astype(BF16)
-    for i in range(8):
-        gated_ref[i] = gated
+    block = sub_ref[0] * 16
+    for b in range(2):
+        piece = gated[b * 8 : (b + 1) * 8].astype(BF16)
+        for i in range(8):
+            gated_ref[block + b * 8 + i] = piece
     keys_ref[...] = keys
     delta_ref[...] = delta
     sd_ref[...] = sd
@@ -180,13 +176,17 @@
     ns_ref[...] = peaks.T
 
 
-def route_body(routes_in, scale_in, mt_ref, w_ref):
+def prepare_body(routes_in, scale_in, *rest):
+    held, mt_ref, w_ref, kept, sems = rest[:4], rest[4], rest[5], rest[6:10], rest[10]
+    copies = [pltpu.make_async_copy(held[i], kept[i], sems.at[i]) for i in range(4)]
+    for copy in copies:
+        copy.start()
     routes_ref, scale_ref = routes_in.get(), scale_in.get()
     n = 2048
     lane = lax.broadcasted_iota(jnp.int32, (8, n), 1)
     expert = lane // 8
-    slot_of = lane // 2 % 2
-    half = lane % 2
+    slot_of = lane // 4 % 2
+    quarter = lane % 4
     sends = jnp.zeros((8, n), F32)
     weight = jnp.zeros((8, n), F32)
     for k in range(TOPK):
@@ -200,32 +200,38 @@
     keep = (sends > 0.0) & (slot == slot_of.astype(F32))
     sel = jnp.where(keep, 1.0, 0.0)
     wsel = jnp.where(keep, weight, 0.0)
-    first = half == 0
-    selects = [jnp.where(first, sel, 0.0), jnp.where(first, 0.0, sel)]
-    weights = [jnp.where(first, wsel, 0.0), jnp.where(first, 0.0, wsel)]
+    selects = [jnp.where(quarter == i, sel, 0.0) for i in range(4)]
+    weights = [jnp.where(quarter == i, wsel, 0.0) for i in range(4)]
     mt_ref[...] = jnp.concatenate(selects, axis=0).T.astype(BF16)
     w_ref[...] = jnp.concatenate(weights, axis=0).astype(BF16)
-
-
-def outproj_body(x_ref, w_ref, out_ref):
-    out_ref[...] = jnp.dot(x_ref[...], w_ref[...], preferred_element_type=F32).astype(BF16)
-
-
-def dispatch_body(attn_ref, resid_ref, mt_ref, hidden_ref, out_ref):
-    attn = jnp.sum(attn_ref[...].astype(F32), axis=0)
-    hidden = (resid_ref[...] + attn).astype(BF16)
-    hidden_ref[...] = hidden
-    hf = hidden.astype(F32)
-    halves = jnp.concatenate([hf[:, :128], hf[:, 128:]], axis=0).astype(BF16)
-    sent = jnp.dot(mt_ref[...], halves, preferred_element_type=F32)
-    out_ref[...] = sent.reshape(512, 4, 128).astype(BF16)
+    for copy in copies:
+        copy.wait()
+
+
+def hidden_body(head_ref, x_ref, resid_ref, w_in, hidden_ref):
+    block = lax.div(head_ref[0], 2)
+    gated = jnp.concatenate([x_ref[h * 8 + block].astype(F32) for h in range(16)], axis=1)
+    attn = jnp.dot(gated.astype(BF16), w_in.get()[...], preferred_element_type=F32)
+    hidden_ref[...] = (resid_ref[...] + attn).astype(BF16)
+
+
+def dispatch_body(side_ref, mine_ref, other_ref, mt_ref, out_ref):
+    first = side_ref[0] == 0
+    mine = mine_ref[...].astype(F32)
+    other = other_ref[...].astype(F32)
+    lo = jnp.where(first, mine, other)
+    hi = jnp.where(first, other, mine)
+    quarters = jnp.concatenate(
+        [lo[:, :128], lo[:, 128:], hi[:, :128], hi[:, 128:]], axis=0
+    ).astype(BF16)
+    out_ref[...] = jnp.dot(mt_ref[...], quarters, preferred_element_type=F32).astype(BF16)
 
 
 def expert_body(x_ref, gain_ref, wgu_ref, wd_ref, out_ref, scr):
-    scr[...] = x_ref[...].astype(F32).reshape(2048, 128)
+    scr[...] = x_ref[...].astype(F32)
 
     def rows_of(c, slot, half):
-        return pl.ds(c * 4 + slot * 2 + half, 64, stride=32)
+        return pl.ds(c // 2 * 8 + slot * 4 + c % 2 * 2 + half, 64, stride=32)
 
     chunks = []
     sq = jnp.zeros((128, 128), F32)
@@ -251,14 +257,20 @@
                 scr[rows_of(c, slot, half), :] = o[
                     slot * 64 : (slot + 1) * 64, half * 128 : (half + 1) * 128
                 ]
-    out_ref[...] = scr[...].reshape(512, 4, 128).astype(BF16)
-
-
-def combine_body(w_ref, x_ref, hidden_ref, out_ref):
-    x = x_ref[...].astype(F32).reshape(2048, 128).astype(BF16)
-    moe = jnp.dot(w_ref[...], x, preferred_element_type=F32)
-    moe = jnp.concatenate([moe[:8], moe[8:]], axis=1)
-    out_ref[...] = (hidden_ref[...].astype(F32) + moe).astype(BF16)
+    out_ref[...] = scr[...].astype(BF16)
+
+
+def combine_body(side_ref, w_ref, x_ref, hidden_ref, mine_ref, other_ref):
+    first = side_ref[0] == 0
+    moe = jnp.dot(w_ref[...], x_ref[...], preferred_element_type=F32)
+    lo = jnp.concatenate([moe[:8], moe[8:16]], axis=1)
+    hi = jnp.concatenate([moe[16:24], moe[24:]], axis=1)
+    mine_ref[...] = hidden_ref[...].astype(F32) + jnp.where(first, lo, hi)
+    other_ref[...] = jnp.where(first, hi, lo)
+
+
+def final_body(mine_ref, other_ref, out_ref):
+    out_ref[...] = (mine_ref[...] + other_ref[...]).astype(BF16)
 
 
 def shape(dims, dtype=BF16):
@@ -287,102 +299,107 @@
     w_down,
 ):
     head = lax.axis_index("head").astype(jnp.int32).reshape(1)
-    sv = state_values.reshape(16, 128, 128)
-    ss = state_scales.reshape(16, 128)
-    part, resid, sv, ss, ngain, w_out, pgain = call(
+    side = lax.axis_index("side").astype(jnp.int32).reshape(1)
+    sub = lax.axis_index("quad").astype(jnp.int32).reshape(1) * 2 + side
+    w_cols = lax.all_gather(w_out, "head", axis=0, tiled=True)
+    part, resid = call(
         project_body,
+        (shape((128, 768)), shape((8, 256), F32)),
+        [SM, HB, HB, HB, HB],
+        (head, inputs, in_gain.reshape(1, 256), w_qkvz, w_ab.T),
+    )
+    part = a2a(part.reshape(8, 16, 768), SUB)
+    mt, wsel, sv, ss, ngain, pgain = call(
+        prepare_body,
         (
-            shape((128, 768)),
-            shape((8, 256), F32),
+            shape((2048, 32)),
+            shape((32, 2048)),
             shape((16, 128, 128)),
             shape((16, 128), F32),
             shape((1, 128), F32),
-            shape((128, 256)),
             shape((8, 1, 256), F32),
         ),
-        [SM, HB, HB, HB, HB] + [KEEP] * 5,
+        [HB, HB] + [KEEP] * 4,
         (
-            head,
-            inputs,
-            in_gain.reshape(1, 256),
-            w_qkvz,
-            w_ab.T,
-            sv,
-            ss,
+            routes,
+            route_scale,
+            state_values.reshape(16, 128, 128),
+            state_scales.reshape(16, 128),
             norm_gain.reshape(1, 128),
-            w_out,
             post_gain.reshape(8, 1, 256),
         ),
-        [pltpu.SemaphoreType.DMA((5,))],
-    )
-    part = a2a(part.reshape(8, 16, 768), "sub")
-    mt, wsel = call(
-        route_body,
-        (shape((2048, 16)), shape((16, 2048))),
-        [HB, HB],
-        (routes, route_scale),
+        [pltpu.SemaphoreType.DMA((4,))],
     )
     gated, keys, delta, sd = call(
         recur_body,
-        (shape((8, 16, 128)), shape((16, 128), F32), shape((16, 128), F32), shape((16, 128), F32)),
-        [VM, SM, SM, VM, VM, VM],
-        (part, a_log, dt_bias, sv, ss, ngain),
-    )
-    gathered = a2a(gated, "sub").reshape(128, 128)
+        (shape((128, 8, 128)), shape((16, 128), F32), shape((16, 128), F32), shape((16, 128), F32)),
+        [SM, VM, SM, SM, VM, VM, VM],
+        (sub, part, a_log, dt_bias, sv, ss, ngain),
+    )
+    gathered = a2a(gated, ("head",) + SUB)
     new_values, new_scales = call(
         state_body,
         (shape((16, 128, 128)), shape((16, 128), F32)),
         [VM] * 4,
         (sv, sd, keys, delta),
     )
-    attn = call(outproj_body, shape((128, 256)), [VM] * 2, (gathered, w_out))
-    attn = a2a(attn.reshape(16, 8, 256), "head")
-    hidden, sent = call(
-        dispatch_body,
-        (shape((8, 256)), shape((512, 4, 128))),
-        [VM] * 3,
-        (attn, resid, mt),
-    )
-    every = ("grp", "head", "sub")
-    received = a2a(sent, every)
+    hidden = call(
+        hidden_body, shape((8, 256)), [SM, VM, VM, HB], (head, gathered, resid, w_cols)
+    )
+    swap = [(0, 1), (1, 0)]
+    neighbour = lax.ppermute(hidden, "side", swap)
+    sent = call(
+        dispatch_body, shape((2048, 128)), [SM, VM, VM, VM], (side, hidden, neighbour, mt)
+    )
+    halves = ("grp", "head", "quad")
+    received = a2a(sent.reshape(256, 8, 128), halves).reshape(2048, 128)
     result = call(
         expert_body,
-        shape((512, 4, 128)),
+        shape((2048, 128)),
         [VM] * 4,
         (received, pgain, w_gate_up, w_down),
         [pltpu.VMEM((2048, 128), F32)],
     )
-    back = a2a(result, every)
-    out = call(combine_body, shape((8, 256)), [VM] * 3, (wsel, back, hidden))
+    back = a2a(result.reshape(256, 8, 128), halves).reshape(2048, 128)
+    mine, other = call(
+        combine_body,
+        (shape((8, 256), F32), shape((8, 256), F32)),
+        [SM] + [VM] * 3,
+        (side, wsel, back, hidden),
+    )
+    other = lax.ppermute(other, "side", swap)
+    out = call(final_body, shape((8, 256)), [VM, VM], (mine, other))
     return (out, new_values.reshape(16, 1, 128, 128), new_scales.reshape(16, 1, 128))
 
 
 def solution(mesh):
+    shape4 = (mesh.shape["grp"], mesh.shape["head"], mesh.shape["sub"] // 2, 2)
+    mesh = jax.sharding.Mesh(mesh.devices.reshape(shape4), ("grp", "head") + SUB)
     placed = (
-        P("grp", "sub"),
-        P("sub"),
-        P("sub", "head"),
-        P("sub", "head"),
+        P("grp", SUB),
+        P(SUB),
+        P(SUB, "head"),
+        P(SUB, "head"),
         P("head"),
         P("head"),
-        P(("grp", "sub"), "head", None, None),
-        P(("grp", "sub"), "head", None),
+        P(("grp",) + SUB, "head", None, None),
+        P(("grp",) + SUB, "head", None),
         P(),
-        P("head", "sub"),
+        P("head", SUB),
         P(),
         P(("grp", "head"), None),
         P(("grp", "head"), None),
-        P(("grp", "head", "sub"), None, None),
-        P(("grp", "head", "sub"), None, None),
+        P(("grp", "head") + SUB, None, None),
+        P(("grp", "head") + SUB, None, None),
     )
     return jax.shard_map(
         local,
         mesh=mesh,
         in_specs=placed,
         out_specs=(
-            P(("grp", "head"), "sub"),
-            P(("grp", "sub"), "head", None, None),
-            P(("grp", "sub"), "head", None),
+            P(("grp", "head"), SUB),
+            P(("grp",) + SUB, "head", None, None),
+            P(("grp",) + SUB, "head", None),
         ),
         check_vma=False,
     )

time: 119 us -> 153 us (1.29)
  blocking collectives: 40 us -> 102 us
  waiting for transfers between devices: 33.3 us -> 8.49 us
  starting transfers between devices: 30.8 us -> 12.7 us
  between operations: 1.98 us -> 15.4 us
  local copies, waits for them, and re-layouts: 0.01 us -> 1.81 us
    all_to_all x2 -> x3, blocking collectives: 40 us -> 102 us  [a2a(): return lax.all_to_all(x, axes, split_axis=0, concat_axis=0, tiled=True)]
    all_to_all x3 -> x1, waiting for transfers between devices: 33.3 us -> 5.5 us  [a2a(): return lax.all_to_all(x, axes, split_axis=0, concat_axis=0, tiled=True)]
    all_to_all x3 -> x1, starting transfers between devices: 30.8 us -> 7.66 us  [a2a(): return lax.all_to_all(x, axes, split_axis=0, concat_axis=0, tiled=True)]
    ppermute x0 -> x2, starting transfers between devices: none -> 5.05 us  [the longest x1 3.13 us: local(): neighbour = lax.ppermute(hidden, 'side', swap)]
    unnamed x4 -> x16, local copies, waits for them, and re-layouts: 0.01 us -> 1.81 us
    pallas_call x8 -> x9, Pallas kernels: 12.1 us -> 11.8 us  [call(): pl.pallas_call(kernel, out_shape=outs, in_specs=ins, out_specs=jax.tree.m...]
  transfers between devices with their start and end apart: 3 -> 4, of which waited for: 3 -> 3; matrix products, arithmetic and copies ran while one was open for 0% -> 0% of each run, Pallas kernels for 3% -> 5%
where the time goes in v4:
time: 153 us
  blocking collectives  102 us (67%)
  between operations  15.4 us (10%)
  starting transfers between devices  12.7 us (8%)
  Pallas kernels  11.8 us (8%)
  waiting for transfers between devices  8.49 us (6%)
  local copies, waits for them, and re-layouts  1.81 us (1%)
    all_to_all x3, blocking collectives, a2a(): return lax.all_to_all(x, axes, split_axis=0, concat_axis=0, tiled=True)  102 us
    pallas_call x9, Pallas kernels, call(): pl.pallas_call(kernel, out_shape=outs, in_specs=ins, out_specs=jax.tree.m...  11.8 us
    all_to_all x1, starting transfers between devices, a2a(): return lax.all_to_all(x, axes, split_axis=0, concat_axis=0, tiled=True)  7.66 us
    all_to_all x1, waiting for transfers between devices, a2a(): return lax.all_to_all(x, axes, split_axis=0, concat_axis=0, tiled=True)  5.5 us
    ppermute x1, starting transfers between devices, local(): neighbour = lax.ppermute(hidden, 'side', swap)  3.13 us
  transfers between devices with their start and end apart: 4, of which 3 were waited for; matrix products, arithmetic and copies ran while one was open for 0% of the time, Pallas kernels for 5%

profile of v4, /device:TPU:1, one launch (start us, length us, event | category | flops | bytes accessed | tf_op | source)
XLA Modules:
  0.0 152.6 jit_solution(7763637604331627009)
XLA Ops:
  7.2 0.0 all-gather.2.cloned.1.call-start
  7.2 0.7 all-gather.2.cloned.1.call-update
  7.9 1.9 %shard_map.167 = (bf16[128,768]{1,0:T(8,128)(2,1)}, f32[8,256]{1,0:T(8,128)S(1)}) custom-call(s32[1]{0:T(128)} %bitcast.5.refs_0_, bf16[128,256]{1,0:T(8,128)(2,1)} %refs_1_.3, f32[1,256]{1,0:T(1,128)} %bitcast.27, bf16[256,512]{1,0:T(8,128)(2,1)} %refs_3_.3, bf16[2,256]{1,0:T(2,128)(2,1)} %bitcast.28), custom_call_target="tpu_custom_call" | custom-call | tf_op jit(solution)/shard_map/pallas_call | solution.py:54
  9.8 7.7 %all-to-all-start = ((bf16[8,16,768]{2,1,0:T(8,128)(2,1)}), bf16[8,16,768]{2,1,0:T(8,128)(2,1)S(1)}, u32[]{:S(2)}, u32[]{:S(2)}) async-start(bf16[8,16,768]{2,1,0:T(8,128)(2,1)} %bitcast.9), calls=%async_computation | async-start | bytes 393216 | tf_op jit(solution)/shard_map/all_to_all | solution.py:281
  18.8 1.3 shard_map.166
  20.1 0.0 copy-start.6
  20.1 0.6 copy-done.6
  20.7 5.5 %all-to-all-done.refs_1_ = bf16[8,16,768]{2,1,0:T(8,128)(2,1)S(1)} async-done(((bf16[8,16,768]{2,1,0:T(8,128)(2,1)}), bf16[8,16,768]{2,1,0:T(8,128)(2,1)S(1)}, u32[]{:S(2)}, u32[]{:S(2)}) %all-to-all-start) | async-done | bytes 196640 | tf_op jit(solution)/shard_map/all_to_all | solution.py:281
  26.2 1.1 shard_map.168
  27.3 0.6 copy-done.2
  27.9 0.6 copy-done.4
  28.5 29.0 %all_to_all.20.refs_1_ = bf16[128,8,128]{2,1,0:T(8,128)(2,1)S(1)} all-to-all(bf16[128,8,128]{2,1,0:T(8,128)(2,1)S(1)} %get-tuple-element.24), channel_id=1, replica_groups=mesh['grp'=4,'head'=16,'quad'=4,'side'=2] {'head','quad','side'}, dimensions={0} | all-to-all | bytes 524288 | tf_op jit(solution)/shard_map/all_to_all | solution.py:281
  57.5 1.1 all-gather.2.cloned.1.call-done.refs_3_
  58.6 1.6 %shard_map.169.refs_1_.refs_3_ = bf16[8,256]{1,0:T(8,128)(2,1)S(1)} custom-call(s32[1]{0:T(128)} %bitcast.5.refs_0_, bf16[128,8,128]{2,1,0:T(8,128)(2,1)S(1)} %all_to_all.20.refs_1_, f32[8,256]{1,0:T(8,128)S(1)} %get-tuple-element.25.refs_2_, bf16[2048,256]{1,0:T(8,128)(2,1)} %all-gather.2.cloned.1.call-done.refs_3_), custom_call_target="tpu_custom_call" | custom-call | tf_op jit(solution)/shard_map/pallas_call | solution.py:54
  60.2 3.1 %collective-permute-start = (bf16[8,256]{1,0:T(8,128)(2,1)S(1)}, bf16[8,256]{1,0:T(8,128)(2,1)S(1)}, u32[]{:S(2)}, u32[]{:S(2)}) collective-permute-start(bf16[8,256]{1,0:T(8,128)(2,1)S(1)} %shard_map.169.refs_1_.refs_3_), channel_id=1, source_target_pairs={{0,1},{1,0},{2,3},{3,2},{4,5},{5,4},{6,7},{7,6},{8,9},{9,8},{10,11... | collective-permute-start | bytes 12296 | tf_op jit(solution)/shard_map/ppermute | solution.py:350
  63.3 1.2 collective-permute-done.refs_2_
  64.5 0.3 shard_map.170
  64.8 42.7 %all_to_all.21 = bf16[256,8,128]{2,1,0:T(8,128)(2,1)S(1)} all-to-all(bf16[256,8,128]{2,1,0:T(8,128)(2,1)S(1)} %bitcast.21), channel_id=1, replica_groups=mesh['grp'=4,'head'=16,'quad'=4,'side'=2] {'grp','head','quad'}, dimensions={0} | all-to-all | bytes 1048576 | tf_op jit(solution)/shard_map/all_to_all | solution.py:281
  107.6 1.9 %shard_map.171 = bf16[2048,128]{1,0:T(8,128)(2,1)S(1)} custom-call(bf16[2048,128]{1,0:T(8,128)(2,1)S(1)} %bitcast.22, f32[8,1,256]{2,1,0:T(1,128)S(1)} %copy-done.7, bf16[1,2048,512]{2,1,0:T(8,128)(2,1)S(1)} %copy-done, bf16[1,256,2048]{2,1,0:T(8,128)(2,1)S(1)} %copy-done.1), custom_call_target="tpu_custom_call" | custom-call | tf_op jit(solution)/shard_map/pallas_call | solution.py:54
  109.5 30.6 %all_to_all.22 = bf16[256,8,128]{2,1,0:T(8,128)(2,1)S(1)} all-to-all(bf16[256,8,128]{2,1,0:T(8,128)(2,1)S(1)} %bitcast.23), channel_id=1, replica_groups=mesh['grp'=4,'head'=16,'quad'=4,'side'=2] {'grp','head','quad'}, dimensions={0} | all-to-all | bytes 1048576 | tf_op jit(solution)/shard_map/all_to_all | solution.py:281
  140.1 0.2 shard_map.172
  140.3 1.9 %collective-permute-start.1 = (f32[8,256]{1,0:T(8,128)S(1)}, f32[8,256]{1,0:T(8,128)S(1)}, u32[]{:S(2)}, u32[]{:S(2)}) collective-permute-start(f32[8,256]{1,0:T(8,128)S(1)} %get-tuple-element.29), channel_id=1, source_target_pairs={{0,1},{1,0},{2,3},{3,2},{4,5},{5,4},{6,7},{7,6},{8,9},{9,8},{10,11... | collective-permute-start | bytes 24584 | tf_op jit(solution)/shard_map/ppermute | solution.py:370
  142.2 2.9 %shard_map.174 = (bf16[16,128,128]{2,1,0:T(8,128)(2,1)}, f32[16,128]{1,0:T(8,128)}) custom-call(bf16[16,128,128]{2,1,0:T(8,128)(2,1)S(1)} %get-tuple-element.21.refs_4_.refs_0_, f32[16,128]{1,0:T(8,128)S(1)} %copy-done.5, f32[16,128]{1,0:T(8,128)S(1)} %get-tuple-element.31.refs_2_, f32[16,128]{1,0:T(8,128)S(1)} %copy-done.3), custom_call_target="tpu_custom_call" | custom-call | tf_op jit(solution)/shard_map/pallas_call | solution.py:54
  145.1 0.6 shard_map.173
  (13 shorter events, 0.0 us)
Async XLA Ops:
  7.2 51.4 %all-gather.2.cloned.1.call-start = ((), (), s32[]{:S(2)}) async-start(), calls=%async_computation.4 | async-start | bytes 1114112 | tf_op jit(solution)/shard_map/all_gather | solution.py:304
  9.8 16.4 %all-to-all-start = ((bf16[8,16,768]{2,1,0:T(8,128)(2,1)}), bf16[8,16,768]{2,1,0:T(8,128)(2,1)S(1)}, u32[]{:S(2)}, u32[]{:S(2)}) async-start(bf16[8,16,768]{2,1,0:T(8,128)(2,1)} %bitcast.9), calls=%async_computation | async-start | bytes 393216 | tf_op jit(solution)/shard_map/all_to_all | solution.py:281
  20.1 0.6 copy-start.6
  27.3 0.6 copy-start.2
  27.9 0.6 copy-start.4
  28.5 79.1 %copy-start = (bf16[1,2048,512]{2,1,0:T(8,128)(2,1)S(1)}, bf16[1,2048,512]{2,1,0:T(8,128)(2,1)}, u32[]{:S(2)}) copy-start(bf16[1,2048,512]{2,1,0:T(8,128)(2,1)} %refs_2_.2) | copy-start | bytes 6291460
  58.6 49.0 %copy-start.1 = (bf16[1,256,2048]{2,1,0:T(8,128)(2,1)S(1)}, bf16[1,256,2048]{2,1,0:T(8,128)(2,1)}, u32[]{:S(2)}) copy-start(bf16[1,256,2048]{2,1,0:T(8,128)(2,1)} %refs_3_.4) | copy-start | bytes 3145732
  58.6 49.0 %copy-start.7 = (f32[8,1,256]{2,1,0:T(1,128)S(1)}, f32[8,1,256]{2,1,0:T(1,128)}, u32[]{:S(2)}) copy-start(f32[8,1,256]{2,1,0:T(1,128)} %copy-done.6) | copy-start | bytes 24580
  60.2 4.4 %collective-permute-start = (bf16[8,256]{1,0:T(8,128)(2,1)S(1)}, bf16[8,256]{1,0:T(8,128)(2,1)S(1)}, u32[]{:S(2)}, u32[]{:S(2)}) collective-permute-start(bf16[8,256]{1,0:T(8,128)(2,1)S(1)} %shard_map.169.refs_1_.refs_3_), channel_id=1, source_target_pairs={{0,1},{1,0},{2,3},{3,2},{4,5},{5,4},{6,7},{7,6},{8,9},{9,8},{10,11... | collective-permute-start | bytes 12296 | tf_op jit(solution)/shard_map/ppermute | solution.py:350
  107.5 34.7 %copy-start.3 = (f32[16,128]{1,0:T(8,128)S(1)}, f32[16,128]{1,0:T(8,128)}, u32[]{:S(2)}) copy-start(f32[16,128]{1,0:T(8,128)} %copy-done.2) | copy-start | bytes 24580
  107.5 34.7 %copy-start.5 = (f32[16,128]{1,0:T(8,128)S(1)}, f32[16,128]{1,0:T(8,128)}, u32[]{:S(2)}) copy-start(f32[16,128]{1,0:T(8,128)} %copy-done.4) | copy-start | bytes 24580
  140.3 4.9 %collective-permute-start.1 = (f32[8,256]{1,0:T(8,128)S(1)}, f32[8,256]{1,0:T(8,128)S(1)}, u32[]{:S(2)}, u32[]{:S(2)}) collective-permute-start(f32[8,256]{1,0:T(8,128)S(1)} %get-tuple-element.29), channel_id=1, source_target_pairs={{0,1},{1,0},{2,3},{3,2},{4,5},{5,4},{6,7},{7,6},{8,9},{9,8},{10,11... | collective-permute-start | bytes 24584 | tf_op jit(solution)/shard_map/ppermute | solution.py:370
Sparse Core Ops, SparseCore 0:
  10.1 48.4 all-gather.1

commit v5 on v3

--- a/solution.py
+++ b/solution.py
@@ -10,6 +10,9 @@
 TOPK = 10
 F32 = jnp.float32
 BF16 = jnp.bfloat16
+HEAD = ("z2", "z1", "z0", "core")
+SUB = ("y2", "y1", "y0")
+EVERY = ("grp", "core", "y0", "z0", "y1", "z1", "y2", "z2")
 
 VM = pl.BlockSpec(memory_space=pltpu.VMEM)
 SM = pl.BlockSpec(memory_space=pltpu.SMEM)
@@ -180,12 +183,17 @@
     ns_ref[...] = peaks.T
 
 
-def route_body(routes_in, scale_in, mt_ref, w_ref):
+def route_body(routes_in, scale_in, after_ref, mt_ref, w_ref):
     routes_ref, scale_ref = routes_in.get(), scale_in.get()
     n = 2048
     lane = lax.broadcasted_iota(jnp.int32, (8, n), 1)
-    expert = lane // 8
-    slot_of = lane // 2 % 2
+
+    def bit(i):
+        return (lane >> (i + 2)) & 1
+
+    z = bit(0) * 4 + bit(2) * 2 + bit(4)
+    expert = (((lane >> 9) * 8 + z) * 2 + bit(6)) * 4 + bit(1) * 2 + bit(3)
+    slot_of = (lane >> 1) & 1
     half = lane % 2
     sends = jnp.zeros((8, n), F32)
     weight = jnp.zeros((8, n), F32)
@@ -224,32 +232,32 @@
 def expert_body(x_ref, gain_ref, wgu_ref, wd_ref, out_ref, scr):
     scr[...] = x_ref[...].astype(F32).reshape(2048, 128)
 
-    def rows_of(c, slot, half):
-        return pl.ds(c * 4 + slot * 2 + half, 64, stride=32)
-
-    chunks = []
+    def rows_of(c, slot, z, half):
+        at = (c & 1) * 32 + (z & 1) * 16 + (c >> 1 & 1) * 8 + (z >> 1 & 1) * 4
+        at = at + (c >> 2) * 2 + (z >> 2)
+        return pl.ds(at * 4 + slot * 2 + half, 8, stride=256)
+
+    where = [(slot, z) for slot in range(2) for z in range(8)]
     sq = jnp.zeros((128, 128), F32)
+    acc = jnp.zeros((128, 512), F32)
     for c in range(8):
         halves = [
-            jnp.concatenate([scr[rows_of(c, slot, half), :] for slot in range(2)], axis=0)
+            jnp.concatenate([scr[rows_of(c, slot, z, half), :] for slot, z in where], axis=0)
             for half in range(2)
         ]
         sq = sq + halves[0] * halves[0] + halves[1] * halves[1]
-        chunks.append(jnp.concatenate(halves, axis=1))
-    rs = lax.rsqrt(jnp.sum(sq, axis=1, keepdims=True) / D + 1e-05)
-    acc = jnp.zeros((128, 512), F32)
-    for c in range(8):
-        xc = (chunks[c] * rs * gain_ref[c]).astype(BF16)
+        xc = (jnp.concatenate(halves, axis=1) * gain_ref[c]).astype(BF16)
         acc = acc + jnp.dot(
             xc, wgu_ref[0, c * 256 : (c + 1) * 256, :], preferred_element_type=F32
         )
+    acc = acc * lax.rsqrt(jnp.sum(sq, axis=1, keepdims=True) / D + 1e-05)
     act = (silu(acc[:, :256]) * acc[:, 256:]).astype(BF16)
     for c in range(8):
         o = jnp.dot(act, wd_ref[0, :, c * 256 : (c + 1) * 256], preferred_element_type=F32)
-        for slot in range(2):
+        for i, (slot, z) in enumerate(where):
             for half in range(2):
-                scr[rows_of(c, slot, half), :] = o[
-                    slot * 64 : (slot + 1) * 64, half * 128 : (half + 1) * 128
+                scr[rows_of(c, slot, z, half), :] = o[
+                    i * 8 : (i + 1) * 8, half * 128 : (half + 1) * 128
                 ]
     out_ref[...] = scr[...].reshape(512, 4, 128).astype(BF16)
 
@@ -286,7 +294,7 @@
     w_gate_up,
     w_down,
 ):
-    head = lax.axis_index("head").astype(jnp.int32).reshape(1)
+    head = lax.axis_index(HEAD).astype(jnp.int32).reshape(1)
     sv = state_values.reshape(16, 128, 128)
     ss = state_scales.reshape(16, 128)
     part, resid, sv, ss, ngain, w_out, pgain = call(
@@ -315,20 +323,20 @@
         ),
         [pltpu.SemaphoreType.DMA((5,))],
     )
-    part = a2a(part.reshape(8, 16, 768), "sub")
-    mt, wsel = call(
-        route_body,
-        (shape((2048, 16)), shape((16, 2048))),
-        [HB, HB],
-        (routes, route_scale),
-    )
+    part = a2a(part.reshape(8, 16, 768), SUB)
     gated, keys, delta, sd = call(
         recur_body,
         (shape((8, 16, 128)), shape((16, 128), F32), shape((16, 128), F32), shape((16, 128), F32)),
         [VM, SM, SM, VM, VM, VM],
         (part, a_log, dt_bias, sv, ss, ngain),
     )
-    gathered = a2a(gated, "sub").reshape(128, 128)
+    mt, wsel = call(
+        route_body,
+        (shape((2048, 16)), shape((16, 2048))),
+        [HB, HB, VM],
+        (routes, route_scale, sd),
+    )
+    gathered = a2a(gated, SUB).reshape(128, 128)
     new_values, new_scales = call(
         state_body,
         (shape((16, 128, 128)), shape((16, 128), F32)),
@@ -336,15 +344,14 @@
         (sv, sd, keys, delta),
     )
     attn = call(outproj_body, shape((128, 256)), [VM] * 2, (gathered, w_out))
-    attn = a2a(attn.reshape(16, 8, 256), "head")
+    attn = a2a(attn.reshape(16, 8, 256), HEAD)
     hidden, sent = call(
         dispatch_body,
         (shape((8, 256)), shape((512, 4, 128))),
         [VM] * 3,
         (attn, resid, mt),
     )
-    every = ("grp", "head", "sub")
-    received = a2a(sent, every)
+    received = a2a(sent, EVERY)
     result = call(
         expert_body,
         shape((512, 4, 128)),
@@ -352,37 +359,37 @@
         (received, pgain, w_gate_up, w_down),
         [pltpu.VMEM((2048, 128), F32)],
     )
-    back = a2a(result, every)
+    back = a2a(result, EVERY)
     out = call(combine_body, shape((8, 256)), [VM] * 3, (wsel, back, hidden))
     return (out, new_values.reshape(16, 1, 128, 128), new_scales.reshape(16, 1, 128))
 
 
 def solution(mesh):
+    names = ("grp",) + HEAD + SUB
+    parts = (mesh.shape["grp"],) + (2,) * 7
+    mesh = jax.sharding.Mesh(mesh.devices.reshape(parts), names)
+    rows = ("grp",) + SUB
     placed = (
-        P("grp", "sub"),
-        P("sub"),
-        P("sub", "head"),
-        P("sub", "head"),
-        P("head"),
-        P("head"),
-        P(("grp", "sub"), "head", None, None),
-        P(("grp", "sub"), "head", None),
+        P("grp", SUB),
+        P(SUB),
+        P(SUB, HEAD),
+        P(SUB, HEAD),
+        P(HEAD),
+        P(HEAD),
+        P(rows, HEAD, None, None),
+        P(rows, HEAD, None),
         P(),
-        P("head", "sub"),
+        P(HEAD, SUB),
         P(),
-        P(("grp", "head"), None),
-        P(("grp", "head"), None),
-        P(("grp", "head", "sub"), None, None),
-        P(("grp", "head", "sub"), None, None),
+        P(("grp",) + HEAD, None),
+        P(("grp",) + HEAD, None),
+        P(names, None, None),
+        P(names, None, None),
     )
     return jax.shard_map(
         local,
         mesh=mesh,
         in_specs=placed,
-        out_specs=(
-            P(("grp", "head"), "sub"),
-            P(("grp", "sub"), "head", None, None),
-            P(("grp", "sub"), "head", None),
-        ),
+        out_specs=(P(("grp",) + HEAD, SUB), P(rows, HEAD, None, None), P(rows, HEAD, None)),
         check_vma=False,
     )

time: 119 us -> 120 us (level)
  blocking collectives: 40 us -> 41.3 us
    all_to_all x2, blocking collectives: 40 us -> 41.3 us  [a2a(): return lax.all_to_all(x, axes, split_axis=0, concat_axis=0, tiled=True)]
where the time goes in v5:
time: 120 us
  blocking collectives  41.3 us (34%)
  waiting for transfers between devices  34.4 us (29%)
  starting transfers between devices  30.2 us (25%)
  Pallas kernels  12.2 us (10%)
  between operations  1.99 us (2%)
    all_to_all x2, blocking collectives, a2a(): return lax.all_to_all(x, axes, split_axis=0, concat_axis=0, tiled=True)  41.3 us
    all_to_all x3, waiting for transfers between devices, a2a(): return lax.all_to_all(x, axes, split_axis=0, concat_axis=0, tiled=True)  34.4 us
    all_to_all x3, starting transfers between devices, a2a(): return lax.all_to_all(x, axes, split_axis=0, concat_axis=0, tiled=True)  30.2 us
    pallas_call x8, Pallas kernels, call(): pl.pallas_call(kernel, out_shape=outs, in_specs=ins, out_specs=jax.tree.m...  12.2 us
  transfers between devices with their start and end apart: 3, of which 3 were waited for; matrix products, arithmetic and copies ran while one was open for 0% of the time, Pallas kernels for 3%

profile of v5, /device:TPU:1, one launch (start us, length us, event | category | flops | bytes accessed | tf_op | source)
XLA Modules:
  0.0 120.0 jit_solution(3277176967040445266)
XLA Ops:
  0.6 0.0 copy-start
  0.7 2.3 %shard_map.166 = (bf16[128,768]{1,0:T(8,128)(2,1)}, f32[8,256]{1,0:T(8,128)S(1)}, bf16[16,128,128]{2,1,0:T(8,128)(2,1)S(1)}, f32[16,128]{1,0:T(8,128)S(1)}, f32[...) custom-call(s32[1]{0:T(128)} %bitcast.refs_0_, bf16[128,256]{1,0:T(8,128)(2,1)} %refs_1_.3, ...), custom_call_target="tpu_custom_call" | custom-call | tf_op jit(solution)/shard_map/pallas_call | solution.py:56
  2.9 7.7 %all-to-all-start = ((bf16[8,16,768]{2,1,0:T(8,128)(2,1)}), bf16[8,16,768]{2,1,0:T(8,128)(2,1)S(1)}, u32[]{:S(2)}, u32[]{:S(2)}) async-start(bf16[8,16,768]{2,1,0:T(8,128)(2,1)} %bitcast.7), calls=%async_computation | async-start | bytes 393216 | tf_op jit(solution)/shard_map/all_to_all | solution.py:277
  11.9 7.4 %all-to-all-done.refs_0_ = bf16[8,16,768]{2,1,0:T(8,128)(2,1)S(1)} async-done(((bf16[8,16,768]{2,1,0:T(8,128)(2,1)}), bf16[8,16,768]{2,1,0:T(8,128)(2,1)S(1)}, u32[]{:S(2)}, u32[]{:S(2)}) %all-to-all-start) | async-done | bytes 196640 | tf_op jit(solution)/shard_map/all_to_all | solution.py:277
  19.3 1.1 shard_map.167
  20.4 9.2 %all_to_all.25 = bf16[8,16,128]{2,1,0:T(8,128)(2,1)S(1)} all-to-all(bf16[8,16,128]{2,1,0:T(8,128)(2,1)S(1)} %get-tuple-element.26), channel_id=1, replica_groups=mesh['grp'=4,'z2'=2,'z1'=2,'z0'=2,'core'=2,'y2'=2,'y1'=2,'y0'=2] {'y2','..., dimensions={0} | all-to-all | bytes 65536 | tf_op jit(solution)/shard_map/all_to_all | solution.py:277
  29.6 0.8 shard_map.169
  30.4 14.2 %all-to-all-start.2 = ((bf16[16,8,256]{2,1,0:T(8,128)(2,1)}), bf16[16,8,256]{2,1,0:T(8,128)(2,1)S(1)}, u32[]{:S(2)}, u32[]{:S(2)}) async-start(bf16[16,8,256]{2,1,0:T(8,128)(2,1)} %bitcast.9), calls=%async_computation.2 | async-start | bytes 131072 | tf_op jit(solution)/shard_map/all_to_all | solution.py:277
  44.6 1.1 shard_map.168
  45.7 6.7 %all-to-all-done.2.refs_0_ = bf16[16,8,256]{2,1,0:T(8,128)(2,1)S(1)} async-done(((bf16[16,8,256]{2,1,0:T(8,128)(2,1)}), bf16[16,8,256]{2,1,0:T(8,128)(2,1)S(1)}, u32[]{:S(2)}, u32[]{:S(2)}) %all-to-all-start.2) | async-done | bytes 65568 | tf_op jit(solution)/shard_map/all_to_all | solution.py:277
  52.4 0.0 copy-start.1
  52.4 0.3 shard_map.170
  52.7 32.1 %all_to_all.26.refs_0_ = bf16[512,4,128]{2,1,0:T(4,128)(2,1)S(1)} all-to-all(bf16[512,4,128]{2,1,0:T(4,128)(2,1)S(1)} %get-tuple-element.30), channel_id=1, replica_groups=mesh['grp'=4,'z2'=2,'z1'=2,'z0'=2,'core'=2,'y2'=2,'y1'=2,'y0'=2] {'grp',..., dimensions={0} | all-to-all | bytes 1048576 | tf_op jit(solution)/shard_map/all_to_all | solution.py:277
  84.7 0.0 copy-done
  84.7 0.0 copy-done.1
  84.8 3.0 %shard_map.171 = bf16[512,4,128]{2,1,0:T(4,128)(2,1)} custom-call(bf16[512,4,128]{2,1,0:T(4,128)(2,1)S(1)} %all_to_all.26.refs_0_, f32[8,1,256]{2,1,0:T(1,128)S(1)} %get-tuple-element.31.refs_1_, bf16[1,2048,512]{2,1,0:T(8,128)(2,1)S(1)} %copy-done, bf16[1,256,2048]{2,1,0:T(8,128)(2,1)S(1)} %copy-done.1), custom_call_target="tpu_custom_call" | custom-call | tf_op jit(solution)/shard_map/pallas_call | solution.py:56
  87.7 8.4 %all-to-all-start.4 = ((bf16[512,4,128]{2,1,0:T(4,128)(2,1)}), bf16[512,4,128]{2,1,0:T(4,128)(2,1)S(1)}, u32[]{:S(2)}, u32[]{:S(2)}) async-start(bf16[512,4,128]{2,1,0:T(4,128)(2,1)} %shard_map.171), calls=%async_computation.4 | async-start | bytes 1048576 | tf_op jit(solution)/shard_map/all_to_all | solution.py:277
  96.1 2.9 %shard_map.173 = (bf16[16,128,128]{2,1,0:T(8,128)(2,1)}, f32[16,128]{1,0:T(8,128)}) custom-call(bf16[16,128,128]{2,1,0:T(8,128)(2,1)S(1)} %get-tuple-element.21.refs_3_.refs_0_, f32[16,128]{1,0:T(8,128)S(1)} %get-tuple-element.24.refs_2_.refs_1_, f32[16,128]{1,0:T(8,128)S(1)} %get-tuple-element.33.refs_2_, f32[16,128]{1,0:T(8,128)S(1)} %get-tuple-element.34.refs_3_), custom_call_target="tpu_custom_call" | custom-call | tf_op jit(solution)/shard_map/pallas_call | solution.py:56
  99.0 20.2 %all-to-all-done.4.refs_1_ = bf16[512,4,128]{2,1,0:T(4,128)(2,1)S(1)} async-done(((bf16[512,4,128]{2,1,0:T(4,128)(2,1)}), bf16[512,4,128]{2,1,0:T(4,128)(2,1)S(1)}, u32[]{:S(2)}, u32[]{:S(2)}) %all-to-all-start.4) | async-done | bytes 524320 | tf_op jit(solution)/shard_map/all_to_all | solution.py:277
  119.2 0.8 shard_map.172
Async XLA Ops:
  0.6 84.1 %copy-start = (bf16[1,2048,512]{2,1,0:T(8,128)(2,1)S(1)}, bf16[1,2048,512]{2,1,0:T(8,128)(2,1)}, u32[]{:S(2)}) copy-start(bf16[1,2048,512]{2,1,0:T(8,128)(2,1)} %refs_2_.2) | copy-start | bytes 6291460
  2.9 16.4 %all-to-all-start = ((bf16[8,16,768]{2,1,0:T(8,128)(2,1)}), bf16[8,16,768]{2,1,0:T(8,128)(2,1)S(1)}, u32[]{:S(2)}, u32[]{:S(2)}) async-start(bf16[8,16,768]{2,1,0:T(8,128)(2,1)} %bitcast.7), calls=%async_computation | async-start | bytes 393216 | tf_op jit(solution)/shard_map/all_to_all | solution.py:277
  30.4 22.0 %all-to-all-start.2 = ((bf16[16,8,256]{2,1,0:T(8,128)(2,1)}), bf16[16,8,256]{2,1,0:T(8,128)(2,1)S(1)}, u32[]{:S(2)}, u32[]{:S(2)}) async-start(bf16[16,8,256]{2,1,0:T(8,128)(2,1)} %bitcast.9), calls=%async_computation.2 | async-start | bytes 131072 | tf_op jit(solution)/shard_map/all_to_all | solution.py:277
  52.4 32.4 %copy-start.1 = (bf16[1,256,2048]{2,1,0:T(8,128)(2,1)S(1)}, bf16[1,256,2048]{2,1,0:T(8,128)(2,1)}, u32[]{:S(2)}) copy-start(bf16[1,256,2048]{2,1,0:T(8,128)(2,1)} %refs_3_.3) | copy-start | bytes 3145732
  87.7 31.5 %all-to-all-start.4 = ((bf16[512,4,128]{2,1,0:T(4,128)(2,1)}), bf16[512,4,128]{2,1,0:T(4,128)(2,1)S(1)}, u32[]{:S(2)}, u32[]{:S(2)}) async-start(bf16[512,4,128]{2,1,0:T(4,128)(2,1)} %shard_map.171), calls=%async_computation.4 | async-start | bytes 1048576 | tf_op jit(solution)/shard_map/all_to_all | solution.py:277

commit v6 on v3

--- a/solution.py
+++ b/solution.py
@@ -166,7 +166,8 @@
     sd_ref[...] = sd
 
 
-def state_body(sv_ref, sd_ref, keys_ref, delta_ref, nv_ref, ns_ref):
+def state_body(sv_ref, sd_ref, keys_ref, delta_ref, nv_ref, ns_ref, done_ref):
+    done_ref[...] = jnp.zeros((8, 128), F32)
     rows = 16
     sdt = sd_ref[...].T
     kt = keys_ref[...].T
@@ -175,7 +176,7 @@
     for r in range(rows):
         s = sv_ref[r].astype(F32) * sdt[:, r : r + 1] + kt[:, r : r + 1] * delta_ref[r : r + 1, :]
         peak = jnp.max(jnp.abs(s), axis=1, keepdims=True) + 1e-06
-        nv_ref[r] = (s / peak).astype(BF16)
+        nv_ref[r] = (s * (1.0 / peak)).astype(BF16)
         peaks = jnp.where(lane == r, peak, peaks)
     ns_ref[...] = peaks.T
 
@@ -211,38 +212,35 @@
     out_ref[...] = jnp.dot(x_ref[...], w_ref[...], preferred_element_type=F32).astype(BF16)
 
 
-def dispatch_body(attn_ref, resid_ref, mt_ref, hidden_ref, out_ref):
+def dispatch_body(attn_ref, resid_ref, mt_ref, after_ref, hidden_ref, out_ref):
     attn = jnp.sum(attn_ref[...].astype(F32), axis=0)
     hidden = (resid_ref[...] + attn).astype(BF16)
     hidden_ref[...] = hidden
     hf = hidden.astype(F32)
     halves = jnp.concatenate([hf[:, :128], hf[:, 128:]], axis=0).astype(BF16)
     sent = jnp.dot(mt_ref[...], halves, preferred_element_type=F32)
-    out_ref[...] = sent.reshape(512, 4, 128).astype(BF16)
+    out_ref[...] = sent.astype(BF16)
 
 
 def expert_body(x_ref, gain_ref, wgu_ref, wd_ref, out_ref, scr):
-    scr[...] = x_ref[...].astype(F32).reshape(2048, 128)
+    scr[...] = x_ref[...].astype(F32)
 
     def rows_of(c, slot, half):
         return pl.ds(c * 4 + slot * 2 + half, 64, stride=32)
 
-    chunks = []
     sq = jnp.zeros((128, 128), F32)
+    acc = jnp.zeros((128, 512), F32)
     for c in range(8):
         halves = [
             jnp.concatenate([scr[rows_of(c, slot, half), :] for slot in range(2)], axis=0)
             for half in range(2)
         ]
         sq = sq + halves[0] * halves[0] + halves[1] * halves[1]
-        chunks.append(jnp.concatenate(halves, axis=1))
-    rs = lax.rsqrt(jnp.sum(sq, axis=1, keepdims=True) / D + 1e-05)
-    acc = jnp.zeros((128, 512), F32)
-    for c in range(8):
-        xc = (chunks[c] * rs * gain_ref[c]).astype(BF16)
+        xc = (jnp.concatenate(halves, axis=1) * gain_ref[c]).astype(BF16)
         acc = acc + jnp.dot(
             xc, wgu_ref[0, c * 256 : (c + 1) * 256, :], preferred_element_type=F32
         )
+    acc = acc * lax.rsqrt(jnp.sum(sq, axis=1, keepdims=True) / D + 1e-05)
     act = (silu(acc[:, :256]) * acc[:, 256:]).astype(BF16)
     for c in range(8):
         o = jnp.dot(act, wd_ref[0, :, c * 256 : (c + 1) * 256], preferred_element_type=F32)
@@ -251,12 +249,11 @@
                 scr[rows_of(c, slot, half), :] = o[
                     slot * 64 : (slot + 1) * 64, half * 128 : (half + 1) * 128
                 ]
-    out_ref[...] = scr[...].reshape(512, 4, 128).astype(BF16)
+    out_ref[...] = scr[...].astype(BF16)
 
 
 def combine_body(w_ref, x_ref, hidden_ref, out_ref):
-    x = x_ref[...].astype(F32).reshape(2048, 128).astype(BF16)
-    moe = jnp.dot(w_ref[...], x, preferred_element_type=F32)
+    moe = jnp.dot(w_ref[...], x_ref[...], preferred_element_type=F32)
     moe = jnp.concatenate([moe[:8], moe[8:]], axis=1)
     out_ref[...] = (hidden_ref[...].astype(F32) + moe).astype(BF16)
 
@@ -329,9 +326,9 @@
         (part, a_log, dt_bias, sv, ss, ngain),
     )
     gathered = a2a(gated, "sub").reshape(128, 128)
-    new_values, new_scales = call(
+    new_values, new_scales, done = call(
         state_body,
-        (shape((16, 128, 128)), shape((16, 128), F32)),
+        (shape((16, 128, 128)), shape((16, 128), F32), shape((8, 128), F32)),
         [VM] * 4,
         (sv, sd, keys, delta),
     )
@@ -339,20 +336,20 @@
     attn = a2a(attn.reshape(16, 8, 256), "head")
     hidden, sent = call(
         dispatch_body,
-        (shape((8, 256)), shape((512, 4, 128))),
-        [VM] * 3,
-        (attn, resid, mt),
+        (shape((8, 256)), shape((2048, 128))),
+        [VM] * 4,
+        (attn, resid, mt, done),
     )
     every = ("grp", "head", "sub")
-    received = a2a(sent, every)
+    received = a2a(sent.reshape(512, 4, 128), every).reshape(2048, 128)
     result = call(
         expert_body,
-        shape((512, 4, 128)),
+        shape((2048, 128)),
         [VM] * 4,
         (received, pgain, w_gate_up, w_down),
         [pltpu.VMEM((2048, 128), F32)],
     )
-    back = a2a(result, every)
+    back = a2a(result.reshape(512, 4, 128), every).reshape(2048, 128)
     out = call(combine_body, shape((8, 256)), [VM] * 3, (wsel, back, hidden))
     return (out, new_values.reshape(16, 1, 128, 128), new_scales.reshape(16, 1, 128))
 

time: 119 us -> 119 us (level)
  blocking collectives: 40 us -> 71.7 us
  waiting for transfers between devices: 33.3 us -> 10.5 us
  starting transfers between devices: 30.8 us -> 22 us
  local copies, waits for them, and re-layouts: 0.01 us -> 1.85 us
  Pallas kernels: 12.1 us -> 10.6 us
    all_to_all x2 -> x3, blocking collectives: 40 us -> 71.7 us  [a2a(): return lax.all_to_all(x, axes, split_axis=0, concat_axis=0, tiled=True)]
    all_to_all x3 -> x2, waiting for transfers between devices: 33.3 us -> 10.5 us  [a2a(): return lax.all_to_all(x, axes, split_axis=0, concat_axis=0, tiled=True)]
    all_to_all x3 -> x2, starting transfers between devices: 30.8 us -> 22 us  [a2a(): return lax.all_to_all(x, axes, split_axis=0, concat_axis=0, tiled=True)]
    unnamed x4 -> x8, local copies, waits for them, and re-layouts: 0.01 us -> 1.85 us
    pallas_call x8, Pallas kernels: 12.1 us -> 10.6 us  [call(): pl.pallas_call(kernel, out_shape=outs, in_specs=ins, out_specs=jax.tree.m...]
  transfers between devices with their start and end apart: 3 -> 2, of which waited for: 3 -> 2; matrix products, arithmetic and copies ran while one was open for 0% -> 0% of each run, Pallas kernels for 3% -> 3%
where the time goes in v6:
time: 119 us
  blocking collectives  71.7 us (60%)
  starting transfers between devices  22 us (18%)
  Pallas kernels  10.6 us (9%)
  waiting for transfers between devices  10.5 us (9%)
  between operations  1.99 us (2%)
  local copies, waits for them, and re-layouts  1.85 us (2%)
    all_to_all x3, blocking collectives, a2a(): return lax.all_to_all(x, axes, split_axis=0, concat_axis=0, tiled=True)  71.7 us
    all_to_all x2, starting transfers between devices, a2a(): return lax.all_to_all(x, axes, split_axis=0, concat_axis=0, tiled=True)  22 us
    pallas_call x8, Pallas kernels, call(): pl.pallas_call(kernel, out_shape=outs, in_specs=ins, out_specs=jax.tree.m...  10.6 us
    all_to_all x2, waiting for transfers between devices, a2a(): return lax.all_to_all(x, axes, split_axis=0, concat_axis=0, tiled=True)  10.5 us
  transfers between devices with their start and end apart: 2, of which 2 were waited for; matrix products, arithmetic and copies ran while one was open for 0% of the time, Pallas kernels for 3%

profile of v6, /device:TPU:1, one launch (start us, length us, event | category | flops | bytes accessed | tf_op | source)
XLA Modules:
  0.0 118.6 jit_solution(17982974585302370593)
XLA Ops:
  0.6 2.1 %shard_map.167 = (bf16[128,768]{1,0:T(8,128)(2,1)}, f32[8,256]{1,0:T(8,128)S(1)}, bf16[16,128,128]{2,1,0:T(8,128)(2,1)S(1)}, f32[16,128]{1,0:T(8,128)S(1)}, f32[...) custom-call(s32[1]{0:T(128)} %bitcast.refs_0_, bf16[128,256]{1,0:T(8,128)(2,1)} %refs_1_.4, ...), custom_call_target="tpu_custom_call" | custom-call | tf_op jit(solution)/shard_map/pallas_call | solution.py:53
  2.8 0.0 copy-start
  2.8 7.8 %all-to-all-start = ((bf16[8,16,768]{2,1,0:T(8,128)(2,1)}), bf16[8,16,768]{2,1,0:T(8,128)(2,1)S(1)}, u32[]{:S(2)}, u32[]{:S(2)}) async-start(bf16[8,16,768]{2,1,0:T(8,128)(2,1)} %bitcast.7), calls=%async_computation | async-start | bytes 393216 | tf_op jit(solution)/shard_map/all_to_all | solution.py:266
  11.9 7.4 %all-to-all-done.refs_0_ = bf16[8,16,768]{2,1,0:T(8,128)(2,1)S(1)} async-done(((bf16[8,16,768]{2,1,0:T(8,128)(2,1)}), bf16[8,16,768]{2,1,0:T(8,128)(2,1)S(1)}, u32[]{:S(2)}, u32[]{:S(2)}) %all-to-all-start) | async-done | bytes 196640 | tf_op jit(solution)/shard_map/all_to_all | solution.py:266
  19.3 1.1 shard_map.168
  20.4 9.2 %all_to_all.25 = bf16[8,16,128]{2,1,0:T(8,128)(2,1)S(1)} all-to-all(bf16[8,16,128]{2,1,0:T(8,128)(2,1)S(1)} %get-tuple-element.26), channel_id=1, replica_groups=mesh['grp'=4,'head'=16,'sub'=8] {'sub'}, dimensions={0} | all-to-all | bytes 65536 | tf_op jit(solution)/shard_map/all_to_all | solution.py:266
  29.6 0.8 shard_map.169
  30.4 14.2 %all-to-all-start.2 = ((bf16[16,8,256]{2,1,0:T(8,128)(2,1)}), bf16[16,8,256]{2,1,0:T(8,128)(2,1)S(1)}, u32[]{:S(2)}, u32[]{:S(2)}) async-start(bf16[16,8,256]{2,1,0:T(8,128)(2,1)} %bitcast.9), calls=%async_computation.2 | async-start | bytes 131072 | tf_op jit(solution)/shard_map/all_to_all | solution.py:266
  44.6 1.1 shard_map.166
  45.6 0.0 copy-start.2
  45.6 0.8 copy-done.2
  46.4 2.9 %shard_map.170 = (bf16[16,128,128]{2,1,0:T(8,128)(2,1)}, f32[16,128]{1,0:T(8,128)}, f32[8,128]{1,0:T(8,128)S(1)}) custom-call(bf16[16,128,128]{2,1,0:T(8,128)(2,1)S(1)} %get-tuple-element.23.refs_3_.refs_0_, f32[16,128]{1,0:T(8,128)S(1)} %get-tuple-element.30.refs_1_, f32[16,128]{1,0:T(8,128)S(1)} %get-tuple-element.31.refs_2_, ...), custom_call_target="tpu_custom_call" | custom-call | tf_op jit(solution)/shard_map/pallas_call | solution.py:53
  49.3 0.0 copy-start.1
  49.3 3.0 %all-to-all-done.2.refs_0_ = bf16[16,8,256]{2,1,0:T(8,128)(2,1)S(1)} async-done(((bf16[16,8,256]{2,1,0:T(8,128)(2,1)}), bf16[16,8,256]{2,1,0:T(8,128)(2,1)S(1)}, u32[]{:S(2)}, u32[]{:S(2)}) %all-to-all-start.2) | async-done | bytes 65568 | tf_op jit(solution)/shard_map/all_to_all | solution.py:266
  52.4 0.0 copy-start.3
  52.4 1.0 copy-done.3
  53.4 0.3 shard_map.171
  53.7 31.1 %all_to_all.26 = bf16[512,4,128]{2,1,0:T(4,128)(2,1)S(1)} all-to-all(bf16[512,4,128]{2,1,0:T(4,128)(2,1)S(1)} %bitcast.23), channel_id=1, replica_groups=mesh['grp'=4,'head'=16,'sub'=8] {'grp','head','sub'}, dimensions={0} | all-to-all | bytes 1048576 | tf_op jit(solution)/shard_map/all_to_all | solution.py:266
  84.7 0.0 copy-done
  84.7 0.0 copy-done.1
  84.8 1.7 %shard_map.172 = bf16[2048,128]{1,0:T(8,128)(2,1)S(1)} custom-call(bf16[2048,128]{1,0:T(8,128)(2,1)S(1)} %bitcast.21, f32[8,1,256]{2,1,0:T(1,128)S(1)} %get-tuple-element.35.refs_1_, bf16[1,2048,512]{2,1,0:T(8,128)(2,1)S(1)} %copy-done, bf16[1,256,2048]{2,1,0:T(8,128)(2,1)S(1)} %copy-done.1), custom_call_target="tpu_custom_call" | custom-call | tf_op jit(solution)/shard_map/pallas_call | solution.py:53
  86.4 31.4 %all_to_all.27 = bf16[512,4,128]{2,1,0:T(4,128)(2,1)S(1)} all-to-all(bf16[512,4,128]{2,1,0:T(4,128)(2,1)S(1)} %bitcast.22), channel_id=1, replica_groups=mesh['grp'=4,'head'=16,'sub'=8] {'grp','head','sub'}, dimensions={0} | all-to-all | bytes 1048576 | tf_op jit(solution)/shard_map/all_to_all | solution.py:266
  117.8 0.8 shard_map.173
Async XLA Ops:
  2.8 82.0 %copy-start = (bf16[1,2048,512]{2,1,0:T(8,128)(2,1)S(1)}, bf16[1,2048,512]{2,1,0:T(8,128)(2,1)}, u32[]{:S(2)}) copy-start(bf16[1,2048,512]{2,1,0:T(8,128)(2,1)} %refs_2_.2) | copy-start | bytes 6291460
  2.8 16.5 %all-to-all-start = ((bf16[8,16,768]{2,1,0:T(8,128)(2,1)}), bf16[8,16,768]{2,1,0:T(8,128)(2,1)S(1)}, u32[]{:S(2)}, u32[]{:S(2)}) async-start(bf16[8,16,768]{2,1,0:T(8,128)(2,1)} %bitcast.7), calls=%async_computation | async-start | bytes 393216 | tf_op jit(solution)/shard_map/all_to_all | solution.py:266
  30.4 22.0 %all-to-all-start.2 = ((bf16[16,8,256]{2,1,0:T(8,128)(2,1)}), bf16[16,8,256]{2,1,0:T(8,128)(2,1)S(1)}, u32[]{:S(2)}, u32[]{:S(2)}) async-start(bf16[16,8,256]{2,1,0:T(8,128)(2,1)} %bitcast.9), calls=%async_computation.2 | async-start | bytes 131072 | tf_op jit(solution)/shard_map/all_to_all | solution.py:266
  45.6 0.8 copy-start.2
  49.3 35.4 %copy-start.1 = (bf16[1,256,2048]{2,1,0:T(8,128)(2,1)S(1)}, bf16[1,256,2048]{2,1,0:T(8,128)(2,1)}, u32[]{:S(2)}) copy-start(bf16[1,256,2048]{2,1,0:T(8,128)(2,1)} %refs_3_.3) | copy-start | bytes 3145732
  52.4 1.0 copy-start.3

commit v7 on v6

--- a/solution.py
+++ b/solution.py
@@ -10,6 +10,7 @@
 TOPK = 10
 F32 = jnp.float32
 BF16 = jnp.bfloat16
+SUB = ("quad", "side")
 
 VM = pl.BlockSpec(memory_space=pltpu.VMEM)
 SM = pl.BlockSpec(memory_space=pltpu.SMEM)
@@ -166,8 +167,7 @@
     sd_ref[...] = sd
 
 
-def state_body(sv_ref, sd_ref, keys_ref, delta_ref, nv_ref, ns_ref, done_ref):
-    done_ref[...] = jnp.zeros((8, 128), F32)
+def state_body(sv_ref, sd_ref, keys_ref, delta_ref, nv_ref, ns_ref):
     rows = 16
     sdt = sd_ref[...].T
     kt = keys_ref[...].T
@@ -183,9 +183,9 @@
 
 def route_body(routes_in, scale_in, mt_ref, w_ref):
     routes_ref, scale_ref = routes_in.get(), scale_in.get()
-    n = 2048
+    n = 1024
     lane = lax.broadcasted_iota(jnp.int32, (8, n), 1)
-    expert = lane // 8
+    expert = lane // 4
     slot_of = lane // 2 % 2
     half = lane % 2
     sends = jnp.zeros((8, n), F32)
@@ -212,7 +212,7 @@
     out_ref[...] = jnp.dot(x_ref[...], w_ref[...], preferred_element_type=F32).astype(BF16)
 
 
-def dispatch_body(attn_ref, resid_ref, mt_ref, after_ref, hidden_ref, out_ref):
+def dispatch_body(attn_ref, resid_ref, mt_ref, hidden_ref, out_ref):
     attn = jnp.sum(attn_ref[...].astype(F32), axis=0)
     hidden = (resid_ref[...] + attn).astype(BF16)
     hidden_ref[...] = hidden
@@ -222,33 +222,33 @@
     out_ref[...] = sent.astype(BF16)
 
 
-def expert_body(x_ref, gain_ref, wgu_ref, wd_ref, out_ref, scr):
+def expert_body(x_ref, gain_ref, wgu_ref, wd_ref, wgu2_ref, wd2_ref, out_ref, scr):
     scr[...] = x_ref[...].astype(F32)
 
-    def rows_of(c, slot, half):
-        return pl.ds(c * 4 + slot * 2 + half, 64, stride=32)
-
-    sq = jnp.zeros((128, 128), F32)
-    acc = jnp.zeros((128, 512), F32)
+    def rows_of(c, half):
+        return pl.ds(c * 2 + half, 64, stride=16)
+
+    sq = jnp.zeros((64, 128), F32)
+    acc = jnp.zeros((64, 512), F32)
+    acc2 = jnp.zeros((64, 512), F32)
     for c in range(8):
-        halves = [
-            jnp.concatenate([scr[rows_of(c, slot, half), :] for slot in range(2)], axis=0)
-            for half in range(2)
-        ]
+        halves = [scr[rows_of(c, half), :] for half in range(2)]
         sq = sq + halves[0] * halves[0] + halves[1] * halves[1]
         xc = (jnp.concatenate(halves, axis=1) * gain_ref[c]).astype(BF16)
-        acc = acc + jnp.dot(
-            xc, wgu_ref[0, c * 256 : (c + 1) * 256, :], preferred_element_type=F32
-        )
-    acc = acc * lax.rsqrt(jnp.sum(sq, axis=1, keepdims=True) / D + 1e-05)
+        part = slice(c * 256, (c + 1) * 256)
+        acc = acc + jnp.dot(xc, wgu_ref[0, part, :], preferred_element_type=F32)
+        acc2 = acc2 + jnp.dot(xc, wgu2_ref[0, part, :], preferred_element_type=F32)
+    rs = lax.rsqrt(jnp.sum(sq, axis=1, keepdims=True) / D + 1e-05)
+    acc = acc * rs
+    acc2 = acc2 * rs
     act = (silu(acc[:, :256]) * acc[:, 256:]).astype(BF16)
+    act2 = (silu(acc2[:, :256]) * acc2[:, 256:]).astype(BF16)
     for c in range(8):
-        o = jnp.dot(act, wd_ref[0, :, c * 256 : (c + 1) * 256], preferred_element_type=F32)
-        for slot in range(2):
-            for half in range(2):
-                scr[rows_of(c, slot, half), :] = o[
-                    slot * 64 : (slot + 1) * 64, half * 128 : (half + 1) * 128
-                ]
+        part = slice(c * 256, (c + 1) * 256)
+        o = jnp.dot(act, wd_ref[0, :, part], preferred_element_type=F32)
+        o = o + jnp.dot(act2, wd2_ref[0, :, part], preferred_element_type=F32)
+        for half in range(2):
+            scr[rows_of(c, half), :] = o[:, half * 128 : (half + 1) * 128]
     out_ref[...] = scr[...].astype(BF16)
 
 
@@ -284,6 +284,9 @@
     w_down,
 ):
     head = lax.axis_index("head").astype(jnp.int32).reshape(1)
+    swap = [(0, 1), (1, 0)]
+    w_gate_up2 = lax.ppermute(w_gate_up, "side", swap)
+    w_down2 = lax.ppermute(w_down, "side", swap)
     sv = state_values.reshape(16, 128, 128)
     ss = state_scales.reshape(16, 128)
     part, resid, sv, ss, ngain, w_out, pgain = call(
@@ -312,10 +315,10 @@
         ),
         [pltpu.SemaphoreType.DMA((5,))],
     )
-    part = a2a(part.reshape(8, 16, 768), "sub")
+    part = a2a(part.reshape(8, 16, 768), SUB)
     mt, wsel = call(
         route_body,
-        (shape((2048, 16)), shape((16, 2048))),
+        (shape((1024, 16)), shape((16, 1024))),
         [HB, HB],
         (routes, route_scale),
     )
@@ -325,10 +328,10 @@
         [VM, SM, SM, VM, VM, VM],
         (part, a_log, dt_bias, sv, ss, ngain),
     )
-    gathered = a2a(gated, "sub").reshape(128, 128)
-    new_values, new_scales, done = call(
+    gathered = a2a(gated, SUB).reshape(128, 128)
+    new_values, new_scales = call(
         state_body,
-        (shape((16, 128, 128)), shape((16, 128), F32), shape((8, 128), F32)),
+        (shape((16, 128, 128)), shape((16, 128), F32)),
         [VM] * 4,
         (sv, sd, keys, delta),
     )
@@ -336,50 +339,52 @@
     attn = a2a(attn.reshape(16, 8, 256), "head")
     hidden, sent = call(
         dispatch_body,
-        (shape((8, 256)), shape((2048, 128))),
-        [VM] * 4,
-        (attn, resid, mt, done),
-    )
-    every = ("grp", "head", "sub")
-    received = a2a(sent.reshape(512, 4, 128), every).reshape(2048, 128)
+        (shape((8, 256)), shape((1024, 128))),
+        [VM] * 3,
+        (attn, resid, mt),
+    )
+    every = ("grp", "head") + SUB
+    received = a2a(sent.reshape(512, 2, 128), every).reshape(1024, 128)
     result = call(
         expert_body,
-        shape((2048, 128)),
-        [VM] * 4,
-        (received, pgain, w_gate_up, w_down),
-        [pltpu.VMEM((2048, 128), F32)],
-    )
-    back = a2a(result.reshape(512, 4, 128), every).reshape(2048, 128)
+        shape((1024, 128)),
+        [VM] * 6,
+        (received, pgain, w_gate_up, w_down, w_gate_up2, w_down2),
+        [pltpu.VMEM((1024, 128), F32)],
+    )
+    back = a2a(result.reshape(512, 2, 128), every).reshape(1024, 128)
     out = call(combine_body, shape((8, 256)), [VM] * 3, (wsel, back, hidden))
     return (out, new_values.reshape(16, 1, 128, 128), new_scales.reshape(16, 1, 128))
 
 
 def solution(mesh):
+    shape4 = (mesh.shape["grp"], mesh.shape["head"], mesh.shape["sub"] // 2, 2)
+    mesh = jax.sharding.Mesh(mesh.devices.reshape(shape4), ("grp", "head") + SUB)
     placed = (
-        P("grp", "sub"),
-        P("sub"),
-        P("sub", "head"),
-        P("sub", "head"),
+        P("grp", SUB),
+        P(SUB),
+        P(SUB, "head"),
+        P(SUB, "head"),
         P("head"),
         P("head"),
-        P(("grp", "sub"), "head", None, None),
-        P(("grp", "sub"), "head", None),
+        P(("grp",) + SUB, "head", None, None),
+        P(("grp",) + SUB, "head", None),
         P(),
-        P("head", "sub"),
+        P("head", SUB),
         P(),
         P(("grp", "head"), None),
         P(("grp", "head"), None),
-        P(("grp", "head", "sub"), None, None),
-        P(("grp", "head", "sub"), None, None),
+        P(("grp", "head") + SUB, None, None),
+        P(("grp", "head") + SUB, None, None),
     )
     return jax.shard_map(
         local,
         mesh=mesh,
         in_specs=placed,
         out_specs=(
-            P(("grp", "head"), "sub"),
-            P(("grp", "sub"), "head", None, None),
-            P(("grp", "sub"), "head", None),
+            P(("grp", "head"), SUB),
+            P(("grp",) + SUB, "head", None, None),
+            P(("grp",) + SUB, "head", None),
         ),
         check_vma=False,
     )

time: 119 us -> 172 us (1.45)
  waiting for transfers between devices: 10.5 us -> 84.2 us
  blocking collectives: 71.7 us -> 36 us
  starting transfers between devices: 22 us -> 35.4 us
  Pallas kernels: 10.6 us -> 12.7 us
    all_to_all x2 -> x3, waiting for transfers between devices: 10.5 us -> 84.1 us  [a2a(): return lax.all_to_all(x, axes, split_axis=0, concat_axis=0, tiled=True)]
    all_to_all x3 -> x2, blocking collectives: 71.7 us -> 36 us  [a2a(): return lax.all_to_all(x, axes, split_axis=0, concat_axis=0, tiled=True)]
    all_to_all x2 -> x3, starting transfers between devices: 22 us -> 29.3 us  [a2a(): return lax.all_to_all(x, axes, split_axis=0, concat_axis=0, tiled=True)]
    ppermute x0 -> x2, starting transfers between devices: none -> 6.09 us  [the longest x1 4.17 us: local(): w_gate_up2 = lax.ppermute(w_gate_up, 'side', swap)]
    pallas_call x8, Pallas kernels: 10.6 us -> 12.7 us  [call(): pl.pallas_call(kernel, out_shape=outs, in_specs=ins, out_specs=jax.tree.m...]
  transfers between devices with their start and end apart: 2 -> 5, of which waited for: 2 -> 3; matrix products, arithmetic and copies ran while one was open for 0% -> 0% of each run, Pallas kernels for 3% -> 5%
where the time goes in v7:
time: 172 us; the launch traced here: 171 us
  waiting for transfers between devices  84.2 us (49%)
  blocking collectives  36 us (21%)
  starting transfers between devices  35.4 us (21%)
  Pallas kernels  12.7 us (7%)
  between operations  2.01 us (1%)
    all_to_all x3, waiting for transfers between devices, a2a(): return lax.all_to_all(x, axes, split_axis=0, concat_axis=0, tiled=True)  84.1 us
    all_to_all x2, blocking collectives, a2a(): return lax.all_to_all(x, axes, split_axis=0, concat_axis=0, tiled=True)  36 us
    all_to_all x3, starting transfers between devices, a2a(): return lax.all_to_all(x, axes, split_axis=0, concat_axis=0, tiled=True)  29.3 us
    pallas_call x8, Pallas kernels, call(): pl.pallas_call(kernel, out_shape=outs, in_specs=ins, out_specs=jax.tree.m...  12.7 us
    ppermute x1, starting transfers between devices, local(): w_gate_up2 = lax.ppermute(w_gate_up, 'side', swap)  4.17 us
  transfers between devices with their start and end apart: 5, of which 3 were waited for; matrix products, arithmetic and copies ran while one was open for 0% of the time, Pallas kernels for 5%

profile of v7, /device:TPU:1, one launch (start us, length us, event | category | flops | bytes accessed | tf_op | source)
XLA Modules:
  0.0 171.5 jit_solution(1728700567394218579)
XLA Ops:
  0.6 0.0 copy-start
  0.6 4.2 %collective-permute-start = (bf16[1,2048,512]{2,1,0:T(8,128)(2,1)}, bf16[1,2048,512]{2,1,0:T(8,128)(2,1)}, u32[]{:S(2)}, u32[]{:S(2)}) collective-permute-start(bf16[1,2048,512]{2,1,0:T(8,128)(2,1)} %refs_2_.2), channel_id=1, source_target_pairs={{0,1},{1,0},{2,3},{3,2},{4,5},{5,4},{6,7},{7,6},{8,9},{9,8},{10,11... | collective-permute-start | bytes 6291464 | tf_op jit(solution)/shard_map/ppermute | solution.py:288
  4.8 1.9 %collective-permute-start.1 = (bf16[1,256,2048]{2,1,0:T(8,128)(2,1)}, bf16[1,256,2048]{2,1,0:T(8,128)(2,1)}, u32[]{:S(2)}, u32[]{:S(2)}) collective-permute-start(bf16[1,256,2048]{2,1,0:T(8,128)(2,1)} %refs_3_.3), channel_id=1, source_target_pairs={{0,1},{1,0},{2,3},{3,2},{4,5},{5,4},{6,7},{7,6},{8,9},{9,8},{10,11... | collective-permute-start | bytes 3145736 | tf_op jit(solution)/shard_map/ppermute | solution.py:289
  6.8 2.1 %shard_map.167 = (bf16[128,768]{1,0:T(8,128)(2,1)}, f32[8,256]{1,0:T(8,128)S(1)}, bf16[16,128,128]{2,1,0:T(8,128)(2,1)S(1)}, f32[16,128]{1,0:T(8,128)S(1)}, f32[...) custom-call(s32[1]{0:T(128)} %bitcast.refs_0_, bf16[128,256]{1,0:T(8,128)(2,1)} %refs_1_.4, ...), custom_call_target="tpu_custom_call" | custom-call | tf_op jit(solution)/shard_map/pallas_call | solution.py:54
  8.9 7.0 %all-to-all-start = ((bf16[8,16,768]{2,1,0:T(8,128)(2,1)}), bf16[8,16,768]{2,1,0:T(8,128)(2,1)S(1)}, u32[]{:S(2)}, u32[]{:S(2)}) async-start(bf16[8,16,768]{2,1,0:T(8,128)(2,1)} %bitcast.7), calls=%async_computation | async-start | bytes 393216 | tf_op jit(solution)/shard_map/all_to_all | solution.py:266
  17.2 63.1 %all-to-all-done.refs_0_ = bf16[8,16,768]{2,1,0:T(8,128)(2,1)S(1)} async-done(((bf16[8,16,768]{2,1,0:T(8,128)(2,1)}), bf16[8,16,768]{2,1,0:T(8,128)(2,1)S(1)}, u32[]{:S(2)}, u32[]{:S(2)}) %all-to-all-start) | async-done | bytes 196640 | tf_op jit(solution)/shard_map/all_to_all | solution.py:266
  80.3 1.1 shard_map.168
  81.3 10.1 %all_to_all.25 = bf16[8,16,128]{2,1,0:T(8,128)(2,1)S(1)} all-to-all(bf16[8,16,128]{2,1,0:T(8,128)(2,1)S(1)} %get-tuple-element.25), channel_id=1, replica_groups=mesh['grp'=4,'head'=16,'quad'=4,'side'=2] {'quad','side'}, dimensions={0} | all-to-all | bytes 65536 | tf_op jit(solution)/shard_map/all_to_all | solution.py:266
  91.4 0.8 shard_map.169
  92.2 13.6 %all-to-all-start.2 = ((bf16[16,8,256]{2,1,0:T(8,128)(2,1)}), bf16[16,8,256]{2,1,0:T(8,128)(2,1)S(1)}, u32[]{:S(2)}, u32[]{:S(2)}) async-start(bf16[16,8,256]{2,1,0:T(8,128)(2,1)} %bitcast.9), calls=%async_computation.2 | async-start | bytes 131072 | tf_op jit(solution)/shard_map/all_to_all | solution.py:266
  105.8 1.0 shard_map.166
  106.7 6.8 %all-to-all-done.2.refs_0_ = bf16[16,8,256]{2,1,0:T(8,128)(2,1)S(1)} async-done(((bf16[16,8,256]{2,1,0:T(8,128)(2,1)}), bf16[16,8,256]{2,1,0:T(8,128)(2,1)S(1)}, u32[]{:S(2)}, u32[]{:S(2)}) %all-to-all-start.2) | async-done | bytes 65568 | tf_op jit(solution)/shard_map/all_to_all | solution.py:266
  113.6 0.2 shard_map.170
  113.8 25.9 %all_to_all.26 = bf16[512,2,128]{2,1,0:T(2,128)(2,1)S(1)} all-to-all(bf16[512,2,128]{2,1,0:T(2,128)(2,1)S(1)} %bitcast.22), channel_id=1, replica_groups=mesh['grp'=4,'head'=16,'quad'=4,'side'=2] {'grp','head','quad','side'}, dimensions={0} | all-to-all | bytes 524288 | tf_op jit(solution)/shard_map/all_to_all | solution.py:266
  139.7 0.0 collective-permute-done.1.refs_5_
  139.7 0.0 collective-permute-done.refs_4_
  139.7 0.0 copy-done
  139.7 0.0 copy-start.1
  139.7 1.2 copy-done.1
  140.9 3.9 %shard_map.171 = bf16[1024,128]{1,0:T(8,128)(2,1)} custom-call(bf16[1024,128]{1,0:T(8,128)(2,1)S(1)} %bitcast.21, f32[8,1,256]{2,1,0:T(1,128)S(1)} %get-tuple-element.30.refs_1_, bf16[1,2048,512]{2,1,0:T(8,128)(2,1)S(1)} %copy-done, bf16[1,256,2048]{2,1,0:T(8,128)(2,1)S(1)} %copy-done.1, bf16[1,2048,512]{2,1,0:T(8,128)(2,1)} %collective-permute-done.refs_4_, ...), custom_call_target="tpu_custom_call" | custom-call | tf_op jit(solution)/shard_map/pallas_call | solution.py:54
  144.8 8.8 %all-to-all-start.4 = ((bf16[512,2,128]{2,1,0:T(2,128)(2,1)}), bf16[512,2,128]{2,1,0:T(2,128)(2,1)S(1)}, u32[]{:S(2)}, u32[]{:S(2)}) async-start(bf16[512,2,128]{2,1,0:T(2,128)(2,1)} %bitcast.12), calls=%async_computation.4 | async-start | bytes 524288 | tf_op jit(solution)/shard_map/all_to_all | solution.py:266
  153.6 2.9 %shard_map.173 = (bf16[16,128,128]{2,1,0:T(8,128)(2,1)}, f32[16,128]{1,0:T(8,128)}) custom-call(bf16[16,128,128]{2,1,0:T(8,128)(2,1)S(1)} %get-tuple-element.22.refs_3_.refs_0_, f32[16,128]{1,0:T(8,128)S(1)} %get-tuple-element.32.refs_1_, f32[16,128]{1,0:T(8,128)S(1)} %get-tuple-element.33.refs_2_, f32[16,128]{1,0:T(8,128)S(1)} %get-tuple-element.34.refs_3_), custom_call_target="tpu_custom_call" | custom-call | tf_op jit(solution)/shard_map/pallas_call | solution.py:54
  156.5 14.2 %all-to-all-done.4 = bf16[512,2,128]{2,1,0:T(2,128)(2,1)S(1)} async-done(((bf16[512,2,128]{2,1,0:T(2,128)(2,1)}), bf16[512,2,128]{2,1,0:T(2,128)(2,1)S(1)}, u32[]{:S(2)}, u32[]{:S(2)}) %all-to-all-start.4) | async-done | bytes 262176 | tf_op jit(solution)/shard_map/all_to_all | solution.py:266
  170.7 0.7 shard_map.172
Async XLA Ops:
  0.6 139.0 %copy-start = (bf16[1,2048,512]{2,1,0:T(8,128)(2,1)S(1)}, bf16[1,2048,512]{2,1,0:T(8,128)(2,1)}, u32[]{:S(2)}) copy-start(bf16[1,2048,512]{2,1,0:T(8,128)(2,1)} %refs_2_.2) | copy-start | bytes 6291460
  0.6 139.0 %collective-permute-start = (bf16[1,2048,512]{2,1,0:T(8,128)(2,1)}, bf16[1,2048,512]{2,1,0:T(8,128)(2,1)}, u32[]{:S(2)}, u32[]{:S(2)}) collective-permute-start(bf16[1,2048,512]{2,1,0:T(8,128)(2,1)} %refs_2_.2), channel_id=1, source_target_pairs={{0,1},{1,0},{2,3},{3,2},{4,5},{5,4},{6,7},{7,6},{8,9},{9,8},{10,11... | collective-permute-start | bytes 6291464 | tf_op jit(solution)/shard_map/ppermute | solution.py:288
  4.8 134.8 %collective-permute-start.1 = (bf16[1,256,2048]{2,1,0:T(8,128)(2,1)}, bf16[1,256,2048]{2,1,0:T(8,128)(2,1)}, u32[]{:S(2)}, u32[]{:S(2)}) collective-permute-start(bf16[1,256,2048]{2,1,0:T(8,128)(2,1)} %refs_3_.3), channel_id=1, source_target_pairs={{0,1},{1,0},{2,3},{3,2},{4,5},{5,4},{6,7},{7,6},{8,9},{9,8},{10,11... | collective-permute-start | bytes 3145736 | tf_op jit(solution)/shard_map/ppermute | solution.py:289
  8.9 71.4 %all-to-all-start = ((bf16[8,16,768]{2,1,0:T(8,128)(2,1)}), bf16[8,16,768]{2,1,0:T(8,128)(2,1)S(1)}, u32[]{:S(2)}, u32[]{:S(2)}) async-start(bf16[8,16,768]{2,1,0:T(8,128)(2,1)} %bitcast.7), calls=%async_computation | async-start | bytes 393216 | tf_op jit(solution)/shard_map/all_to_all | solution.py:266
  92.2 21.4 %all-to-all-start.2 = ((bf16[16,8,256]{2,1,0:T(8,128)(2,1)}), bf16[16,8,256]{2,1,0:T(8,128)(2,1)S(1)}, u32[]{:S(2)}, u32[]{:S(2)}) async-start(bf16[16,8,256]{2,1,0:T(8,128)(2,1)} %bitcast.9), calls=%async_computation.2 | async-start | bytes 131072 | tf_op jit(solution)/shard_map/all_to_all | solution.py:266
  139.7 1.2 copy-start.1
  144.8 25.9 %all-to-all-start.4 = ((bf16[512,2,128]{2,1,0:T(2,128)(2,1)}), bf16[512,2,128]{2,1,0:T(2,128)(2,1)S(1)}, u32[]{:S(2)}, u32[]{:S(2)}) async-start(bf16[512,2,128]{2,1,0:T(2,128)(2,1)} %bitcast.12), calls=%async_computation.4 | async-start | bytes 524288 | tf_op jit(solution)/shard_map/all_to_all | solution.py:266
